TPU v7x, 128 devices: a whole 4x4x4 slice. The times are simulated.
128 devices in a mesh: px: 8 (over x, core), py: 16 (over z, y).
Axes of the slice: x: 4, y: 4, z: 4, core: 2. Of those that a mesh axis runs over, the one named last changes fastest.
Arguments:
- residual: float32 [32, 64, 8, 8, 8, 128], P('px', 'py'), may hold values from -4 to 4
- element_stiffness_scale: float32 [32, 64, 128], P('px', 'py'), may hold values from 0.25 to 4
- fine_basis: float32 [3, 10, 10], replicated, may hold values from -2 to 2
- fine_eigen: float32 [3, 10], replicated, may hold values from 0.3 to 3
- middle_basis: float32 [3, 6, 6], replicated, may hold values from -2.5 to 2.5
- middle_eigen: float32 [3, 6], replicated, may hold values from 0.3 to 3
Outputs:
- correction: float32 [32, 64, 8, 8, 8, 128], P('px', 'py')
All inputs are finite; a program needn't handle non-finite values.
Results may differ from a plain program's by a relative error of at most 0.000098.
Values sent between devices are 32-bit elements; how exact they have to be, the bound alone decides.
No kernel may reach another device: no remote copies, remote signals or barrier semaphores. Data moves between devices by JAX's collectives and lax.ppermute only.
A program may use at most 128 MiB of HBM per device.

v0:
```python
import math

import jax
import jax.numpy as jnp
from jax import lax
from jax.sharding import PartitionSpec as P

HIGHEST = lax.Precision.HIGHEST
coarse_stiff = 24.0
coarse_mass = 0.5


def extended_2(cells, sides, width):
    for axis, dim in sides:
        count = lax.axis_size(axis)
        head = lax.slice_in_dim(cells, 0, width, axis=dim)
        tail = lax.slice_in_dim(cells, cells.shape[dim] - width, cells.shape[dim], axis=dim)
        cells = jnp.concatenate(
            [
                lax.ppermute(tail, axis, [(i, (i + 1) % count) for i in range(count)]),
                cells,
                lax.ppermute(head, axis, [((i + 1) % count, i) for i in range(count)]),
            ],
            axis=dim,
        )
    return cells


def lobatto(node_count):
    positions = jnp.arange(node_count, dtype=jnp.int32).astype(jnp.float32)
    return -jnp.cos(positions * (math.pi / (node_count - 1)))


def interpolation(fine_count, coarse_count):
    fine_points = lobatto(fine_count)
    coarse_points = lobatto(coarse_count)
    numerator = fine_points[:, None, None] - coarse_points[None, None, :]
    distance = coarse_points[None, :, None] - coarse_points[None, None, :]
    same_node = jnp.eye(coarse_count, dtype=bool)[None]
    factors = jnp.where(
        same_node, jnp.float32(1.0), numerator / jnp.where(same_node, jnp.float32(1.0), distance)
    )
    return jnp.prod(factors, axis=2)


def inverse_multiplicity(node_count):
    positions = jnp.arange(node_count, dtype=jnp.int32)
    line_weight = jnp.where((positions == 0) | (positions == node_count - 1), 0.5, 1.0).astype(
        jnp.float32
    )
    return (line_weight[:, None, None] * line_weight[None, :, None] * line_weight[None, None, :])[
        ..., None
    ]


def hartley(node_count):
    positions = jnp.arange(node_count, dtype=jnp.int32)
    phase = positions[:, None] * positions[None, :] % node_count
    angle = phase.astype(jnp.float32) * (2.0 * math.pi / node_count)
    return jnp.cos(angle) + jnp.sin(angle)


def line_eigen(positions, node_count):
    return 2.0 - 2.0 * jnp.cos(positions.astype(jnp.float32) * (2.0 * math.pi / node_count))


def coarse_denominator(line_x, line_y, line_z):
    return (
        coarse_stiff * (line_x[:, None, None] + line_y[None, :, None] + line_z[None, None, :])
        + coarse_mass
    )


def coarse_solve(vertex):
    count_x, count_y, count_z = vertex.shape
    spectrum = jnp.einsum("kx,xyz->kyz", hartley(count_x), vertex, precision=HIGHEST)
    spectrum = jnp.einsum("ky,xyz->xkz", hartley(count_y), spectrum, precision=HIGHEST)
    spectrum = jnp.einsum("kz,xyz->xyk", hartley(count_z), spectrum, precision=HIGHEST)
    denominator = coarse_denominator(
        line_eigen(jnp.arange(count_x, dtype=jnp.int32), count_x),
        line_eigen(jnp.arange(count_y, dtype=jnp.int32), count_y),
        line_eigen(jnp.arange(count_z, dtype=jnp.int32), count_z),
    )
    spectrum = spectrum / denominator
    spectrum = jnp.einsum("kx,xyz->kyz", hartley(count_x), spectrum, precision=HIGHEST)
    spectrum = jnp.einsum("ky,xyz->xkz", hartley(count_y), spectrum, precision=HIGHEST)
    spectrum = jnp.einsum("kz,xyz->xyk", hartley(count_z), spectrum, precision=HIGHEST)
    return spectrum / float(count_x * count_y * count_z)


def corner_values(block):
    size_x = block.shape[0] - 1
    size_y = block.shape[1] - 1
    planes = []
    for step_a in (0, 1):
        for step_b in (0, 1):
            for step_c in (0, 1):
                shifted = block[step_a : step_a + size_x, step_b : step_b + size_y]
                planes.append(jnp.roll(shifted, -step_c, axis=2))
    stacked = jnp.stack(planes, axis=2)
    return stacked.reshape(size_x, size_y, 2, 2, 2, block.shape[2])


def restrict(values, interp):
    values = jnp.einsum("fi,...fghz->...ighz", interp, values, precision=HIGHEST)
    values = jnp.einsum("gj,...ighz->...ijhz", interp, values, precision=HIGHEST)
    return jnp.einsum("hk,...ijhz->...ijkz", interp, values, precision=HIGHEST)


def prolong(values, interp):
    values = jnp.einsum("fi,...ighz->...fghz", interp, values, precision=HIGHEST)
    values = jnp.einsum("gj,...fjhz->...fghz", interp, values, precision=HIGHEST)
    return jnp.einsum("hk,...fgkz->...fghz", interp, values, precision=HIGHEST)


def local_solve(extended, elem_scale, eigen_basis, eigen_values):
    spectrum = jnp.einsum("ai,...abcz->...ibcz", eigen_basis[0], extended, precision=HIGHEST)
    spectrum = jnp.einsum("bj,...ibcz->...ijcz", eigen_basis[1], spectrum, precision=HIGHEST)
    spectrum = jnp.einsum("ck,...ijcz->...ijkz", eigen_basis[2], spectrum, precision=HIGHEST)
    total = (
        eigen_values[0][:, None, None]
        + eigen_values[1][None, :, None]
        + eigen_values[2][None, None, :]
    )
    spectrum = spectrum / (elem_scale[..., None, None, None, :] * total[..., None])
    result = jnp.einsum("ai,...ijkz->...ajkz", eigen_basis[0], spectrum, precision=HIGHEST)
    result = jnp.einsum("bj,...ajkz->...abkz", eigen_basis[1], result, precision=HIGHEST)
    return jnp.einsum("ck,...abkz->...abcz", eigen_basis[2], result, precision=HIGHEST)


def replace_ends(values, axis, low_new, high_new):
    count = values.shape[axis]
    middle = lax.slice_in_dim(values, 1, count - 1, axis=axis)
    return jnp.concatenate(
        [jnp.expand_dims(low_new, axis), middle, jnp.expand_dims(high_new, axis)], axis=axis
    )


def sum_faces(values, layer_depth):
    node_count = values.shape[2]
    last_node = node_count - 1
    low_side = values[:, :, :, 0]
    high_side = values[:, :, :, last_node]
    edge_layers = jnp.stack([low_side[:, 0], high_side[:, -1]], axis=1)
    padded = extended_2(edge_layers, (("py", 1),), 1)
    below_high = jnp.concatenate([padded[:, 0:1], high_side[:, :-1]], axis=1)
    above_low = jnp.concatenate([low_side[:, 1:], padded[:, 3:4]], axis=1)
    values = replace_ends(values, 3, low_side + below_high, high_side + above_low)
    low_side = values[:, :, :, :, 0]
    high_side = values[:, :, :, :, last_node]
    values = replace_ends(
        values,
        4,
        low_side + jnp.roll(high_side, 1, axis=4),
        high_side + jnp.roll(low_side, -1, axis=4),
    )
    first_slab = values[0:1, :, :layer_depth]
    final_slab = values[-1:, :, node_count - layer_depth :]
    padded = extended_2(jnp.concatenate([first_slab, final_slab], axis=0), (("px", 0),), 1)
    low_side = values[:, :, 0]
    high_side = values[:, :, last_node]
    below_high = jnp.concatenate([padded[0:1, :, -1], high_side[:-1]], axis=0)
    above_low = jnp.concatenate([low_side[1:], padded[3:4, :, 0]], axis=0)
    values = replace_ends(values, 2, low_side + below_high, high_side + above_low)
    return (values, padded[0, :, 0], padded[3, :, -1])


def face_total(values):
    return sum_faces(values, 1)[0]


def assemble(values, left_layer, right_layer, south_layer, north_layer):
    node_count = values.shape[2]
    inner_node = node_count - 2
    lower_layer = jnp.roll(values[:, :, :, :, inner_node], 1, axis=4)
    upper_layer = jnp.roll(values[:, :, :, :, 1], -1, axis=4)
    core = jnp.concatenate(
        [lower_layer[:, :, :, :, None], values, upper_layer[:, :, :, :, None]], axis=4
    )
    pad_c = ((0, 0), (0, 0), (0, 0), (0, 0), (1, 1), (0, 0))
    south_full = jnp.pad(south_layer[:, :, :, None], pad_c)
    north_full = jnp.pad(north_layer[:, :, :, None], pad_c)
    middle = jnp.concatenate([south_full, core, north_full], axis=3)
    pad_bc = ((0, 0), (0, 0), (0, 0), (1, 1), (1, 1), (0, 0))
    left_full = jnp.pad(left_layer[:, :, None], pad_bc)
    right_full = jnp.pad(right_layer[:, :, None], pad_bc)
    return jnp.concatenate([left_full, middle, right_full], axis=2)


def extend_local(values, left_face, right_face):
    node_count = values.shape[2]
    inner_node = node_count - 2
    rims = jnp.stack([values[:, 0, :, 1], values[:, -1, :, inner_node]], axis=1)
    padded = extended_2(rims, (("py", 1),), 1)
    left_layer = jnp.concatenate([left_face[None], values[:-1, :, inner_node]], axis=0)
    right_layer = jnp.concatenate([values[1:, :, 1], right_face[None]], axis=0)
    south_layer = jnp.concatenate([padded[:, 0:1], values[:, :-1, :, inner_node]], axis=1)
    north_layer = jnp.concatenate([values[:, 1:, :, 1], padded[:, 3:4]], axis=1)
    return assemble(values, left_layer, right_layer, south_layer, north_layer)


def smooth_level(values, element_stiffness_scale, eigen_basis, eigen_values):
    node_count = values.shape[2]
    rhs_sum, left_face, right_face = sum_faces(values, 2)
    extended = extend_local(rhs_sum, left_face, right_face)
    solved = local_solve(extended, element_stiffness_scale, eigen_basis, eigen_values)[
        :, :, 1:-1, 1:-1, 1:-1
    ]
    weight = inverse_multiplicity(node_count)
    return (rhs_sum, weight * face_total(solved))


def on_device(
    residual, element_stiffness_scale, fine_basis, fine_eigen, middle_basis, middle_eigen
):
    fine_count = residual.shape[2]
    middle_count = middle_basis.shape[1] - 2
    local_x, local_y, depth_z = (residual.shape[0], residual.shape[1], residual.shape[5])
    interp_fine = interpolation(fine_count, middle_count)
    interp_mid = interpolation(middle_count, 2)
    fine_weight = inverse_multiplicity(fine_count)
    middle_weight = inverse_multiplicity(middle_count)
    fine_rhs, fine_part = smooth_level(residual, element_stiffness_scale, fine_basis, fine_eigen)
    middle_in = restrict(fine_weight * fine_rhs, interp_fine)
    middle_rhs, middle_part = smooth_level(
        middle_in, element_stiffness_scale, middle_basis, middle_eigen
    )
    coarse_rhs = face_total(restrict(middle_weight * middle_rhs, interp_mid))
    vertex = coarse_rhs[:, :, 0, 0, 0]
    count_px = lax.axis_size("px")
    count_py = lax.axis_size("py")
    full_x = local_x * count_px
    full_y = local_y * count_py
    gathered = lax.all_gather(vertex, ("px", "py"), axis=0, tiled=True)
    whole = gathered.reshape(count_px, count_py, local_x, local_y, depth_z)
    whole = whole.transpose(0, 2, 1, 3, 4).reshape(full_x, full_y, depth_z)
    solution = coarse_solve(whole)
    wrapped = jnp.concatenate([solution, solution[:1]], axis=0)
    wrapped = jnp.concatenate([wrapped, wrapped[:, :1]], axis=1)
    start_x = lax.axis_index("px") * local_x
    start_y = lax.axis_index("py") * local_y
    block = lax.dynamic_slice(
        wrapped, (start_x, start_y, jnp.int32(0)), (local_x + 1, local_y + 1, depth_z)
    )
    corner = corner_values(block)
    return fine_part + prolong(middle_part + prolong(corner, interp_mid), interp_fine)


def solution(mesh):
    placed = (P("px", "py", None, None, None, None), P("px", "py", None), P(), P(), P(), P())
    return jax.shard_map(
        on_device,
        mesh=mesh,
        in_specs=placed,
        out_specs=P("px", "py", None, None, None, None),
        check_vma=False,
    )
```

profile of v0, /device:TPU:0, one launch (start us, length us, event | category | flops | bytes accessed | tf_op | source)
XLA Modules:
  0.0 385.1 jit_solution(7389166265158484368)
XLA Ops:
  22.2 3.7 collective-permute-start.1
  38.6 4.7 %copy.422 = f32[4,4,8,8,6,128]{5,4,3,1,2,0:T(8,128)S(1)} copy(f32[4,4,8,8,6,128]{5,3,1,2,0,4:T(8,128)} %pad_maximum_fusion.5) | data formatting | bytes 6291456 | tf_op jit(solution)/shard_map/slice | solution.py:133
  54.6 5.6 %fusion.65 = f32[4,4,4,8,8,128]{5,2,4,3,1,0:T(4,128)S(1)} fusion(f32[4,4,8,8,8,128]{5,4,3,1,2,0:T(8,128)S(1)} %get-tuple-element.28, f32[8,4]{0,1:T(4,128)S(1)} %fusion.130), kind=kOutput, calls=%fused_computation.73 | convolution fusion | flops 50331648 | bytes 6291584 | tf_op jit(solution)/shard_map/fi,...fghz->...ighz/dot_general | solution.py:105
  60.2 3.0 fusion.70
  64.2 5.9 %collective-permute-start.11 = (f32[4,1,4,4,128]{4,3,2,0,1:T(4,128)S(1)}, f32[4,1,4,4,128]{4,3,2,0,1:T(4,128)S(1)}, u32[]{:S(2)}, u32[]{:S(2)}) collective-permute-start(f32[4,1,4,4,128]{4,3,2,0,1:T(4,128)S(1)} %slice.737), channel_id=1, source_target_pairs={{1,0},{2,1},{3,2},{4,3},{5,4},{6,5},{7,6},{8,7},{9,8},{10,9},{11,1... | collective-permute-start | bytes 98312 | tf_op jit(solution)/shard_map/ppermute | solution.py:22
  73.3 7.2 %collective-permute-done.10 = f32[4,1,4,4,128]{4,3,2,0,1:T(4,128)S(1)} collective-permute-done((f32[4,1,4,4,128]{4,3,2,0,1:T(4,128)S(1)}, f32[4,1,4,4,128]{4,3,2,0,1:T(4,128)S(1)}, u32[]{:S(2)}, u32[]{:S(2)}) %collective-permute-start.10) | collective-permute-done | bytes 32800 | tf_op jit(solution)/shard_map/ppermute | solution.py:20
  85.4 3.1 collective-permute-done.12
  94.1 5.1 %copy.430 = f32[4,4,8,10,10,128]{5,2,4,3,1,0:T(8,128)S(1)} copy(f32[4,4,8,10,10,128]{5,4,3,1,2,0:T(8,128)S(1)} %fusion.14) | data formatting | bytes 13107200 | tf_op jit(solution)/shard_map/concatenate | solution.py:183
  99.2 16.3 %fusion.24 = f32[4,4,10,10,10,128]{5,2,4,3,1,0:T(8,128)S(1)} fusion(f32[4,4,1,8,8,128]{5,2,4,3,1,0:T(1,128)S(1)} %bitcast.505, f32[4,4,1,8,8,128]{5,2,4,3,1,0:T(1,128)S(1)} %bitcast.504, f32[4,4,8,10,10,128]{5,2,4,3,1,0:T(8,128)S(1)} %copy.430, f32[1,10,10]{2,0,1:T(1,128)S(1)} %get-tuple-element.87), kind=kOutput, calls=%fused_computation.26 | convolution fusion | flops 258048000 | bytes 15794576 | tf_op jit(solution)/shard_map/ai,...abcz->...ibcz/dot_general | solution.py:117
  115.5 21.5 %fusion.15 = f32[4,4,10,10,10,128]{5,3,4,2,1,0:T(8,128)} fusion(f32[4,4,10,10,10,128]{5,2,4,3,1,0:T(8,128)S(1)} %fusion.24, f32[1,10,10]{2,0,1:T(1,128)S(1)} %get-tuple-element.86), kind=kOutput, calls=%fused_computation.23 | convolution fusion | flops 245760000 | bytes 16384400 | tf_op jit(solution)/shard_map/bj,...ibcz->...ijcz/dot_general | solution.py:118
  137.1 24.1 %bitcast_divide_fusion = f32[4,4,10,10,10,128]{5,4,3,2,1,0:T(8,128)} fusion(f32[4,4,10,10,10,128]{5,3,4,2,1,0:T(8,128)} %fusion.15, f32[10,10,10]{2,1,0:T(8,128)S(1)} %copy-done.9, f32[4,4,128]{2,1,0:T(4,128)S(1)} %copy-done.15, f32[1,10,10]{2,0,1:T(1,128)S(1)} %get-tuple-element.85), kind=kOutput, calls=%fused_computation.8 | convolution fusion | flops 249856000 | bytes 16396592 | tf_op jit(solution)/shard_map/ck,...ijcz->...ijkz/dot_general | solution.py:119
  161.2 24.0 %fusion.18 = f32[4,4,10,10,10,128]{5,2,4,3,1,0:T(8,128)S(1)} fusion(f32[4,4,10,10,10,128]{5,4,3,2,1,0:T(8,128)} %bitcast_divide_fusion, f32[1,10,10]{2,0,1:T(1,128)S(1)} %get-tuple-element.87), kind=kOutput, calls=%fused_computation.24 | convolution fusion | flops 245760000 | bytes 16384400 | tf_op jit(solution)/shard_map/ai,...ijkz->...ajkz/dot_general | solution.py:126
  185.2 21.5 %fusion.21 = f32[4,4,10,10,10,128]{5,3,4,2,1,0:T(8,128)} fusion(f32[4,4,10,10,10,128]{5,2,4,3,1,0:T(8,128)S(1)} %fusion.18, f32[1,10,10]{2,0,1:T(1,128)S(1)} %get-tuple-element.86), kind=kOutput, calls=%fused_computation.25 | convolution fusion | flops 245760000 | bytes 16384400 | tf_op jit(solution)/shard_map/bj,...ajkz->...abkz/dot_general | solution.py:127
  206.7 22.8 %fusion.4 = f32[4,4,10,10,128,10]{4,5,3,2,1,0:T(8,128)} fusion(f32[4,4,10,10,10,128]{5,3,4,2,1,0:T(8,128)} %fusion.21, f32[1,10,10]{2,0,1:T(1,128)S(1)} %get-tuple-element.85), kind=kOutput, calls=%fused_computation.10 | convolution fusion | flops 245760000 | bytes 16384400 | tf_op jit(solution)/shard_map/ck,...abkz->...abcz/dot_general | solution.py:128
  229.4 14.5 %copy.679 = f32[4,4,10,10,128,10]{4,2,0,5,1,3:T(8,128)} copy(f32[4,4,10,10,128,10]{4,5,3,2,1,0:T(8,128)} %fusion.4) | data formatting | bytes 16384000 | tf_op jit(solution)/shard_map/ck,...abkz->...abcz/dot_general | solution.py:128
  245.5 5.3 %collective-permute-start.15 = (f32[4,1,4,4,128]{4,3,2,0,1:T(4,128)S(1)}, f32[4,1,4,4,128]{4,3,2,0,1:T(4,128)S(1)}, u32[]{:S(2)}, u32[]{:S(2)}) collective-permute-start(f32[4,1,4,4,128]{4,3,2,0,1:T(4,128)S(1)} %get-tuple-element.53), channel_id=1, source_target_pairs={{1,0},{2,1},{3,2},{4,3},{5,4},{6,5},{7,6},{8,7},{9,8},{10,9},{11,1... | collective-permute-start | bytes 98312 | tf_op jit(solution)/shard_map/ppermute | solution.py:22
  251.5 3.3 slice.723
  254.8 3.8 copy.447
  258.7 5.4 %collective-permute-start.21 = (f32[4,1,2,2,128]{4,3,2,1,0:T(2,128)S(1)}, f32[4,1,2,2,128]{4,3,2,1,0:T(2,128)S(1)}, u32[]{:S(2)}, u32[]{:S(2)}) collective-permute-start(f32[4,1,2,2,128]{4,3,2,1,0:T(2,128)S(1)} %slice.786), channel_id=1, source_target_pairs={{1,0},{2,1},{3,2},{4,3},{5,4},{6,5},{7,6},{8,7},{9,8},{10,9},{11,1... | collective-permute-start | bytes 24584 | tf_op jit(solution)/shard_map/ppermute | solution.py:22
  278.6 3.0 fusion.62
  284.7 7.5 %collective-permute-done.16 = f32[4,1,4,4,128]{4,2,1,0,3:T(4,128)S(1)} collective-permute-done((f32[4,1,4,4,128]{4,2,1,0,3:T(4,128)S(1)}, f32[4,1,4,4,128]{4,2,1,0,3:T(4,128)S(1)}, u32[]{:S(2)}, u32[]{:S(2)}) %collective-permute-start.16) | collective-permute-done | bytes 32800 | tf_op jit(solution)/shard_map/ppermute | solution.py:20
  304.8 5.4 %collective-permute-start.7 = (f32[4,1,8,8,128]{4,2,0,3,1:T(8,128)S(1)}, f32[4,1,8,8,128]{4,2,0,3,1:T(8,128)S(1)}, u32[]{:S(2)}, u32[]{:S(2)}) collective-permute-start(f32[4,1,8,8,128]{4,2,0,3,1:T(8,128)S(1)} %slice.725), channel_id=1, source_target_pairs={{1,0},{2,1},{3,2},{4,3},{5,4},{6,5},{7,6},{8,7},{9,8},{10,9},{11,1... | collective-permute-start | bytes 393224 | tf_op jit(solution)/shard_map/ppermute | solution.py:22
  333.4 20.6 %all-gather.3.cloned.1.call-done = f32[512,4,1,1,1,128]{5,1,4,3,2,0:T(4,128)} async-done(((f32[4,4,1,1,1,128]{5,1,4,3,2,0:T(4,128)}), f32[512,4,1,1,1,128]{5,1,4,3,2,0:T(4,128)}) %all-gather.3.cloned.1.call-update) | async-done | bytes 1048592 | tf_op jit(solution)/shard_map/all_gather | solution.py:234
  371.4 4.3 %fusion.30 = f32[4,4,8,8,8,128]{5,4,3,1,2,0:T(8,128)S(1)} fusion(f32[4,4,1,8,8,128]{5,4,3,1,2,0:T(8,128)S(1)} %copy-done.8, f32[4,4,6,8,8,128]{5,4,3,1,2,0:T(8,128)S(1)} %slice.730, f32[4,4,1,8,8,128]{5,4,3,1,2,0:T(8,128)S(1)} %copy-done.7, f32[4,4,8,8,4,128]{5,3,4,2,1,0:T(8,128)S(1)} %convolution_bitcast_fusion, ...), kind=kOutput, calls=%fused_computation.34 | convolution fusion | flops 54525952 | bytes 10487936 | tf_op jit(solution)/shard_map/hk,...fgkz->...fghz/dot_general | solution.py:113
  (286 shorter events, 128.5 us)
Async XLA Ops:
  6.5 347.5 %all-gather.3.cloned.1.call-start = ((), (), s32[]{:S(2)}) async-start(), calls=%async_computation | async-start | bytes 1056768 | tf_op jit(solution)/shard_map/all_gather | solution.py:234
  10.2 10.1 %collective-permute-start = (f32[4,1,8,8,128]{4,2,0,3,1:T(8,128)S(1)}, f32[4,1,8,8,128]{4,2,0,3,1:T(8,128)S(1)}, u32[]{:S(2)}, u32[]{:S(2)}) collective-permute-start(f32[4,1,8,8,128]{4,2,0,3,1:T(8,128)S(1)} %bitcast.519), channel_id=1, source_target_pairs={{0,1},{1,2},{2,3},{3,4},{4,5},{5,6},{6,7},{7,8},{8,9},{9,10},{10,1... | collective-permute-start | bytes 393224 | tf_op jit(solution)/shard_map/ppermute | solution.py:20
  22.2 6.4 %collective-permute-start.1 = (f32[4,1,8,8,128]{4,1,2,0,3:T(1,128)S(1)}, f32[4,1,8,8,128]{4,1,2,0,3:T(1,128)S(1)}, u32[]{:S(2)}, u32[]{:S(2)}) collective-permute-start(f32[4,1,8,8,128]{4,1,2,0,3:T(1,128)S(1)} %slice.699), channel_id=1, source_target_pairs={{1,0},{2,1},{3,2},{4,3},{5,4},{6,5},{7,6},{8,7},{9,8},{10,9},{11,1... | collective-permute-start | bytes 393224 | tf_op jit(solution)/shard_map/ppermute | solution.py:22
  44.7 7.0 %collective-permute-start.2 = (f32[1,4,2,8,8,128]{5,4,3,1,2,0:T(8,128)S(1)}, f32[1,4,2,8,8,128]{5,4,3,1,2,0:T(8,128)S(1)}, u32[]{:S(2)}, u32[]{:S(2)}) collective-permute-start(f32[1,4,2,8,8,128]{5,4,3,1,2,0:T(8,128)S(1)} %get-tuple-element.24), channel_id=1, source_target_pairs={{0,16},{16,32},{32,48},{48,64},{64,80},{80,96},{96,112},{112,0},{1... | collective-permute-start | bytes 786440 | tf_op jit(solution)/shard_map/ppermute | solution.py:20
  44.7 7.0 %collective-permute-start.3 = (f32[1,4,2,8,8,128]{5,4,3,1,2,0:T(8,128)S(1)}, f32[1,4,2,8,8,128]{5,4,3,1,2,0:T(8,128)S(1)}, u32[]{:S(2)}, u32[]{:S(2)}) collective-permute-start(f32[1,4,2,8,8,128]{5,4,3,1,2,0:T(8,128)S(1)} %get-tuple-element.25), channel_id=1, source_target_pairs={{16,0},{32,16},{48,32},{64,48},{80,64},{96,80},{112,96},{0,112},{1... | collective-permute-start | bytes 786440 | tf_op jit(solution)/shard_map/ppermute | solution.py:22
  64.2 8.8 %collective-permute-start.11 = (f32[4,1,4,4,128]{4,3,2,0,1:T(4,128)S(1)}, f32[4,1,4,4,128]{4,3,2,0,1:T(4,128)S(1)}, u32[]{:S(2)}, u32[]{:S(2)}) collective-permute-start(f32[4,1,4,4,128]{4,3,2,0,1:T(4,128)S(1)} %slice.737), channel_id=1, source_target_pairs={{1,0},{2,1},{3,2},{4,3},{5,4},{6,5},{7,6},{8,7},{9,8},{10,9},{11,1... | collective-permute-start | bytes 98312 | tf_op jit(solution)/shard_map/ppermute | solution.py:22
  70.1 21.1 %collective-permute-start.5 = (f32[4,1,8,8,128]{4,3,2,0,1:T(8,128)S(1)}, f32[4,1,8,8,128]{4,3,2,0,1:T(8,128)S(1)}, u32[]{:S(2)}, u32[]{:S(2)}) collective-permute-start(f32[4,1,8,8,128]{4,3,2,0,1:T(8,128)S(1)} %get-tuple-element.34), channel_id=1, source_target_pairs={{1,0},{2,1},{3,2},{4,3},{5,4},{6,5},{7,6},{8,7},{9,8},{10,9},{11,1... | collective-permute-start | bytes 393224 | tf_op jit(solution)/shard_map/ppermute | solution.py:22
  70.2 21.3 %collective-permute-start.4 = (f32[4,1,8,8,128]{4,3,1,2,0:T(8,128)S(1)}, f32[4,1,8,8,128]{4,3,1,2,0:T(8,128)S(1)}, u32[]{:S(2)}, u32[]{:S(2)}) collective-permute-start(f32[4,1,8,8,128]{4,3,1,2,0:T(8,128)S(1)} %get-tuple-element.35), channel_id=1, source_target_pairs={{0,1},{1,2},{2,3},{3,4},{4,5},{5,6},{6,7},{7,8},{8,9},{9,10},{10,1... | collective-permute-start | bytes 393224 | tf_op jit(solution)/shard_map/ppermute | solution.py:20
  73.2 7.3 %collective-permute-start.10 = (f32[4,1,4,4,128]{4,3,2,0,1:T(4,128)S(1)}, f32[4,1,4,4,128]{4,3,2,0,1:T(4,128)S(1)}, u32[]{:S(2)}, u32[]{:S(2)}) collective-permute-start(f32[4,1,4,4,128]{4,3,2,0,1:T(4,128)S(1)} %slice.733), channel_id=1, source_target_pairs={{0,1},{1,2},{2,3},{3,4},{4,5},{5,6},{6,7},{7,8},{8,9},{9,10},{10,1... | collective-permute-start | bytes 98312 | tf_op jit(solution)/shard_map/ppermute | solution.py:20
  82.0 3.4 collective-permute-start.13
  83.6 4.9 %collective-permute-start.12 = (f32[1,4,2,4,4,128]{5,4,3,1,2,0:T(4,128)S(1)}, f32[1,4,2,4,4,128]{5,4,3,1,2,0:T(4,128)S(1)}, u32[]{:S(2)}, u32[]{:S(2)}) collective-permute-start(f32[1,4,2,4,4,128]{5,4,3,1,2,0:T(4,128)S(1)} %copy.569), channel_id=1, source_target_pairs={{0,16},{16,32},{32,48},{48,64},{64,80},{80,96},{96,112},{112,0},{1... | collective-permute-start | bytes 196616 | tf_op jit(solution)/shard_map/ppermute | solution.py:20
  245.4 13.2 %collective-permute-start.20 = (f32[4,1,2,2,128]{4,3,2,1,0:T(2,128)S(1)}, f32[4,1,2,2,128]{4,3,2,1,0:T(2,128)S(1)}, u32[]{:S(2)}, u32[]{:S(2)}) collective-permute-start(f32[4,1,2,2,128]{4,3,2,1,0:T(2,128)S(1)} %slice.783), channel_id=1, source_target_pairs={{0,1},{1,2},{2,3},{3,4},{4,5},{5,6},{6,7},{7,8},{8,9},{9,10},{10,1... | collective-permute-start | bytes 24584 | tf_op jit(solution)/shard_map/ppermute | solution.py:20
  245.5 21.5 %collective-permute-start.15 = (f32[4,1,4,4,128]{4,3,2,0,1:T(4,128)S(1)}, f32[4,1,4,4,128]{4,3,2,0,1:T(4,128)S(1)}, u32[]{:S(2)}, u32[]{:S(2)}) collective-permute-start(f32[4,1,4,4,128]{4,3,2,0,1:T(4,128)S(1)} %get-tuple-element.53), channel_id=1, source_target_pairs={{1,0},{2,1},{3,2},{4,3},{5,4},{6,5},{7,6},{8,7},{9,8},{10,9},{11,1... | collective-permute-start | bytes 98312 | tf_op jit(solution)/shard_map/ppermute | solution.py:22
  250.8 16.2 %collective-permute-start.14 = (f32[4,1,4,4,128]{4,3,2,1,0:T(4,128)S(1)}, f32[4,1,4,4,128]{4,3,2,1,0:T(4,128)S(1)}, u32[]{:S(2)}, u32[]{:S(2)}) collective-permute-start(f32[4,1,4,4,128]{4,3,2,1,0:T(4,128)S(1)} %get-tuple-element.54), channel_id=1, source_target_pairs={{0,1},{1,2},{2,3},{3,4},{4,5},{5,6},{6,7},{7,8},{8,9},{9,10},{10,1... | collective-permute-start | bytes 98312 | tf_op jit(solution)/shard_map/ppermute | solution.py:20
  251.1 50.8 %collective-permute-start.6 = (f32[4,1,8,8,128]{4,2,0,3,1:T(8,128)S(1)}, f32[4,1,8,8,128]{4,2,0,3,1:T(8,128)S(1)}, u32[]{:S(2)}, u32[]{:S(2)}) collective-permute-start(f32[4,1,8,8,128]{4,2,0,3,1:T(8,128)S(1)} %slice.721), channel_id=1, source_target_pairs={{0,1},{1,2},{2,3},{3,4},{4,5},{5,6},{6,7},{7,8},{8,9},{9,10},{10,1... | collective-permute-start | bytes 393224 | tf_op jit(solution)/shard_map/ppermute | solution.py:20
  258.7 6.8 %collective-permute-start.21 = (f32[4,1,2,2,128]{4,3,2,1,0:T(2,128)S(1)}, f32[4,1,2,2,128]{4,3,2,1,0:T(2,128)S(1)}, u32[]{:S(2)}, u32[]{:S(2)}) collective-permute-start(f32[4,1,2,2,128]{4,3,2,1,0:T(2,128)S(1)} %slice.786), channel_id=1, source_target_pairs={{1,0},{2,1},{3,2},{4,3},{5,4},{6,5},{7,6},{8,7},{9,8},{10,9},{11,1... | collective-permute-start | bytes 24584 | tf_op jit(solution)/shard_map/ppermute | solution.py:22
  266.9 28.0 %collective-permute-start.22 = (f32[1,4,1,2,2,128]{5,4,3,2,1,0:T(2,128)S(1)}, f32[1,4,1,2,2,128]{5,4,3,2,1,0:T(2,128)S(1)}, u32[]{:S(2)}, u32[]{:S(2)}) collective-permute-start(f32[1,4,1,2,2,128]{5,4,3,2,1,0:T(2,128)S(1)} %fusion.129), channel_id=1, source_target_pairs={{0,16},{16,32},{32,48},{48,64},{64,80},{80,96},{96,112},{112,0},{1... | collective-permute-start | bytes 24584 | tf_op jit(solution)/shard_map/ppermute | solution.py:20
  284.6 7.6 %collective-permute-start.16 = (f32[4,1,4,4,128]{4,2,1,0,3:T(4,128)S(1)}, f32[4,1,4,4,128]{4,2,1,0,3:T(4,128)S(1)}, u32[]{:S(2)}, u32[]{:S(2)}) collective-permute-start(f32[4,1,4,4,128]{4,2,1,0,3:T(4,128)S(1)} %slice.767), channel_id=1, source_target_pairs={{0,1},{1,2},{2,3},{3,4},{4,5},{5,6},{6,7},{7,8},{8,9},{9,10},{10,1... | collective-permute-start | bytes 98312 | tf_op jit(solution)/shard_map/ppermute | solution.py:20
  292.9 4.1 %collective-permute-start.17 = (f32[4,1,4,4,128]{4,2,1,0,3:T(4,128)}, f32[4,1,4,4,128]{4,2,1,0,3:T(4,128)S(1)}, u32[]{:S(2)}, u32[]{:S(2)}) collective-permute-start(f32[4,1,4,4,128]{4,2,1,0,3:T(4,128)} %slice.771), channel_id=1, source_target_pairs={{1,0},{2,1},{3,2},{4,3},{5,4},{6,5},{7,6},{8,7},{9,8},{10,9},{11,1... | collective-permute-start | bytes 98312 | tf_op jit(solution)/shard_map/ppermute | solution.py:22
  298.9 11.3 %collective-permute-start.18 = (f32[1,4,1,4,4,128]{5,4,3,2,1,0:T(4,128)S(1)}, f32[1,4,1,4,4,128]{5,4,3,2,1,0:T(4,128)S(1)}, u32[]{:S(2)}, u32[]{:S(2)}) collective-permute-start(f32[1,4,1,4,4,128]{5,4,3,2,1,0:T(4,128)S(1)} %get-tuple-element.45), channel_id=1, source_target_pairs={{0,16},{16,32},{32,48},{48,64},{64,80},{80,96},{96,112},{112,0},{1... | collective-permute-start | bytes 98312 | tf_op jit(solution)/shard_map/ppermute | solution.py:20
  299.0 11.3 %collective-permute-start.19 = (f32[1,4,1,4,4,128]{5,4,3,2,1,0:T(4,128)S(1)}, f32[1,4,1,4,4,128]{5,4,3,2,1,0:T(4,128)S(1)}, u32[]{:S(2)}, u32[]{:S(2)}) collective-permute-start(f32[1,4,1,4,4,128]{5,4,3,2,1,0:T(4,128)S(1)} %get-tuple-element.46), channel_id=1, source_target_pairs={{16,0},{32,16},{48,32},{64,48},{80,64},{96,80},{112,96},{0,112},{1... | collective-permute-start | bytes 98312 | tf_op jit(solution)/shard_map/ppermute | solution.py:22
  304.8 7.9 %collective-permute-start.7 = (f32[4,1,8,8,128]{4,2,0,3,1:T(8,128)S(1)}, f32[4,1,8,8,128]{4,2,0,3,1:T(8,128)S(1)}, u32[]{:S(2)}, u32[]{:S(2)}) collective-permute-start(f32[4,1,8,8,128]{4,2,0,3,1:T(8,128)S(1)} %slice.725), channel_id=1, source_target_pairs={{1,0},{2,1},{3,2},{4,3},{5,4},{6,5},{7,6},{8,7},{9,8},{10,9},{11,1... | collective-permute-start | bytes 393224 | tf_op jit(solution)/shard_map/ppermute | solution.py:22
  326.4 5.7 %collective-permute-start.8 = (f32[1,4,1,8,8,128]{5,4,3,1,2,0:T(8,128)S(1)}, f32[1,4,1,8,8,128]{5,4,3,1,2,0:T(8,128)S(1)}, u32[]{:S(2)}, u32[]{:S(2)}) collective-permute-start(f32[1,4,1,8,8,128]{5,4,3,1,2,0:T(8,128)S(1)} %get-tuple-element.20), channel_id=1, source_target_pairs={{0,16},{16,32},{32,48},{48,64},{64,80},{80,96},{96,112},{112,0},{1... | collective-permute-start | bytes 393224 | tf_op jit(solution)/shard_map/ppermute | solution.py:20
  326.4 5.6 %collective-permute-start.9 = (f32[1,4,1,8,8,128]{5,4,3,1,2,0:T(8,128)S(1)}, f32[1,4,1,8,8,128]{5,4,3,1,2,0:T(8,128)S(1)}, u32[]{:S(2)}, u32[]{:S(2)}) collective-permute-start(f32[1,4,1,8,8,128]{5,4,3,1,2,0:T(8,128)S(1)} %get-tuple-element.21), channel_id=1, source_target_pairs={{16,0},{32,16},{48,32},{64,48},{80,64},{96,80},{112,96},{0,112},{1... | collective-permute-start | bytes 393224 | tf_op jit(solution)/shard_map/ppermute | solution.py:22
  (19 other events, 211.8 us)
Sparse Core Ops, SparseCore 0:
  295.7 58.3 all-gather.2
where the time goes:
time: 392 us; the launch traced here: 385 us
  matrix products  177 us (45%)
  local copies, waits for them, and re-layouts  64 us (16%)
  waiting for transfers between devices  51.9 us (13%)
  starting transfers between devices  42.2 us (11%)
  other arithmetic  34.7 us (9%)
  between operations  15.1 us (4%)
    ppermute x11, starting transfers between devices, extended_2(): lax.ppermute(head, axis, [((i + 1) % count, i) for i in range(count)])  38.2 us
    dot_general x2, matrix products, local_solve(): jnp.einsum('ai,...ijkz->...ajkz', eigen_basis[0], spectrum, precision=HIG...  26.7 us
    dot_general x2, matrix products, local_solve(): jnp.einsum('ck,...ijcz->...ijkz', eigen_basis[2], spectrum, precision=HIG...  26.7 us
    dot_general x2, matrix products, local_solve(): jnp.einsum('ck,...abkz->...abcz', eigen_basis[2], result, precision=HIGHEST)  25.2 us
    dot_general x2, matrix products, local_solve(): jnp.einsum('bj,...ajkz->...abkz', eigen_basis[1], result, precision=HIGHEST)  24.4 us
    dot_general x2, matrix products, local_solve(): jnp.einsum('bj,...ibcz->...ijcz', eigen_basis[1], spectrum, precision=HIG...  24.2 us
    ppermute x12, waiting for transfers between devices, extended_2(): lax.ppermute(tail, axis, [(i, (i + 1) % count) for i in range(count)])  22.3 us
    all_gather x1, waiting for transfers between devices, on_device(): gathered = lax.all_gather(vertex, ('px', 'py'), axis=0, tiled=True)  20.6 us
  transfers between devices with their start and end apart: 24, of which 12 were waited for; matrix products, arithmetic and copies ran while one was open for 17% of the time, Pallas kernels for 0%

commit v1 on v0

v1 whole, which is shorter than its diff:
```python
import functools
import math

import jax
import jax.numpy as jnp
import ml_dtypes
import numpy as np
from jax import lax
from jax.experimental import pallas as pl
from jax.experimental.pallas import tpu as pltpu
from jax.sharding import PartitionSpec as P

F32, BF16 = jnp.float32, jnp.bfloat16
HIGHEST = lax.Precision.HIGHEST
LANES = 128
EX = EY = 4
VMEM_LIMIT = 56 * 1024 * 1024


def lobatto(count):
    return -np.cos(np.arange(count) * (np.pi / (count - 1)))


def interpolation(fine_count, coarse_count):
    fine, coarse = lobatto(fine_count), lobatto(coarse_count)
    out = np.ones((fine_count, coarse_count))
    for j in range(coarse_count):
        for m in range(coarse_count):
            if m != j:
                out[:, j] *= (fine - coarse[m]) / (coarse[j] - coarse[m])
    return out


def hartley(count):
    phase = np.outer(np.arange(count), np.arange(count)) % count
    angle = phase * (2.0 * np.pi / count)
    return np.cos(angle) + np.sin(angle)


def line_eigen(count):
    return 2.0 - 2.0 * np.cos(np.arange(count) * (2.0 * np.pi / count))


def split_np(values):
    values = np.asarray(values, np.float32)
    high = values.astype(ml_dtypes.bfloat16)
    low = (values - high.astype(np.float32)).astype(ml_dtypes.bfloat16)
    return high, low


def split(values):
    high = values.astype(BF16)
    return high, (values - high.astype(F32)).astype(BF16)


def dot(left, right):
    return jnp.dot(left, right, preferred_element_type=F32)


def exact_dot(left, right, contract=((1,), (0,))):
    return lax.dot_general(
        left, right, (contract, ((), ())), precision=HIGHEST, preferred_element_type=F32
    )


INTERP_FINE = interpolation(8, 4)
INTERP_MID = interpolation(4, 2)
INTERP_ALL = INTERP_FINE @ INTERP_MID


def kron3(m):
    return np.kron(np.kron(m, m), m)


def restrict_matrix():
    rows = np.zeros((80, 512))
    rows[:64] = kron3(INTERP_FINE).T
    rows[64:72] = kron3(INTERP_ALL).T
    high, low = split_np(rows)
    return np.concatenate([high, low], axis=0)


def prolong_matrix():
    fine = kron3(INTERP_FINE)
    coarse = np.zeros((512, 16))
    coarse[:, :8] = kron3(INTERP_ALL)
    fine_high, fine_low = split_np(fine)
    coarse_high, coarse_low = split_np(coarse)
    return np.concatenate(
        [fine_high, fine_high, fine_low, coarse_high, coarse_high, coarse_low], axis=1
    )


def vertex_matrices():
    out = np.zeros((2, 32, 128), np.float32)
    for ex in range(EX):
        for ey in range(EY):
            for i in (0, 1):
                for j in (0, 1):
                    for k in (0, 1):
                        column = (ex * EY + ey) * 8 + i * 4 + j * 2 + k
                        out[k, (ex + i) * 5 + ey + j, column] = 1.0
    return out


class Level:
    def __init__(self, n):
        self.n = n
        self.wide = n + 2
        self.core = n * n
        self.rim = 4 * n
        self.depth = self.core + self.rim
        self.modes = -(-(self.wide * self.wide) // 16) * 16
        self.planes = EX * n + 4

    def tables(self):
        n, wide = self.n, self.wide
        first = np.zeros((2 * self.modes, wide), np.float32)
        second = np.zeros((2 * self.modes, wide), np.float32)
        for half in (0, 1):
            for j in range(wide):
                for k in range(wide):
                    first[half * self.modes + j * wide + k, j] = 1.0
                    second[half * self.modes + j * wide + k, k] = 1.0
        inner = list(range(1, n + 1))
        points = [(b, c) for b in inner for c in inner]
        points += [(0, c) for c in inner] + [(n + 1, c) for c in inner]
        points += [(b, 0) for b in inner] + [(b, n + 1) for b in inner]
        pick_b = np.zeros((wide, 2 * self.depth), np.float32)
        pick_c = np.zeros((wide, 2 * self.depth), np.float32)
        for half in (0, 1):
            for column, (b, c) in enumerate(points):
                pick_b[b, half * self.depth + column] = 1.0
                pick_c[c, half * self.depth + column] = 1.0
        return (
            first,
            second,
            pick_b,
            pick_c,
            np.ascontiguousarray(pick_b[:, : self.core].T),
            np.ascontiguousarray(pick_c[:, : self.core].T),
        )


FINE, MID = Level(8), Level(4)

HALO_ROWS = 640
DIAG_ROWS = 40
FACE_ROWS = 320
EDGE_ROWS = 16


def pack_kernel(
    residual,
    restrict,
    vertex_pick,
    hartley_z,
    x_up,
    x_down,
    y_up,
    y_down,
    d_uu,
    d_ud,
    d_du,
    d_dd,
    middle,
    vertex,
    field,
    corners,
    sems,
):
    copies = []
    for ex in range(EX):
        copy = pltpu.make_async_copy(residual.at[ex], field.at[ex], sems.at[ex])
        copy.start()
        copies.append(copy)
    for ex in range(EX):
        copies[ex].wait()
        for pair in range(EY // 2):
            ey = 2 * pair
            values = jnp.concatenate(
                [field[ex, ey].reshape(512, LANES), field[ex, ey + 1].reshape(512, LANES)], axis=1
            )
            high, low = split(values)
            upper = dot(restrict[...], high)
            lower = dot(restrict[0:80, :], low)
            total = upper[0:80] + upper[80:160] + lower
            for h in (0, 1):
                part = total[:, h * LANES : (h + 1) * LANES]
                for i in range(4):
                    middle[ex, ey + h, i] = part[16 * i : 16 * i + 16]
                column = ex * EY + ey + h
                corners[8 * column : 8 * column + 8] = part[64:72]
    for out, ex, nodes, mids in ((x_up, EX - 1, (7, 6), (3, 2)), (x_down, 0, (0, 1), (0, 1))):
        for layer in (0, 1):
            for ey in range(EY):
                row = (layer * EY + ey) * 64
                out[row : row + 64] = field[ex, ey, nodes[layer]]
                row = 512 + (layer * EY + ey) * 16
                out[row : row + 16] = middle[ex, ey, mids[layer]]
    for out, ey, nodes, mids in ((y_up, EY - 1, (7, 6), (3, 2)), (y_down, 0, (0, 1), (0, 1))):
        for layer in (0, 1):
            for ex in range(EX):
                for a in range(8):
                    row = (layer * EX + ex) * 64 + a * 8
                    line = nodes[layer] * 8
                    out[row : row + 8] = field[ex, ey, a, line : line + 8]
                for a in range(4):
                    row = 512 + (layer * EX + ex) * 16 + a * 4
                    line = mids[layer] * 4
                    out[row : row + 4] = middle[ex, ey, a, line : line + 4]
    for out, up_x, up_y in ((d_uu, 1, 1), (d_ud, 1, 0), (d_du, 0, 1), (d_dd, 0, 0)):
        ex, ey = (EX - 1) * up_x, (EY - 1) * up_y
        out[32:40] = jnp.zeros((8, LANES), F32)
        for n, source, base in ((8, field, 0), (4, middle, 24)):
            face_a, inner_a = (n - 1, n - 2) if up_x else (0, 1)
            face_b, inner_b = (n - 1, n - 2) if up_y else (0, 1)
            for line, (a, b) in enumerate(((face_a, face_b), (face_a, inner_b), (inner_a, face_b))):
                out[base + line * n : base + line * n + n] = source[ex, ey, a, b * n : b * n + n]
    values = corners[...]
    low = exact_dot(vertex_pick[0], values)
    high = exact_dot(vertex_pick[1], values)
    total = low + pltpu.roll(high, 1, 1)
    vertex[...] = exact_dot(total, hartley_z[...])


def pack(residual):
    halo = jax.ShapeDtypeStruct((HALO_ROWS, LANES), F32)
    diag = jax.ShapeDtypeStruct((DIAG_ROWS, LANES), F32)
    vmem = pl.BlockSpec(memory_space=pltpu.VMEM)
    return pl.pallas_call(
        pack_kernel,
        out_shape=[halo] * 4
        + [diag] * 4
        + [
            jax.ShapeDtypeStruct((EX, EY, 4, 16, LANES), F32),
            jax.ShapeDtypeStruct((32, LANES), F32),
        ],
        in_specs=[pl.BlockSpec(memory_space=pl.ANY)] + [vmem] * 3,
        out_specs=[vmem] * 10,
        scratch_shapes=[
            pltpu.VMEM((EX, EY, 8, 64, LANES), F32),
            pltpu.VMEM((128, LANES), F32),
            pltpu.SemaphoreType.DMA((EX,)),
        ],
        compiler_params=pltpu.CompilerParams(vmem_limit_bytes=VMEM_LIMIT),
        cost_estimate=pl.CostEstimate(flops=10**9, bytes_accessed=8 * 10**6, transcendentals=0),
        name="pack",
    )(
        residual,
        jnp.asarray(restrict_matrix()),
        jnp.asarray(vertex_matrices()),
        jnp.asarray(hartley(128), F32),
    )


def sum_lines(ref, lead, n, scale=None):
    count = ref.shape[-2] // n
    low_rows = lead + (pl.ds(0, count, stride=n), slice(None))
    high_rows = lead + (pl.ds(n - 1, count, stride=n), slice(None))
    low, high = ref[low_rows], ref[high_rows]
    new_low = low + pltpu.roll(high, 1, 1)
    new_high = high + pltpu.roll(low, LANES - 1, 1)
    if scale is not None:
        new_low, new_high = new_low * scale, new_high * scale
    ref[low_rows] = new_low
    ref[high_rows] = new_high


def halo_lines(level, halo, layer, plane):
    n = level.n
    start = layer * EX * n * n + plane * n + (0 if n == 8 else 512)
    return halo[start : start + n]


def diag_line(level, diag, line):
    n = level.n
    start = line * n + (0 if n == 8 else 24)
    return diag[start : start + n]


def assemble(level, planes, rims, sides, x_low, x_high, y_low, y_high, diags):
    n, core = level.n, level.core
    last = EX * n + 3
    base = 0 if n == 8 else 512
    for ey in range(EY):
        row = base + ey * core
        planes[ey, 2] += x_low[row : row + core]
        planes[ey, last - 2] += x_high[row : row + core]
        for ex in range(EX - 1):
            left = 2 + ex * n + n - 1
            total = planes[ey, left] + planes[ey, left + 1]
            planes[ey, left] = total
            planes[ey, left + 1] = total
        row = base + (EY + ey) * core
        planes[ey, 0] = x_low[row : row + core]
        planes[ey, last] = x_high[row : row + core]
    for side, halo in ((0, y_low), (1, y_high)):
        for layer in (0, 1):
            kind = 2 * side + layer
            start = base + layer * EX * core
            sides[kind] = halo[start : start + EX * core]
            sides[kind, 0:n] += diag_line(level, diags[0][side], layer)
            sides[kind, EX * core - n : EX * core] += diag_line(level, diags[1][side], layer)
            for ex in range(EX - 1):
                row = ex * core + core
                total = sides[kind, row - n : row] + sides[kind, row : row + n]
                sides[kind, row - n : row] = total
                sides[kind, row : row + n] = total
    for plane in range(EX * n):
        row = plane * n
        planes[0, 2 + plane, 0:n] += sides[0, row : row + n]
        planes[EY - 1, 2 + plane, core - n : core] += sides[2, row : row + n]
    for plane, diag in ((0, diags[0]), (last, diags[1])):
        planes[0, plane, 0:n] += diag_line(level, diag[0], 2)
        planes[EY - 1, plane, core - n : core] += diag_line(level, diag[1], 2)
    for ey in range(EY - 1):
        for plane in [0, last] + list(range(2, 2 + EX * n)):
            total = planes[ey, plane, core - n : core] + planes[ey + 1, plane, 0:n]
            planes[ey, plane, core - n : core] = total
            planes[ey + 1, plane, 0:n] = total
    for ey in range(EY):
        for plane in [0, last] + list(range(2, 2 + EX * n)):
            sum_lines(planes, (ey, plane), n)
    for kind in (1, 3):
        sum_lines(sides, (kind,), n)
    for ey in range(EY):
        for plane in range(EX * n):
            at = 2 + plane
            row = plane * n
            low = planes[ey - 1, at, core - 2 * n : core - n] if ey else sides[1, row : row + n]
            high = planes[ey + 1, at, n : 2 * n] if ey < EY - 1 else sides[3, row : row + n]
            rims[ey, plane, 0:n] = low
            rims[ey, plane, n : 2 * n] = high
            rims[ey, plane, 2 * n : 3 * n] = pltpu.roll(
                planes[ey, at, pl.ds(n - 2, n, stride=n), :], 1, 1
            )
            rims[ey, plane, 3 * n : 4 * n] = pltpu.roll(
                planes[ey, at, pl.ds(1, n, stride=n), :], LANES - 1, 1
            )


def build_tables(level, tables, basis, eigen, forward, backward, inverse):
    first, second, pick_b, pick_c, core_b, core_c = tables
    modes, depth = level.modes, level.depth
    rows_b = exact_dot(first[0:modes], basis[1], ((1,), (1,)))
    rows_c = exact_dot(second[0:modes], basis[2], ((1,), (1,)))
    matrix = exact_dot(rows_b, pick_b[...]) * exact_dot(rows_c, pick_c[...])
    high, low = split(matrix)
    keep = lax.broadcasted_iota(jnp.int32, matrix.shape, 1) < depth
    forward[0:modes] = high
    forward[modes : 2 * modes] = jnp.where(keep, low.astype(F32), 0.0).astype(BF16)
    out_b = exact_dot(exact_dot(core_b[...], basis[1]), first[...], ((1,), (1,)))
    out_c = exact_dot(exact_dot(core_c[...], basis[2]), second[...], ((1,), (1,)))
    matrix = out_b * out_c
    high, low = split(matrix)
    keep = lax.broadcasted_iota(jnp.int32, matrix.shape, 1) < modes
    backward[0 : level.core] = high
    backward[level.core : 2 * level.core] = jnp.where(keep, low.astype(F32), 0.0).astype(BF16)
    wide = level.wide
    spread_b = jnp.broadcast_to(eigen[1:2, :], (LANES, wide))
    spread_c = jnp.broadcast_to(eigen[2:3, :], (LANES, wide))
    lines = exact_dot(first[0:modes], spread_b, ((1,), (1,)))
    lines += exact_dot(second[0:modes], spread_c, ((1,), (1,)))
    for i in range(wide):
        inverse[i] = 1.0 / (lines + eigen[0:1, i : i + 1])


def solve_pair(level, q, planes, rims, coeff, forward, backward, inverse, scale, spectrum, hats, out):
    n, wide, core, modes, depth = level.n, level.wide, level.core, level.modes, level.depth
    ex = q // 2
    ey = (q % 2) * 2
    base = ex * n
    offsets = [0] + [2 + a for a in range(n)] + [n + 3]

    def contract(load, nodes, row):
        held = [[load(h, e) for h in (0, 1)] for e in nodes]
        for i in range(wide):
            for h in (0, 1):
                total = coeff[nodes[0], i] * held[0][h]
                for position in range(1, len(nodes)):
                    total += coeff[nodes[position], i] * held[position][h]
                high, low = split(total)
                lanes = slice(h * LANES, (h + 1) * LANES)
                spectrum[i, row : row + 16, lanes] = high
                spectrum[i, depth + row : depth + row + 16, lanes] = low

    for row in range(0, core, 16):
        contract(
            lambda h, e, row=row: planes[ey + h, base + offsets[e], row : row + 16],
            list(range(wide)),
            row,
        )
    for row in range(0, level.rim, 16):
        contract(
            lambda h, e, row=row: rims[ey + h, base + e - 1, row : row + 16],
            list(range(1, n + 1)),
            core + row,
        )
    for i in range(wide):
        both = dot(forward[...], spectrum[i])
        damp = inverse[i]
        hat = (both[0:modes] + both[modes : 2 * modes]) * jnp.concatenate([damp, damp], axis=1)
        high, low = split(hat)
        both = dot(backward[...], jnp.concatenate([high, low], axis=0))
        hats[i] = both[0:core] + both[core : 2 * core]
    for h in (0, 1):
        inv = 1.0 / scale[ex, pl.ds(ey + h, 1), :]
        lanes = slice(h * LANES, (h + 1) * LANES)
        for row in range(0, core, 16):
            held = [hats[i, row : row + 16, lanes] for i in range(wide)]
            for a in range(n):
                total = coeff[a + 1, 0] * held[0]
                for i in range(1, wide):
                    total += coeff[a + 1, i] * held[i]
                out[q, h, a, row : row + 16] = total * inv


def schwarz_kernel(
    residual,
    middle,
    scale,
    fine_basis,
    fine_coeff,
    fine_eigen,
    middle_basis,
    middle_coeff,
    middle_eigen,
    *refs,
):
    halos, refs = refs[:8], refs[8:]
    fine_tables, refs = refs[:6], refs[6:]
    middle_tables, refs = refs[:6], refs[6:]
    fine_out, middle_out, refs = refs[0], refs[1], refs[2:]
    sends, refs = refs[:8], refs[8:]
    (
        planes,
        rims,
        sides,
        forward,
        backward,
        inverse,
        spectrum,
        hats,
        planes_m,
        rims_m,
        sides_m,
        forward_m,
        backward_m,
        inverse_m,
        spectrum_m,
        hats_m,
        solved,
        in_sems,
        out_sems,
    ) = refs
    x_low, x_high, y_low, y_high, d_ll, d_lh, d_hl, d_hh = halos
    diags = ((d_ll, d_lh), (d_hl, d_hh))
    copies = []
    for ex in range(EX):
        for ey in range(EY):
            copy = pltpu.make_async_copy(
                residual.at[ex, ey], planes.at[ey, pl.ds(2 + 8 * ex, 8)], in_sems.at[ex * EY + ey]
            )
            copy.start()
            copies.append(copy)
    for ex in range(EX):
        for ey in range(EY):
            planes_m[ey, 2 + 4 * ex : 6 + 4 * ex] = middle[ex, ey]
    build_tables(FINE, fine_tables, fine_basis, fine_eigen, forward, backward, inverse)
    build_tables(MID, middle_tables, middle_basis, middle_eigen, forward_m, backward_m, inverse_m)
    assemble(MID, planes_m, rims_m, sides_m, x_low, x_high, y_low, y_high, diags)

    def middle_step(q, carry):
        solve_pair(
            MID, q, planes_m, rims_m, middle_coeff, forward_m, backward_m, inverse_m, scale,
            spectrum_m, hats_m, middle_out,
        )
        return carry

    lax.fori_loop(0, 8, middle_step, 0)
    for copy in copies:
        copy.wait()
    assemble(FINE, planes, rims, sides, x_low, x_high, y_low, y_high, diags)

    def fine_step(q, carry):
        solve_pair(
            FINE, q, planes, rims, fine_coeff, forward, backward, inverse, scale,
            spectrum, hats, solved,
        )
        pltpu.make_async_copy(solved.at[q], fine_out.at[q], out_sems.at[q]).start()
        return carry

    lax.fori_loop(0, 8, fine_step, 0)

    x_up, x_down, y_up, y_down, d_uu, d_ud, d_du, d_dd = sends
    for n, source, base in ((8, solved, 0), (4, middle_out, 256)):
        core = n * n
        for out, ex, node in ((x_up, EX - 1, n - 1), (x_down, 0, 0)):
            for ey in range(EY):
                row = base + ey * core
                out[row : row + core] = source[2 * ex + ey // 2, ey % 2, node]
        for out, ey, node in ((y_up, EY - 1, n - 1), (y_down, 0, 0)):
            for ex in range(EX):
                for a in range(n):
                    row = base + (ex * n + a) * n
                    out[row : row + n] = source[
                        2 * ex + ey // 2, ey % 2, a, node * n : node * n + n
                    ]
    for out, up_x, up_y in ((d_uu, 1, 1), (d_ud, 1, 0), (d_du, 0, 1), (d_dd, 0, 0)):
        out[8:16] = jnp.zeros((8, LANES), F32)
        for n, source, base in ((8, solved, 0), (4, middle_out, 8)):
            a, b = (n - 1) * up_x, (n - 1) * up_y
            q, h = 2 * (EX - 1) * up_x + up_y, up_y
            out[base : base + n] = source[q, h, a, b * n : b * n + n]
    for q in range(8):
        pltpu.make_async_copy(solved.at[q], fine_out.at[q], out_sems.at[q]).wait()


def schwarz(residual, middle, scale, fine_basis, fine_eigen, middle_basis, middle_eigen, halos):
    vmem = pl.BlockSpec(memory_space=pltpu.VMEM)
    smem = pl.BlockSpec(memory_space=pltpu.SMEM)
    hbm = pl.BlockSpec(memory_space=pl.ANY)
    tables = [jnp.asarray(t) for level in (FINE, MID) for t in level.tables()]
    face = jax.ShapeDtypeStruct((FACE_ROWS, LANES), F32)
    edge = jax.ShapeDtypeStruct((EDGE_ROWS, LANES), F32)

    def scratch(level):
        return [
            pltpu.VMEM((EY, level.planes, level.core, LANES), F32),
            pltpu.VMEM((EY, EX * level.n, level.rim, LANES), F32),
            pltpu.VMEM((4, EX * level.core, LANES), F32),
            pltpu.VMEM((2 * level.modes, 2 * level.depth), BF16),
            pltpu.VMEM((2 * level.core, 2 * level.modes), BF16),
            pltpu.VMEM((level.wide, level.modes, LANES), F32),
            pltpu.VMEM((level.wide, 2 * level.depth, 2 * LANES), BF16),
            pltpu.VMEM((level.wide, level.core, 2 * LANES), F32),
        ]

    return pl.pallas_call(
        schwarz_kernel,
        out_shape=[
            jax.ShapeDtypeStruct((8, 2, 8, 64, LANES), F32),
            jax.ShapeDtypeStruct((8, 2, 4, 16, LANES), F32),
        ]
        + [face] * 4
        + [edge] * 4,
        in_specs=[hbm, vmem, vmem, vmem, smem, vmem, vmem, smem, vmem] + [vmem] * 20,
        out_specs=[hbm] + [vmem] * 9,
        scratch_shapes=scratch(FINE)
        + scratch(MID)
        + [
            pltpu.VMEM((8, 2, 8, 64, LANES), F32),
            pltpu.SemaphoreType.DMA((16,)),
            pltpu.SemaphoreType.DMA((8,)),
        ],
        compiler_params=pltpu.CompilerParams(vmem_limit_bytes=VMEM_LIMIT),
        cost_estimate=pl.CostEstimate(
            flops=8 * 10**9, bytes_accessed=12 * 10**6, transcendentals=0
        ),
        name="schwarz",
    )(
        residual, middle, scale, fine_basis, fine_basis[0], fine_eigen,
        middle_basis, middle_basis[0], middle_eigen, *halos, *tables,
    )


def coarse_kernel(place, rows_x, gathered, forward_y, back_y, hartley_z, lines, out, held, part):
    own_x, own_y = place[0], place[1]

    def y_step(p, carry):
        before = lax.rem(p + 7, 8)
        slabs = []
        for lx in range(4):
            pieces = []
            for ly in range(5):
                piece = gathered[pl.ds(p * 512 + lx * 5 + ly, 16, stride=32), :]
                if lx == 0:
                    piece += gathered[pl.ds(before * 512 + 20 + ly, 16, stride=32), :]
                pieces.append(piece)
            slabs.append(jnp.concatenate(pieces, axis=0))
        for half in (0, 2):
            high, low = split(jnp.concatenate([slabs[half], slabs[half + 1]], axis=1))
            both = dot(forward_y[...], jnp.concatenate([high, low], axis=0))
            total = both[0:64] + both[64:128]
            held[4 * p + half] = total[:, 0:LANES]
            held[4 * p + half + 1] = total[:, LANES : 2 * LANES]
        return carry

    lax.fori_loop(0, 8, y_step, 0)
    angle = 2.0 * np.pi / 32
    eigen_x = line_eigen(32)

    def x_step(chunk, carry):
        rows = pl.ds(pl.multiple_of(chunk * 8, 8), 8)
        values = [held[x, rows, :] for x in range(32)]
        even = [values[0]] + [values[x] + values[32 - x] for x in range(1, 16)] + [values[16]]
        odd = [None] + [values[x] - values[32 - x] for x in range(1, 16)]
        base = lines[rows, :]
        totals = [None] * 5
        for k in range(17):
            cosine = even[0]
            for x in range(1, 17):
                cosine = cosine + float(np.cos(angle * (k * x % 32))) * even[x]
            modes = [(k, cosine)]
            if 0 < k < 16:
                sine = float(np.sin(angle * k)) * odd[1]
                for x in range(2, 16):
                    sine = sine + float(np.sin(angle * (k * x % 32))) * odd[x]
                modes = [(k, cosine + sine), (32 - k, cosine - sine)]
            damp = 1.0 / (base + float(24.0 * eigen_x[k]))
            for kx, value in modes:
                value = value * damp
                for lx in range(5):
                    term = rows_x[lax.rem(own_x * 4 + lx, 32), kx] * value
                    totals[lx] = term if totals[lx] is None else totals[lx] + term
        for lx in range(5):
            part[lx, rows, :] = totals[lx]
        return carry

    lax.fori_loop(0, 8, x_step, 0)
    own_rows = back_y[own_y]
    solved = jnp.concatenate([exact_dot(own_rows, part[lx]) for lx in range(5)], axis=0)
    out[...] = exact_dot(solved, hartley_z[...]) * (1.0 / (32 * 64 * 128))


def coarse(gathered):
    vmem = pl.BlockSpec(memory_space=pltpu.VMEM)
    smem = pl.BlockSpec(memory_space=pltpu.SMEM)
    place = jnp.stack([lax.axis_index("px"), lax.axis_index("py")]).astype(jnp.int32)
    table_y = hartley(64)
    forward = np.zeros((64, 160), np.float32)
    back = np.zeros((16, 8, 64), np.float32)
    for q in range(16):
        for ly in range(5):
            forward[:, ly * 16 + q] = table_y[:, (4 * q + ly) % 64]
            back[q, ly] = table_y[(4 * q + ly) % 64]
    forward[:, 80:] = forward[:, :80]
    high, low = split_np(forward)
    low[:, 80:] = 0
    lines = 24.0 * (line_eigen(64)[:, None] + line_eigen(128)[None, :]) + 0.5
    return pl.pallas_call(
        coarse_kernel,
        out_shape=jax.ShapeDtypeStruct((40, LANES), F32),
        in_specs=[smem, smem] + [vmem] * 5,
        out_specs=vmem,
        scratch_shapes=[
            pltpu.VMEM((32, 64, LANES), F32),
            pltpu.VMEM((5, 64, LANES), F32),
        ],
        compiler_params=pltpu.CompilerParams(vmem_limit_bytes=VMEM_LIMIT),
        cost_estimate=pl.CostEstimate(
            flops=2 * 10**9, bytes_accessed=4 * 10**6, transcendentals=0
        ),
        name="coarse",
    )(
        place,
        jnp.asarray(hartley(32), F32),
        gathered,
        jnp.asarray(np.concatenate([high, low], axis=0)),
        jnp.asarray(back),
        jnp.asarray(hartley(128), F32),
        jnp.asarray(lines, F32),
    )


def average_faces(level, field, sides, x_low, x_high, y_low, y_high, diags):
    n, core = level.n, level.core
    base = 0 if n == 8 else 256
    edge = 0 if n == 8 else 8

    def at(ex, ey):
        return 2 * ex + ey // 2, ey % 2

    for ey in range(EY):
        row = base + ey * core
        q, h = at(0, ey)
        field[q, h, 0] = 0.5 * (field[q, h, 0] + x_low[row : row + core])
        q, h = at(EX - 1, ey)
        field[q, h, n - 1] = 0.5 * (field[q, h, n - 1] + x_high[row : row + core])
        for ex in range(EX - 1):
            q, h = at(ex, ey)
            total = 0.5 * (field[q, h, n - 1] + field[q + 2, h, 0])
            field[q, h, n - 1] = total
            field[q + 2, h, 0] = total
    for side, halo in ((0, y_low), (1, y_high)):
        sides[side] = halo[base : base + EX * core]
        low = diags[0][side][edge : edge + n]
        high = diags[1][side][edge : edge + n]
        end = EX * core
        sides[side, 0:n] = 0.5 * (sides[side, 0:n] + low)
        sides[side, end - n : end] = 0.5 * (sides[side, end - n : end] + high)
        for ex in range(EX - 1):
            row = ex * core + core
            total = 0.5 * (sides[side, row - n : row] + sides[side, row : row + n])
            sides[side, row - n : row] = total
            sides[side, row : row + n] = total
    for ex in range(EX):
        for a in range(n):
            row = (ex * n + a) * n
            q, h = at(ex, 0)
            field[q, h, a, 0:n] = 0.5 * (field[q, h, a, 0:n] + sides[0, row : row + n])
            q, h = at(ex, EY - 1)
            field[q, h, a, core - n : core] = 0.5 * (
                field[q, h, a, core - n : core] + sides[1, row : row + n]
            )
            for ey in range(EY - 1):
                q, h = at(ex, ey)
                p, g = at(ex, ey + 1)
                total = 0.5 * (field[q, h, a, core - n : core] + field[p, g, a, 0:n])
                field[q, h, a, core - n : core] = total
                field[p, g, a, 0:n] = total


def finish_kernel(
    fine, middle, coarse_part, prolong, x_low, x_high, y_low, y_high, d_ll, d_lh, d_hl, d_hh,
    out, field, sides, field_m, sides_m, corner, result, in_sems, out_sems,
):
    copies = []
    for q in range(8):
        copy = pltpu.make_async_copy(fine.at[q], field.at[q], in_sems.at[q])
        copy.start()
        copies.append(copy)
    diags = ((d_ll, d_lh), (d_hl, d_hh))
    field_m[...] = middle[...]
    average_faces(MID, field_m, sides_m, x_low, x_high, y_low, y_high, diags)
    near = coarse_part[...]
    far = pltpu.roll(near, LANES - 1, 1)
    for q in range(8):
        for h in (0, 1):
            ex, ey = q // 2, (q % 2) * 2 + h
            corner[q, h, 8:16] = jnp.zeros((8, LANES), F32)
            for i in (0, 1):
                for j in (0, 1):
                    row = (ex + i) * 8 + ey + j
                    place = i * 4 + j * 2
                    corner[q, h, place : place + 1] = near[row : row + 1]
                    corner[q, h, place + 1 : place + 2] = far[row : row + 1]
    for copy in copies:
        copy.wait()
    average_faces(FINE, field, sides, x_low, x_high, y_low, y_high, diags)

    def step(q, carry):
        for h in (0, 1):
            for a in range(4):
                sum_lines(field_m, (q, h, a), 4, 0.5)
            for a in range(8):
                sum_lines(field, (q, h, a), 8, 0.5)
        level = jnp.concatenate(
            [field_m[q, 0].reshape(64, LANES), field_m[q, 1].reshape(64, LANES)], axis=1
        )
        high, low = split(level)
        ends = jnp.concatenate([corner[q, 0], corner[q, 1]], axis=1)
        ends_high, ends_low = split(ends)
        stacked = jnp.concatenate([high, low, high, ends_high, ends_low, ends_high], axis=0)
        total = dot(prolong[...], stacked)
        for h in (0, 1):
            part = total[:, h * LANES : (h + 1) * LANES]
            result[q, h] = field[q, h] + part.reshape(8, 64, LANES)
        pltpu.make_async_copy(result.at[q], out.at[q], out_sems.at[q]).start()
        return carry

    lax.fori_loop(0, 8, step, 0)
    for q in range(8):
        pltpu.make_async_copy(result.at[q], out.at[q], out_sems.at[q]).wait()


def finish(fine, middle, coarse_part, halos):
    vmem = pl.BlockSpec(memory_space=pltpu.VMEM)
    hbm = pl.BlockSpec(memory_space=pl.ANY)
    return pl.pallas_call(
        finish_kernel,
        out_shape=jax.ShapeDtypeStruct((8, 2, 8, 64, LANES), F32),
        in_specs=[hbm] + [vmem] * 11,
        out_specs=hbm,
        scratch_shapes=[
            pltpu.VMEM((8, 2, 8, 64, LANES), F32),
            pltpu.VMEM((2, EX * 64, LANES), F32),
            pltpu.VMEM((8, 2, 4, 16, LANES), F32),
            pltpu.VMEM((2, EX * 16, LANES), F32),
            pltpu.VMEM((8, 2, 16, LANES), F32),
            pltpu.VMEM((8, 2, 8, 64, LANES), F32),
            pltpu.SemaphoreType.DMA((8,)),
            pltpu.SemaphoreType.DMA((8,)),
        ],
        compiler_params=pltpu.CompilerParams(vmem_limit_bytes=VMEM_LIMIT),
        cost_estimate=pl.CostEstimate(
            flops=2 * 10**9, bytes_accessed=8 * 10**6, transcendentals=0
        ),
        name="finish",
    )(fine, middle, coarse_part, jnp.asarray(prolong_matrix()), *halos)


def shift(values, axis, step):
    count = lax.axis_size(axis)
    return lax.ppermute(values, axis, [(i, (i + step) % count) for i in range(count)])


def shift_both(values, step_x, step_y):
    count_x, count_y = lax.axis_size("px"), lax.axis_size("py")
    pairs = [
        (i * count_y + j, (i + step_x) % count_x * count_y + (j + step_y) % count_y)
        for i in range(count_x)
        for j in range(count_y)
    ]
    return lax.ppermute(values, ("px", "py"), pairs)


def exchange(sends):
    x_up, x_down, y_up, y_down, d_uu, d_ud, d_du, d_dd = sends
    return (
        shift(x_up, "px", 1),
        shift(x_down, "px", -1),
        shift(y_up, "py", 1),
        shift(y_down, "py", -1),
        shift_both(d_uu, 1, 1),
        shift_both(d_ud, 1, -1),
        shift_both(d_du, -1, 1),
        shift_both(d_dd, -1, -1),
    )


def on_device(residual, scale, fine_basis, fine_eigen, middle_basis, middle_eigen):
    shape = residual.shape
    residual = residual.reshape(EX, EY, 8, 64, LANES)
    packed = pack(residual)
    sends, middle, vertex = packed[:8], packed[8], packed[9]
    halos = exchange(sends)
    devices = lax.axis_size("px") * lax.axis_size("py")
    copies = jnp.broadcast_to(vertex[None], (devices, 32, LANES))
    gathered = lax.all_to_all(copies, ("px", "py"), 0, 0).reshape(devices * 32, LANES)
    solved = schwarz(
        residual, middle, scale, fine_basis, fine_eigen, middle_basis, middle_eigen, halos
    )
    fine_solved, middle_solved, faces = solved[0], solved[1], solved[2:]
    faces = exchange(faces)
    coarse_part = coarse(gathered)
    return finish(fine_solved, middle_solved, coarse_part, faces).reshape(shape)


def solution(mesh):
    placed = (P("px", "py", None, None, None, None), P("px", "py", None), P(), P(), P(), P())
    return jax.shard_map(
        on_device,
        mesh=mesh,
        in_specs=placed,
        out_specs=P("px", "py", None, None, None, None),
        check_vma=False,
    )
```

time: 392 us -> 134 us (0.34); the launches traced: 385 us -> 134 us
  matrix products: 177 us -> 0 us
  local copies, waits for them, and re-layouts: 64 us -> 6.39 us
  Pallas kernels: 0 us -> 56.3 us
  other arithmetic: 34.7 us -> 0.65 us
  waiting for transfers between devices: 51.9 us -> 24.8 us
  between operations: 15.1 us -> 0.29 us
    dot_general x30 -> x0, matrix products: 177 us -> none  [the longest x2 26.7 us: local_solve(): jnp.einsum('ai,...ijkz->...ajkz', eigen_basis[0], spectrum, precision=HIG...]
    pallas_call x0 -> x4, Pallas kernels: none -> 56.3 us  [the longest x1 37.1 us: schwarz(): pl.pallas_call(schwarz_kernel, out_shape=[jax.ShapeDtypeStruct((8, 2, 8,...]
    slice x55 -> x0, local copies, waits for them, and re-layouts: 25.9 us -> none  [the longest x15 15.7 us: replace_ends(): middle = lax.slice_in_dim(values, 1, count - 1, axis=axis)]
    all_gather x1 -> x0, waiting for transfers between devices: 20.6 us -> none  [on_device(): gathered = lax.all_gather(vertex, ('px', 'py'), axis=0, tiled=True)]
    add x29 -> x0, other arithmetic: 16.3 us -> none  [the longest x10 6.34 us: sum_faces(): low_side + below_high]
    dot_general x2 -> x0, local copies, waits for them, and re-layouts: 15.1 us -> none  [local_solve(): jnp.einsum('ck,...abkz->...abcz', eigen_basis[2], result, precision=HIGHEST)]
    concatenate x18 -> x0, other arithmetic: 13.6 us -> none  [the longest x9 9.4 us: replace_ends(): jnp.concatenate([jnp.expand_dims(low_new, axis), middle, jnp.expand_dims(...]
    concatenate x24 -> x0, local copies, waits for them, and re-layouts: 12.6 us -> none  [the longest x1 5.07 us: assemble(): middle = jnp.concatenate([south_full, core, north_full], axis=3)]
  transfers between devices with their start and end apart: 24 -> 17, of which waited for: 12 -> 3; matrix products, arithmetic and copies ran while one was open for 17% -> 2% of each run, Pallas kernels for 0% -> 33%
where the time goes in v1:
time: 134 us
  Pallas kernels  56.3 us (42%)
  starting transfers between devices  45.7 us (34%)
  waiting for transfers between devices  24.8 us (19%)
  local copies, waits for them, and re-layouts  6.39 us (5%)
    pallas_call x1, Pallas kernels, schwarz(): pl.pallas_call(schwarz_kernel, out_shape=[jax.ShapeDtypeStruct((8, 2, 8,...  37.1 us
    ppermute x8, waiting for transfers between devices, shift_both(): return lax.ppermute(values, ('px', 'py'), pairs)  23.6 us
    ppermute x8, starting transfers between devices, shift_both(): return lax.ppermute(values, ('px', 'py'), pairs)  17.9 us
    ppermute x8, starting transfers between devices, shift(): lax.ppermute(values, axis, [(i, (i + step) % count) for i in range(count)])  16.6 us
    all_to_all x1, starting transfers between devices, on_device(): lax.all_to_all(copies, ('px', 'py'), 0, 0).reshape(devices * 32, LANES)  11.2 us
    pallas_call x1, Pallas kernels, finish(): pl.pallas_call(finish_kernel, out_shape=jax.ShapeDtypeStruct((8, 2, 8, 64...  7.34 us
    pallas_call x1, Pallas kernels, coarse(): pl.pallas_call(coarse_kernel, out_shape=jax.ShapeDtypeStruct((40, LANES),...  6.76 us
    pallas_call x1, Pallas kernels, pack(): pl.pallas_call(pack_kernel, out_shape=[halo] * 4 + [diag] * 4 + [jax.Shap...  5.15 us
  transfers between devices with their start and end apart: 17, of which 3 were waited for; matrix products, arithmetic and copies ran while one was open for 2% of the time, Pallas kernels for 33%

profile of v1, /device:TPU:0, one launch (start us, length us, event | category | flops | bytes accessed | tf_op | source)
XLA Modules:
  0.0 134.1 jit_solution(8682485175138731510)
XLA Ops:
  0.0 5.1 %pack.1 = (f32[640,128]{1,0:T(8,128)}, f32[640,128]{1,0:T(8,128)}, f32[640,128]{1,0:T(8,128)}, f32[640,128]{1,0:T(8,128)}, f32[40,128]{1,0:T(8,128)}, /*index=5*...) custom-call(f32[4,4,8,64,128]{4,3,2,1,0:T(8,128)} %bitcast.9, ...), custom_call_target="tpu_custom_call" | custom-call | flops 1000000000 | bytes 8000000 | tf_op jit(solution)/shard_map/pack/pallas_call | solution.py:231
  5.2 2.4 %broadcast_in_dim.2 = f32[128,32,128]{2,1,0:T(8,128)} broadcast(f32[32,128]{1,0:T(8,128)} %get-tuple-element.36), dimensions={1,2} | broadcast | bytes 2113536 | tf_op jit(solution)/shard_map/broadcast_in_dim | solution.py:830
  7.6 11.2 %all-to-all-start = ((f32[128,32,128]{2,1,0:T(8,128)}), f32[128,32,128]{2,1,0:T(8,128)S(1)}, u32[]{:S(2)}, u32[]{:S(2)}) async-start(f32[128,32,128]{2,1,0:T(8,128)} %broadcast_in_dim.2), calls=%async_computation | async-start | bytes 4194304 | tf_op jit(solution)/shard_map/all_to_all | solution.py:831
  18.8 0.8 collective-permute-start.4
  19.5 4.7 %collective-permute-start.5 = (f32[40,128]{1,0:T(8,128)}, f32[40,128]{1,0:T(8,128)S(1)}, u32[]{:S(2)}, u32[]{:S(2)}) collective-permute-start(f32[40,128]{1,0:T(8,128)} %get-tuple-element.31), channel_id=1, source_target_pairs={{0,31},{1,16},{2,17},{3,18},{4,19},{5,20},{6,21},{7,22},{8,23},{9,... | collective-permute-start | bytes 61448 | tf_op jit(solution)/shard_map/ppermute | solution.py:806
  24.3 0.8 collective-permute-start
  25.1 2.2 %collective-permute-start.1 = (f32[640,128]{1,0:T(8,128)}, f32[640,128]{1,0:T(8,128)S(1)}, u32[]{:S(2)}, u32[]{:S(2)}) collective-permute-start(f32[640,128]{1,0:T(8,128)} %get-tuple-element.27), channel_id=1, source_target_pairs={{0,112},{16,0},{32,16},{48,32},{64,48},{80,64},{96,80},{112,96},{1... | collective-permute-start | bytes 983048 | tf_op jit(solution)/shard_map/ppermute | solution.py:796
  27.3 21.6 %collective-permute-done.4.refs_4_ = f32[40,128]{1,0:T(8,128)S(1)} collective-permute-done((f32[40,128]{1,0:T(8,128)}, f32[40,128]{1,0:T(8,128)S(1)}, u32[]{:S(2)}, u32[]{:S(2)}) %collective-permute-start.4) | collective-permute-done | bytes 20512 | tf_op jit(solution)/shard_map/ppermute | solution.py:806
  48.9 5.4 %collective-permute-start.3 = (f32[640,128]{1,0:T(8,128)S(1)}, f32[640,128]{1,0:T(8,128)}, u32[]{:S(2)}, u32[]{:S(2)}) collective-permute-start(f32[640,128]{1,0:T(8,128)S(1)} %copy-done.13), channel_id=1, source_target_pairs={{0,15},{1,0},{2,1},{3,2},{4,3},{5,4},{6,5},{7,6},{8,7},{9,8},{10,9... | collective-permute-start | bytes 983048 | tf_op jit(solution)/shard_map/ppermute | solution.py:796
  54.3 0.6 slice_bitcast_fusion.fine_coeff
  55.0 1.3 slice_bitcast_fusion.1.middle_coeff
  56.3 1.9 %collective-permute-done.7.refs_7_ = f32[40,128]{1,0:T(8,128)S(1)} collective-permute-done((f32[40,128]{1,0:T(8,128)S(1)}, f32[40,128]{1,0:T(8,128)S(1)}, u32[]{:S(2)}, u32[]{:S(2)}) %collective-permute-start.7) | collective-permute-done | bytes 20512 | tf_op jit(solution)/shard_map/ppermute | solution.py:806
  58.2 1.2 collective-permute-done.2.refs_2_
  59.5 37.1 %schwarz.1 = (f32[8,2,8,64,128]{4,3,2,1,0:T(8,128)}, f32[8,2,4,16,128]{4,3,2,1,0:T(8,128)}, f32[320,128]{1,0:T(8,128)}, f32[320,128]{1,0:T(8,128)}, f32[320,128]...) custom-call(f32[4,4,8,64,128]{4,3,2,1,0:T(8,128)} %bitcast.10, ...), custom_call_target="tpu_custom_call" | custom-call | flops 8000000000 | bytes 12000000 | tf_op jit(solution)/shard_map/schwarz/pallas_call | solution.py:540
  96.6 5.7 %collective-permute-start.13 = (f32[16,128]{1,0:T(8,128)}, f32[16,128]{1,0:T(8,128)S(1)}, u32[]{:S(2)}, u32[]{:S(2)}) collective-permute-start(f32[16,128]{1,0:T(8,128)} %get-tuple-element.42), channel_id=1, source_target_pairs={{0,31},{1,16},{2,17},{3,18},{4,19},{5,20},{6,21},{7,22},{8,23},{9,... | collective-permute-start | bytes 24584 | tf_op jit(solution)/shard_map/ppermute | solution.py:806
  102.3 0.6 pad_add_fusion.place
  103.0 6.5 %collective-permute-start.15 = (f32[16,128]{1,0:T(8,128)}, f32[16,128]{1,0:T(8,128)S(1)}, u32[]{:S(2)}, u32[]{:S(2)}) collective-permute-start(f32[16,128]{1,0:T(8,128)} %get-tuple-element.44), channel_id=1, source_target_pairs={{0,127},{1,112},{2,113},{3,114},{4,115},{5,116},{6,117},{7,118},{8... | collective-permute-start | bytes 24584 | tf_op jit(solution)/shard_map/ppermute | solution.py:806
  109.5 0.8 collective-permute-start.8
  110.3 2.2 %collective-permute-start.9 = (f32[320,128]{1,0:T(8,128)}, f32[320,128]{1,0:T(8,128)S(1)}, u32[]{:S(2)}, u32[]{:S(2)}) collective-permute-start(f32[320,128]{1,0:T(8,128)} %get-tuple-element.38), channel_id=1, source_target_pairs={{0,112},{16,0},{32,16},{48,32},{64,48},{80,64},{96,80},{112,96},{1... | collective-permute-start | bytes 491528 | tf_op jit(solution)/shard_map/ppermute | solution.py:796
  112.5 5.3 %collective-permute-start.11 = (f32[320,128]{1,0:T(8,128)}, f32[320,128]{1,0:T(8,128)S(1)}, u32[]{:S(2)}, u32[]{:S(2)}) collective-permute-start(f32[320,128]{1,0:T(8,128)} %get-tuple-element.40), channel_id=1, source_target_pairs={{0,15},{1,0},{2,1},{3,2},{4,3},{5,4},{6,5},{7,6},{8,7},{9,8},{10,9... | collective-permute-start | bytes 491528 | tf_op jit(solution)/shard_map/ppermute | solution.py:796
  117.8 1.3 copy-done
  119.1 6.8 %coarse.1.coarse_part = f32[40,128]{1,0:T(8,128)} custom-call(s32[2]{0:T(128)} %pad_add_fusion.place, f32[32,32]{1,0:T(8,128)} %constant.64.clone.rows_x, f32[4096,128]{1,0:T(8,128)} %bitcast.11, bf16[128,160]{1,0:T(8,128)(2,1)} %constant.65.clone.forward_y, f32[16,8,64]{2,1,0:T(8,128)} %constant.66.clone.back_y, f32[128,128]{1,0:T(8,128)} %constant.51.clone.hartley_z, ...), custom_call_target="tpu_custom_call" | custom-call | flops 2000000000 | bytes 4000000 | tf_op jit(solution)/shard_map/coarse/pallas_call | solution.py:642
  126.0 0.5 copy-done.10
  126.8 7.3 %finish.1 = f32[8,2,8,64,128]{4,3,2,1,0:T(8,128)} custom-call(f32[8,2,8,64,128]{4,3,2,1,0:T(8,128)} %get-tuple-element.34.fine, f32[8,2,4,16,128]{4,3,2,1,0:T(8,128)} %get-tuple-element.35.middle, f32[40,128]{1,0:T(8,128)} %coarse.1.coarse_part, bf16[512,240]{1,0:T(8,128)(2,1)} %constant.68.clone.prolong, f32[320,128]{1,0:T(8,128)} %copy-done.1, ...), custom_call_target="tpu_custom_call" | custom-call | flops 2000000000 | bytes 8000000 | tf_op jit(solution)/shard_map/finish/pallas_call | solution.py:771
  (61 shorter events, 0.6 us)
Async XLA Ops:
  5.2 19.1 %copy-start.20 = (f32[40,128]{1,0:T(8,128)S(1)}, f32[40,128]{1,0:T(8,128)}, u32[]{:S(2)}) copy-start(f32[40,128]{1,0:T(8,128)} %get-tuple-element.32) | copy-start | bytes 61444
  5.2 22.1 %copy-start.6 = (f32[3,10,10]{2,0,1:T(4,128)S(1)}, f32[3,10,10]{2,0,1:T(4,128)}, u32[]{:S(2)}) copy-start(f32[3,10,10]{2,0,1:T(4,128)} %param.29) | copy-start | bytes 3604
  5.2 43.7 %copy-start.14 = (f32[640,128]{1,0:T(8,128)S(1)}, f32[640,128]{1,0:T(8,128)}, u32[]{:S(2)}) copy-start(f32[640,128]{1,0:T(8,128)} %get-tuple-element.28) | copy-start | bytes 983044
  5.2 43.7 %copy-start.13 = (f32[640,128]{1,0:T(8,128)S(1)}, f32[640,128]{1,0:T(8,128)}, u32[]{:S(2)}) copy-start(f32[640,128]{1,0:T(8,128)} %get-tuple-element.29) | copy-start | bytes 983044
  5.2 49.7 %copy-start.18 = (f32[40,128]{1,0:T(8,128)S(1)}, f32[40,128]{1,0:T(8,128)}, u32[]{:S(2)}) copy-start(f32[40,128]{1,0:T(8,128)} %get-tuple-element.33) | copy-start | bytes 61444
  7.6 110.2 %all-to-all-start = ((f32[128,32,128]{2,1,0:T(8,128)}), f32[128,32,128]{2,1,0:T(8,128)S(1)}, u32[]{:S(2)}, u32[]{:S(2)}) async-start(f32[128,32,128]{2,1,0:T(8,128)} %broadcast_in_dim.2), calls=%async_computation | async-start | bytes 4194304 | tf_op jit(solution)/shard_map/all_to_all | solution.py:831
  18.8 30.1 %collective-permute-start.4 = (f32[40,128]{1,0:T(8,128)}, f32[40,128]{1,0:T(8,128)S(1)}, u32[]{:S(2)}, u32[]{:S(2)}) collective-permute-start(f32[40,128]{1,0:T(8,128)} %get-tuple-element.30), channel_id=1, source_target_pairs={{0,17},{1,18},{2,19},{3,20},{4,21},{5,22},{6,23},{7,24},{8,25},{9,... | collective-permute-start | bytes 61448 | tf_op jit(solution)/shard_map/ppermute | solution.py:806
  19.5 29.4 %collective-permute-start.5 = (f32[40,128]{1,0:T(8,128)}, f32[40,128]{1,0:T(8,128)S(1)}, u32[]{:S(2)}, u32[]{:S(2)}) collective-permute-start(f32[40,128]{1,0:T(8,128)} %get-tuple-element.31), channel_id=1, source_target_pairs={{0,31},{1,16},{2,17},{3,18},{4,19},{5,20},{6,21},{7,22},{8,23},{9,... | collective-permute-start | bytes 61448 | tf_op jit(solution)/shard_map/ppermute | solution.py:806
  24.3 30.6 %collective-permute-start.6 = (f32[40,128]{1,0:T(8,128)S(1)}, f32[40,128]{1,0:T(8,128)S(1)}, u32[]{:S(2)}, u32[]{:S(2)}) collective-permute-start(f32[40,128]{1,0:T(8,128)S(1)} %copy-done.20), channel_id=1, source_target_pairs={{0,113},{1,114},{2,115},{3,116},{4,117},{5,118},{6,119},{7,120},{8... | collective-permute-start | bytes 61448 | tf_op jit(solution)/shard_map/ppermute | solution.py:806
  24.3 33.9 %collective-permute-start = (f32[640,128]{1,0:T(8,128)}, f32[640,128]{1,0:T(8,128)S(1)}, u32[]{:S(2)}, u32[]{:S(2)}) collective-permute-start(f32[640,128]{1,0:T(8,128)} %get-tuple-element.26), channel_id=1, source_target_pairs={{0,16},{16,32},{32,48},{48,64},{64,80},{80,96},{96,112},{112,0},{1... | collective-permute-start | bytes 983048 | tf_op jit(solution)/shard_map/ppermute | solution.py:796
  25.1 33.1 %collective-permute-start.1 = (f32[640,128]{1,0:T(8,128)}, f32[640,128]{1,0:T(8,128)S(1)}, u32[]{:S(2)}, u32[]{:S(2)}) collective-permute-start(f32[640,128]{1,0:T(8,128)} %get-tuple-element.27), channel_id=1, source_target_pairs={{0,112},{16,0},{32,16},{48,32},{64,48},{80,64},{96,80},{112,96},{1... | collective-permute-start | bytes 983048 | tf_op jit(solution)/shard_map/ppermute | solution.py:796
  27.3 32.1 %copy-start.5 = (f32[3,10,10]{2,1,0:T(8,128)}, f32[3,10,10]{2,1,0:T(8,128)S(1)}, u32[]{:S(2)}) copy-start(f32[3,10,10]{2,1,0:T(8,128)S(1)} %copy.29.fine_basis) | copy-start | bytes 3604
  48.9 10.5 %collective-permute-start.2 = (f32[640,128]{1,0:T(8,128)S(1)}, f32[640,128]{1,0:T(8,128)}, u32[]{:S(2)}, u32[]{:S(2)}) collective-permute-start(f32[640,128]{1,0:T(8,128)S(1)} %copy-done.14), channel_id=1, source_target_pairs={{0,1},{1,2},{2,3},{3,4},{4,5},{5,6},{6,7},{7,8},{8,9},{9,10},{10,1... | collective-permute-start | bytes 983048 | tf_op jit(solution)/shard_map/ppermute | solution.py:796
  48.9 10.5 %collective-permute-start.3 = (f32[640,128]{1,0:T(8,128)S(1)}, f32[640,128]{1,0:T(8,128)}, u32[]{:S(2)}, u32[]{:S(2)}) collective-permute-start(f32[640,128]{1,0:T(8,128)S(1)} %copy-done.13), channel_id=1, source_target_pairs={{0,15},{1,0},{2,1},{3,2},{4,3},{5,4},{6,5},{7,6},{8,7},{9,8},{10,9... | collective-permute-start | bytes 983048 | tf_op jit(solution)/shard_map/ppermute | solution.py:796
  54.9 3.3 %collective-permute-start.7 = (f32[40,128]{1,0:T(8,128)S(1)}, f32[40,128]{1,0:T(8,128)S(1)}, u32[]{:S(2)}, u32[]{:S(2)}) collective-permute-start(f32[40,128]{1,0:T(8,128)S(1)} %copy-done.18), channel_id=1, source_target_pairs={{0,127},{1,112},{2,113},{3,114},{4,115},{5,116},{6,117},{7,118},{8... | collective-permute-start | bytes 61448 | tf_op jit(solution)/shard_map/ppermute | solution.py:806
  96.5 13.7 %collective-permute-start.12 = (f32[16,128]{1,0:T(8,128)}, f32[16,128]{1,0:T(8,128)S(1)}, u32[]{:S(2)}, u32[]{:S(2)}) collective-permute-start(f32[16,128]{1,0:T(8,128)} %get-tuple-element.41), channel_id=1, source_target_pairs={{0,17},{1,18},{2,19},{3,20},{4,21},{5,22},{6,23},{7,24},{8,25},{9,... | collective-permute-start | bytes 24584 | tf_op jit(solution)/shard_map/ppermute | solution.py:806
  96.6 15.8 %collective-permute-start.13 = (f32[16,128]{1,0:T(8,128)}, f32[16,128]{1,0:T(8,128)S(1)}, u32[]{:S(2)}, u32[]{:S(2)}) collective-permute-start(f32[16,128]{1,0:T(8,128)} %get-tuple-element.42), channel_id=1, source_target_pairs={{0,31},{1,16},{2,17},{3,18},{4,19},{5,20},{6,21},{7,22},{8,23},{9,... | collective-permute-start | bytes 24584 | tf_op jit(solution)/shard_map/ppermute | solution.py:806
  102.3 10.2 %collective-permute-start.14 = (f32[16,128]{1,0:T(8,128)}, f32[16,128]{1,0:T(8,128)S(1)}, u32[]{:S(2)}, u32[]{:S(2)}) collective-permute-start(f32[16,128]{1,0:T(8,128)} %get-tuple-element.43), channel_id=1, source_target_pairs={{0,113},{1,114},{2,115},{3,116},{4,117},{5,118},{6,119},{7,120},{8... | collective-permute-start | bytes 24584 | tf_op jit(solution)/shard_map/ppermute | solution.py:806
  103.0 22.9 %collective-permute-start.15 = (f32[16,128]{1,0:T(8,128)}, f32[16,128]{1,0:T(8,128)S(1)}, u32[]{:S(2)}, u32[]{:S(2)}) collective-permute-start(f32[16,128]{1,0:T(8,128)} %get-tuple-element.44), channel_id=1, source_target_pairs={{0,127},{1,112},{2,113},{3,114},{4,115},{5,116},{6,117},{7,118},{8... | collective-permute-start | bytes 24584 | tf_op jit(solution)/shard_map/ppermute | solution.py:806
  109.5 16.4 %collective-permute-start.8 = (f32[320,128]{1,0:T(8,128)}, f32[320,128]{1,0:T(8,128)S(1)}, u32[]{:S(2)}, u32[]{:S(2)}) collective-permute-start(f32[320,128]{1,0:T(8,128)} %get-tuple-element.37), channel_id=1, source_target_pairs={{0,16},{16,32},{32,48},{48,64},{64,80},{80,96},{96,112},{112,0},{1... | collective-permute-start | bytes 491528 | tf_op jit(solution)/shard_map/ppermute | solution.py:796
  110.3 15.7 %copy-start.7 = (f32[16,128]{1,0:T(8,128)}, f32[16,128]{1,0:T(8,128)S(1)}, u32[]{:S(2)}) copy-start(f32[16,128]{1,0:T(8,128)S(1)} %collective-permute-done.12.d_ll) | copy-start | bytes 24580
  110.3 15.7 %collective-permute-start.9 = (f32[320,128]{1,0:T(8,128)}, f32[320,128]{1,0:T(8,128)S(1)}, u32[]{:S(2)}, u32[]{:S(2)}) collective-permute-start(f32[320,128]{1,0:T(8,128)} %get-tuple-element.38), channel_id=1, source_target_pairs={{0,112},{16,0},{32,16},{48,32},{64,48},{80,64},{96,80},{112,96},{1... | collective-permute-start | bytes 491528 | tf_op jit(solution)/shard_map/ppermute | solution.py:796
  112.5 13.5 %collective-permute-start.10 = (f32[320,128]{1,0:T(8,128)}, f32[320,128]{1,0:T(8,128)S(1)}, u32[]{:S(2)}, u32[]{:S(2)}) collective-permute-start(f32[320,128]{1,0:T(8,128)} %get-tuple-element.39), channel_id=1, source_target_pairs={{0,1},{1,2},{2,3},{3,4},{4,5},{5,6},{6,7},{7,8},{8,9},{9,10},{10,1... | collective-permute-start | bytes 491528 | tf_op jit(solution)/shard_map/ppermute | solution.py:796
  112.5 13.5 %collective-permute-start.11 = (f32[320,128]{1,0:T(8,128)}, f32[320,128]{1,0:T(8,128)S(1)}, u32[]{:S(2)}, u32[]{:S(2)}) collective-permute-start(f32[320,128]{1,0:T(8,128)} %get-tuple-element.40), channel_id=1, source_target_pairs={{0,15},{1,0},{2,1},{3,2},{4,3},{5,4},{6,5},{7,6},{8,7},{9,8},{10,9... | collective-permute-start | bytes 491528 | tf_op jit(solution)/shard_map/ppermute | solution.py:796
  (14 other events, 61.2 us)

commit v2 on v1

--- a/solution.py
+++ b/solution.py
@@ -14,7 +14,10 @@
 HIGHEST = lax.Precision.HIGHEST
 LANES = 128
 EX = EY = 4
-VMEM_LIMIT = 56 * 1024 * 1024
+MID_GROUP = 4
+LAG = 5
+MIB = 1024 * 1024
+VMEM_LIMIT = 60 * MIB
 
 
 def lobatto(count):
@@ -144,38 +147,45 @@
 
 FINE, MID = Level(8), Level(4)
 
-HALO_ROWS = 640
-DIAG_ROWS = 40
+LAYER_ROWS = 640
+X_ROWS = 648
+Y_ROWS = 664
 FACE_ROWS = 320
-EDGE_ROWS = 16
+VERTEX_ROWS = 24
+
+
+def plane_line(n, side):
+    return (640 if n == 8 else 656) + side * n
 
 
 def pack_kernel(
     residual,
-    restrict,
-    vertex_pick,
-    hartley_z,
+    restrict_in,
+    vertex_pick_in,
+    hartley_in,
     x_up,
     x_down,
     y_up,
     y_down,
-    d_uu,
-    d_ud,
-    d_du,
-    d_dd,
     middle,
     vertex,
     field,
     corners,
+    restrict,
+    vertex_pick,
+    hartley_z,
     sems,
 ):
+    moves = [(restrict_in, restrict)]
+    moves += [(residual.at[ex], field.at[ex]) for ex in range(EX)]
+    moves += [(vertex_pick_in, vertex_pick), (hartley_in, hartley_z)]
     copies = []
+    for place, (source, target) in enumerate(moves):
+        copies.append(pltpu.make_async_copy(source, target, sems.at[place]))
+        copies[-1].start()
+    copies[0].wait()
     for ex in range(EX):
-        copy = pltpu.make_async_copy(residual.at[ex], field.at[ex], sems.at[ex])
-        copy.start()
-        copies.append(copy)
-    for ex in range(EX):
-        copies[ex].wait()
+        copies[1 + ex].wait()
         for pair in range(EY // 2):
             ey = 2 * pair
             values = jnp.concatenate(
@@ -209,39 +219,46 @@
                     row = 512 + (layer * EX + ex) * 16 + a * 4
                     line = mids[layer] * 4
                     out[row : row + 4] = middle[ex, ey, a, line : line + 4]
-    for out, up_x, up_y in ((d_uu, 1, 1), (d_ud, 1, 0), (d_du, 0, 1), (d_dd, 0, 0)):
-        ex, ey = (EX - 1) * up_x, (EY - 1) * up_y
-        out[32:40] = jnp.zeros((8, LANES), F32)
-        for n, source, base in ((8, field, 0), (4, middle, 24)):
-            face_a, inner_a = (n - 1, n - 2) if up_x else (0, 1)
-            face_b, inner_b = (n - 1, n - 2) if up_y else (0, 1)
-            for line, (a, b) in enumerate(((face_a, face_b), (face_a, inner_b), (inner_a, face_b))):
-                out[base + line * n : base + line * n + n] = source[ex, ey, a, b * n : b * n + n]
+    for out in (y_up, y_down):
+        for n, base in ((8, 0), (4, 512)):
+            core = n * n
+            for row in [base + k * core for k in (1, 2, 3, 5, 6, 7)]:
+                total = out[row - n : row] + out[row : row + n]
+                out[row - n : row] = total
+                out[row : row + n] = total
+    copies[EX + 1].wait()
+    copies[EX + 2].wait()
     values = corners[...]
     low = exact_dot(vertex_pick[0], values)
     high = exact_dot(vertex_pick[1], values)
     total = low + pltpu.roll(high, 1, 1)
-    vertex[...] = exact_dot(total, hartley_z[...])
+    total = exact_dot(total, hartley_z[...])
+    vertex[...] = total
+    x_up[LAYER_ROWS:X_ROWS] = total[20:28]
+    x_down[LAYER_ROWS:X_ROWS] = jnp.zeros((8, LANES), F32)
 
 
 def pack(residual):
-    halo = jax.ShapeDtypeStruct((HALO_ROWS, LANES), F32)
-    diag = jax.ShapeDtypeStruct((DIAG_ROWS, LANES), F32)
+    x_halo = jax.ShapeDtypeStruct((X_ROWS, LANES), F32)
+    y_halo = jax.ShapeDtypeStruct((LAYER_ROWS, LANES), F32)
     vmem = pl.BlockSpec(memory_space=pltpu.VMEM)
     return pl.pallas_call(
         pack_kernel,
-        out_shape=[halo] * 4
-        + [diag] * 4
+        out_shape=[x_halo] * 2
+        + [y_halo] * 2
         + [
             jax.ShapeDtypeStruct((EX, EY, 4, 16, LANES), F32),
             jax.ShapeDtypeStruct((32, LANES), F32),
         ],
-        in_specs=[pl.BlockSpec(memory_space=pl.ANY)] + [vmem] * 3,
-        out_specs=[vmem] * 10,
+        in_specs=[pl.BlockSpec(memory_space=pltpu.HBM)] * 4,
+        out_specs=[vmem] * 6,
         scratch_shapes=[
             pltpu.VMEM((EX, EY, 8, 64, LANES), F32),
             pltpu.VMEM((128, LANES), F32),
-            pltpu.SemaphoreType.DMA((EX,)),
+            pltpu.VMEM((160, 512), BF16),
+            pltpu.VMEM((2, 32, 128), F32),
+            pltpu.VMEM((128, 128), F32),
+            pltpu.SemaphoreType.DMA((EX + 3,)),
         ],
         compiler_params=pltpu.CompilerParams(vmem_limit_bytes=VMEM_LIMIT),
         cost_estimate=pl.CostEstimate(flops=10**9, bytes_accessed=8 * 10**6, transcendentals=0),
@@ -252,6 +269,89 @@
         jnp.asarray(vertex_matrices()),
         jnp.asarray(hartley(128), F32),
     )
+
+
+def join_kernel(x_low, x_high, y_up, y_down, vertex, after, up, down, summed):
+    del after
+    for out, source, ey, ends in ((up, y_up, EY - 1, True), (down, y_down, 0, False)):
+        out[0:LAYER_ROWS] = source[...]
+        for n, base in ((8, 0), (4, 512)):
+            core = n * n
+            nodes = (n - 1, n - 2) if ends else (0, 1)
+            for layer in (0, 1):
+                line = base + ey * core + nodes[layer] * n
+                row = base + layer * EX * core
+                out[row : row + n] += x_low[line : line + n]
+                row += EX * core - n
+                out[row : row + n] += x_high[line : line + n]
+            line = base + (EY + ey) * core + nodes[0] * n
+            for side, halo in ((0, x_low), (1, x_high)):
+                row = plane_line(n, side)
+                out[row : row + n] = halo[line : line + n]
+    summed[...] = vertex[0:VERTEX_ROWS]
+    summed[0:5] += x_low[LAYER_ROWS : LAYER_ROWS + 5]
+    summed[20:24] = jnp.zeros((4, LANES), F32)
+
+
+def join(x_low, x_high, y_up, y_down, vertex, after):
+    vmem = pl.BlockSpec(memory_space=pltpu.VMEM)
+    halo = jax.ShapeDtypeStruct((Y_ROWS, LANES), F32)
+    return pl.pallas_call(
+        join_kernel,
+        out_shape=[halo, halo, jax.ShapeDtypeStruct((VERTEX_ROWS, LANES), F32)],
+        in_specs=[vmem] * 5 + [pl.BlockSpec(memory_space=pl.ANY)],
+        out_specs=[vmem] * 3,
+        compiler_params=pltpu.CompilerParams(vmem_limit_bytes=VMEM_LIMIT),
+        cost_estimate=pl.CostEstimate(flops=10**6, bytes_accessed=3 * 10**6, transcendentals=0),
+        name="join",
+    )(x_low, x_high, y_up, y_down, vertex, after)
+
+
+def join_faces_kernel(x_low, x_high, y_up, y_down, up, down):
+    for out, source, ey, ends in ((up, y_up, EY - 1, True), (down, y_down, 0, False)):
+        out[...] = source[...]
+        for n, base in ((8, 0), (4, 256)):
+            core = n * n
+            line = base + ey * core + (core - n if ends else 0)
+            out[base : base + n] = 0.5 * (source[base : base + n] + x_low[line : line + n])
+            row = base + EX * core - n
+            out[row : row + n] = 0.5 * (source[row : row + n] + x_high[line : line + n])
+            for ex in range(EX - 1):
+                row = base + ex * core + core
+                total = 0.5 * (source[row - n : row] + source[row : row + n])
+                out[row - n : row] = total
+                out[row : row + n] = total
+
+
+def join_faces(x_low, x_high, y_up, y_down):
+    vmem = pl.BlockSpec(memory_space=pltpu.VMEM)
+    face = jax.ShapeDtypeStruct((FACE_ROWS, LANES), F32)
+    return pl.pallas_call(
+        join_faces_kernel,
+        out_shape=[face, face],
+        in_specs=[vmem] * 4,
+        out_specs=[vmem] * 2,
+        compiler_params=pltpu.CompilerParams(vmem_limit_bytes=VMEM_LIMIT),
+        cost_estimate=pl.CostEstimate(flops=10**6, bytes_accessed=10**6, transcendentals=0),
+        name="join_faces",
+    )(x_low, x_high, y_up, y_down)
+
+
+def spread_kernel(source, out):
+    out[...] = jnp.broadcast_to(source[...][None], out.shape)
+
+
+def spread(values, count):
+    vmem = pl.BlockSpec(memory_space=pltpu.VMEM)
+    return pl.pallas_call(
+        spread_kernel,
+        out_shape=jax.ShapeDtypeStruct((count,) + values.shape, F32),
+        in_specs=[vmem],
+        out_specs=vmem,
+        compiler_params=pltpu.CompilerParams(vmem_limit_bytes=VMEM_LIMIT),
+        cost_estimate=pl.CostEstimate(flops=10**6, bytes_accessed=2 * 10**6, transcendentals=0),
+        name="spread",
+    )(values)
 
 
 def sum_lines(ref, lead, n, scale=None):
@@ -267,19 +367,7 @@
     ref[high_rows] = new_high
 
 
-def halo_lines(level, halo, layer, plane):
-    n = level.n
-    start = layer * EX * n * n + plane * n + (0 if n == 8 else 512)
-    return halo[start : start + n]
-
-
-def diag_line(level, diag, line):
-    n = level.n
-    start = line * n + (0 if n == 8 else 24)
-    return diag[start : start + n]
-
-
-def assemble(level, planes, rims, sides, x_low, x_high, y_low, y_high, diags):
+def assemble(level, planes, rims, sides, x_low, x_high, y_low, y_high):
     n, core = level.n, level.core
     last = EX * n + 3
     base = 0 if n == 8 else 512
@@ -300,20 +388,14 @@
             kind = 2 * side + layer
             start = base + layer * EX * core
             sides[kind] = halo[start : start + EX * core]
-            sides[kind, 0:n] += diag_line(level, diags[0][side], layer)
-            sides[kind, EX * core - n : EX * core] += diag_line(level, diags[1][side], layer)
-            for ex in range(EX - 1):
-                row = ex * core + core
-                total = sides[kind, row - n : row] + sides[kind, row : row + n]
-                sides[kind, row - n : row] = total
-                sides[kind, row : row + n] = total
     for plane in range(EX * n):
         row = plane * n
         planes[0, 2 + plane, 0:n] += sides[0, row : row + n]
         planes[EY - 1, 2 + plane, core - n : core] += sides[2, row : row + n]
-    for plane, diag in ((0, diags[0]), (last, diags[1])):
-        planes[0, plane, 0:n] += diag_line(level, diag[0], 2)
-        planes[EY - 1, plane, core - n : core] += diag_line(level, diag[1], 2)
+    for side, plane in ((0, 0), (1, last)):
+        row = plane_line(n, side)
+        planes[0, plane, 0:n] += y_low[row : row + n]
+        planes[EY - 1, plane, core - n : core] += y_high[row : row + n]
     for ey in range(EY - 1):
         for plane in [0, last] + list(range(2, 2 + EX * n)):
             total = planes[ey, plane, core - n : core] + planes[ey + 1, plane, 0:n]
@@ -366,14 +448,13 @@
         inverse[i] = 1.0 / (lines + eigen[0:1, i : i + 1])
 
 
-def solve_pair(level, q, planes, rims, coeff, forward, backward, inverse, scale, spectrum, hats, out):
+def solve_pairs(
+    level, start, group, planes, rims, coeff, forward, backward, inverse, scale, spectrum, hats, out
+):
     n, wide, core, modes, depth = level.n, level.wide, level.core, level.modes, level.depth
-    ex = q // 2
-    ey = (q % 2) * 2
-    base = ex * n
     offsets = [0] + [2 + a for a in range(n)] + [n + 3]
 
-    def contract(load, nodes, row):
+    def contract(slot, load, nodes, row):
         held = [[load(h, e) for h in (0, 1)] for e in nodes]
         for i in range(wide):
             for h in (0, 1):
@@ -382,80 +463,123 @@
                     total += coeff[nodes[position], i] * held[position][h]
                 high, low = split(total)
                 lanes = slice(h * LANES, (h + 1) * LANES)
-                spectrum[i, row : row + 16, lanes] = high
-                spectrum[i, depth + row : depth + row + 16, lanes] = low
-
-    for row in range(0, core, 16):
-        contract(
-            lambda h, e, row=row: planes[ey + h, base + offsets[e], row : row + 16],
-            list(range(wide)),
-            row,
-        )
-    for row in range(0, level.rim, 16):
-        contract(
-            lambda h, e, row=row: rims[ey + h, base + e - 1, row : row + 16],
-            list(range(1, n + 1)),
-            core + row,
-        )
-    for i in range(wide):
-        both = dot(forward[...], spectrum[i])
-        damp = inverse[i]
-        hat = (both[0:modes] + both[modes : 2 * modes]) * jnp.concatenate([damp, damp], axis=1)
-        high, low = split(hat)
-        both = dot(backward[...], jnp.concatenate([high, low], axis=0))
-        hats[i] = both[0:core] + both[core : 2 * core]
-    for h in (0, 1):
-        inv = 1.0 / scale[ex, pl.ds(ey + h, 1), :]
-        lanes = slice(h * LANES, (h + 1) * LANES)
+                spectrum[slot, i, row : row + 16, lanes] = high
+                spectrum[slot, i, depth + row : depth + row + 16, lanes] = low
+
+    for slot in range(group):
+        q = start + slot
+        base, ey = q // 2 * n, q % 2 * 2
         for row in range(0, core, 16):
-            held = [hats[i, row : row + 16, lanes] for i in range(wide)]
-            for a in range(n):
-                total = coeff[a + 1, 0] * held[0]
-                for i in range(1, wide):
-                    total += coeff[a + 1, i] * held[i]
-                out[q, h, a, row : row + 16] = total * inv
+            contract(
+                slot,
+                lambda h, e, row=row: planes[ey + h, base + offsets[e], row : row + 16],
+                list(range(wide)),
+                row,
+            )
+        for row in range(0, level.rim, 16):
+            contract(
+                slot,
+                lambda h, e, row=row: rims[ey + h, base + e - 1, row : row + 16],
+                list(range(1, n + 1)),
+                core + row,
+            )
+    waiting = []
+    steps = [(slot, i) for slot in range(group) for i in range(wide)]
+    for step in range(len(steps) + LAG):
+        if step < len(steps):
+            slot, i = steps[step]
+            both = dot(forward[...], spectrum[slot, i])
+            damp = inverse[i]
+            hat = (both[0:modes] + both[modes : 2 * modes]) * jnp.concatenate([damp, damp], axis=1)
+            waiting.append(jnp.concatenate(split(hat), axis=0))
+        if step >= LAG:
+            slot, i = steps[step - LAG]
+            both = dot(backward[...], waiting[step - LAG])
+            hats[slot, i] = both[0:core] + both[core : 2 * core]
+    for slot in range(group):
+        q = start + slot
+        ex, ey = q // 2, q % 2 * 2
+        for h in (0, 1):
+            inv = 1.0 / scale[ex, pl.ds(ey + h, 1), :]
+            lanes = slice(h * LANES, (h + 1) * LANES)
+            for row in range(0, core, 16):
+                held = [hats[slot, i, row : row + 16, lanes] for i in range(wide)]
+                for a in range(n):
+                    total = coeff[a + 1, 0] * held[0]
+                    for i in range(1, wide):
+                        total += coeff[a + 1, i] * held[i]
+                    out[q, h, a, row : row + 16] = total * inv
+
+
+def tables_kernel(fine_basis, fine_eigen, middle_basis, middle_eigen, after, *refs):
+    del after
+    fine_in, middle_in, outs = refs[:6], refs[6:12], refs[12:]
+    build_tables(FINE, fine_in, fine_basis, fine_eigen, *outs[:3])
+    build_tables(MID, middle_in, middle_basis, middle_eigen, *outs[3:6])
+    outs[6][...] = fine_basis[0]
+    outs[7][...] = middle_basis[0]
+
+
+def solve_tables(fine_basis, fine_eigen, middle_basis, middle_eigen, after):
+    vmem = pl.BlockSpec(memory_space=pltpu.VMEM)
+    shapes = []
+    for level in (FINE, MID):
+        shapes += [
+            jax.ShapeDtypeStruct((2 * level.modes, 2 * level.depth), BF16),
+            jax.ShapeDtypeStruct((2 * level.core, 2 * level.modes), BF16),
+            jax.ShapeDtypeStruct((level.wide, level.modes, LANES), F32),
+        ]
+    shapes += [jax.ShapeDtypeStruct((level.wide, level.wide), F32) for level in (FINE, MID)]
+    return pl.pallas_call(
+        tables_kernel,
+        out_shape=shapes,
+        in_specs=[vmem] * 4 + [pl.BlockSpec(memory_space=pl.ANY)] + [vmem] * 12,
+        out_specs=[vmem] * 8,
+        compiler_params=pltpu.CompilerParams(vmem_limit_bytes=VMEM_LIMIT),
+        cost_estimate=pl.CostEstimate(flops=10**8, bytes_accessed=10**6, transcendentals=0),
+        name="tables",
+    )(
+        fine_basis, fine_eigen, middle_basis, middle_eigen, after,
+        *[jnp.asarray(t) for level in (FINE, MID) for t in level.tables()],
+    )
 
 
 def schwarz_kernel(
     residual,
     middle,
     scale,
-    fine_basis,
     fine_coeff,
-    fine_eigen,
-    middle_basis,
     middle_coeff,
-    middle_eigen,
-    *refs,
+    x_low,
+    x_high,
+    y_low,
+    y_high,
+    forward,
+    backward,
+    inverse,
+    forward_m,
+    backward_m,
+    inverse_m,
+    fine_out,
+    middle_out,
+    x_up,
+    x_down,
+    y_up,
+    y_down,
+    planes,
+    rims,
+    sides,
+    spectrum,
+    hats,
+    planes_m,
+    rims_m,
+    sides_m,
+    spectrum_m,
+    hats_m,
+    solved,
+    in_sems,
+    out_sems,
 ):
-    halos, refs = refs[:8], refs[8:]
-    fine_tables, refs = refs[:6], refs[6:]
-    middle_tables, refs = refs[:6], refs[6:]
-    fine_out, middle_out, refs = refs[0], refs[1], refs[2:]
-    sends, refs = refs[:8], refs[8:]
-    (
-        planes,
-        rims,
-        sides,
-        forward,
-        backward,
-        inverse,
-        spectrum,
-        hats,
-        planes_m,
-        rims_m,
-        sides_m,
-        forward_m,
-        backward_m,
-        inverse_m,
-        spectrum_m,
-        hats_m,
-        solved,
-        in_sems,
-        out_sems,
-    ) = refs
-    x_low, x_high, y_low, y_high, d_ll, d_lh, d_hl, d_hh = halos
-    diags = ((d_ll, d_lh), (d_hl, d_hh))
     copies = []
     for ex in range(EX):
         for ey in range(EY):
@@ -467,33 +591,29 @@
     for ex in range(EX):
         for ey in range(EY):
             planes_m[ey, 2 + 4 * ex : 6 + 4 * ex] = middle[ex, ey]
-    build_tables(FINE, fine_tables, fine_basis, fine_eigen, forward, backward, inverse)
-    build_tables(MID, middle_tables, middle_basis, middle_eigen, forward_m, backward_m, inverse_m)
-    assemble(MID, planes_m, rims_m, sides_m, x_low, x_high, y_low, y_high, diags)
-
-    def middle_step(q, carry):
-        solve_pair(
-            MID, q, planes_m, rims_m, middle_coeff, forward_m, backward_m, inverse_m, scale,
-            spectrum_m, hats_m, middle_out,
+    assemble(MID, planes_m, rims_m, sides_m, x_low, x_high, y_low, y_high)
+
+    def middle_step(step, carry):
+        solve_pairs(
+            MID, step * MID_GROUP, MID_GROUP, planes_m, rims_m, middle_coeff, forward_m, backward_m,
+            inverse_m, scale, spectrum_m, hats_m, middle_out,
         )
         return carry
 
-    lax.fori_loop(0, 8, middle_step, 0)
+    lax.fori_loop(0, 8 // MID_GROUP, middle_step, 0)
     for copy in copies:
         copy.wait()
-    assemble(FINE, planes, rims, sides, x_low, x_high, y_low, y_high, diags)
+    assemble(FINE, planes, rims, sides, x_low, x_high, y_low, y_high)
 
     def fine_step(q, carry):
-        solve_pair(
-            FINE, q, planes, rims, fine_coeff, forward, backward, inverse, scale,
-            spectrum, hats, solved,
+        solve_pairs(
+            FINE, q, 1, planes, rims, fine_coeff, forward, backward,
+            inverse, scale, spectrum, hats, solved,
         )
         pltpu.make_async_copy(solved.at[q], fine_out.at[q], out_sems.at[q]).start()
         return carry
 
     lax.fori_loop(0, 8, fine_step, 0)
-
-    x_up, x_down, y_up, y_down, d_uu, d_ud, d_du, d_dd = sends
     for n, source, base in ((8, solved, 0), (4, middle_out, 256)):
         core = n * n
         for out, ex, node in ((x_up, EX - 1, n - 1), (x_down, 0, 0)):
@@ -507,34 +627,23 @@
                     out[row : row + n] = source[
                         2 * ex + ey // 2, ey % 2, a, node * n : node * n + n
                     ]
-    for out, up_x, up_y in ((d_uu, 1, 1), (d_ud, 1, 0), (d_du, 0, 1), (d_dd, 0, 0)):
-        out[8:16] = jnp.zeros((8, LANES), F32)
-        for n, source, base in ((8, solved, 0), (4, middle_out, 8)):
-            a, b = (n - 1) * up_x, (n - 1) * up_y
-            q, h = 2 * (EX - 1) * up_x + up_y, up_y
-            out[base : base + n] = source[q, h, a, b * n : b * n + n]
     for q in range(8):
         pltpu.make_async_copy(solved.at[q], fine_out.at[q], out_sems.at[q]).wait()
 
 
-def schwarz(residual, middle, scale, fine_basis, fine_eigen, middle_basis, middle_eigen, halos):
+def schwarz(residual, middle, scale, halos, tables):
     vmem = pl.BlockSpec(memory_space=pltpu.VMEM)
     smem = pl.BlockSpec(memory_space=pltpu.SMEM)
-    hbm = pl.BlockSpec(memory_space=pl.ANY)
-    tables = [jnp.asarray(t) for level in (FINE, MID) for t in level.tables()]
+    hbm = pl.BlockSpec(memory_space=pltpu.HBM)
     face = jax.ShapeDtypeStruct((FACE_ROWS, LANES), F32)
-    edge = jax.ShapeDtypeStruct((EDGE_ROWS, LANES), F32)
-
-    def scratch(level):
+
+    def scratch(level, group):
         return [
             pltpu.VMEM((EY, level.planes, level.core, LANES), F32),
             pltpu.VMEM((EY, EX * level.n, level.rim, LANES), F32),
             pltpu.VMEM((4, EX * level.core, LANES), F32),
-            pltpu.VMEM((2 * level.modes, 2 * level.depth), BF16),
-            pltpu.VMEM((2 * level.core, 2 * level.modes), BF16),
-            pltpu.VMEM((level.wide, level.modes, LANES), F32),
-            pltpu.VMEM((level.wide, 2 * level.depth, 2 * LANES), BF16),
-            pltpu.VMEM((level.wide, level.core, 2 * LANES), F32),
+            pltpu.VMEM((group, level.wide, 2 * level.depth, 2 * LANES), BF16),
+            pltpu.VMEM((group, level.wide, level.core, 2 * LANES), F32),
         ]
 
     return pl.pallas_call(
@@ -543,12 +652,11 @@
             jax.ShapeDtypeStruct((8, 2, 8, 64, LANES), F32),
             jax.ShapeDtypeStruct((8, 2, 4, 16, LANES), F32),
         ]
-        + [face] * 4
-        + [edge] * 4,
-        in_specs=[hbm, vmem, vmem, vmem, smem, vmem, vmem, smem, vmem] + [vmem] * 20,
-        out_specs=[hbm] + [vmem] * 9,
-        scratch_shapes=scratch(FINE)
-        + scratch(MID)
+        + [face] * 4,
+        in_specs=[hbm, vmem, vmem, smem, smem] + [vmem] * 10,
+        out_specs=[hbm] + [vmem] * 5,
+        scratch_shapes=scratch(FINE, 1)
+        + scratch(MID, MID_GROUP)
         + [
             pltpu.VMEM((8, 2, 8, 64, LANES), F32),
             pltpu.SemaphoreType.DMA((16,)),
@@ -556,33 +664,29 @@
         ],
         compiler_params=pltpu.CompilerParams(vmem_limit_bytes=VMEM_LIMIT),
         cost_estimate=pl.CostEstimate(
-            flops=8 * 10**9, bytes_accessed=12 * 10**6, transcendentals=0
+            flops=10**11, bytes_accessed=12 * 10**6, transcendentals=0
         ),
         name="schwarz",
-    )(
-        residual, middle, scale, fine_basis, fine_basis[0], fine_eigen,
-        middle_basis, middle_basis[0], middle_eigen, *halos, *tables,
-    )
-
-
-def coarse_kernel(place, rows_x, gathered, forward_y, back_y, hartley_z, lines, out, held, part):
-    own_x, own_y = place[0], place[1]
+    )(residual, middle, scale, *tables[6:], *halos, *tables[:6])
+
+
+def coarse_kernel(rows_x, gathered, table, out, held, part):
+    own_x, own_y = lax.axis_index("px"), lax.axis_index("py")
+    high, low = split(table[0:64])
+    forward_y = jnp.concatenate([high, low], axis=0)[:, 0:80]
 
     def y_step(p, carry):
-        before = lax.rem(p + 7, 8)
         slabs = []
         for lx in range(4):
             pieces = []
             for ly in range(5):
-                piece = gathered[pl.ds(p * 512 + lx * 5 + ly, 16, stride=32), :]
-                if lx == 0:
-                    piece += gathered[pl.ds(before * 512 + 20 + ly, 16, stride=32), :]
-                pieces.append(piece)
+                row = p * (16 * VERTEX_ROWS) + lx * 5 + ly
+                pieces.append(gathered[pl.ds(row, 16, stride=VERTEX_ROWS), :])
             slabs.append(jnp.concatenate(pieces, axis=0))
         for half in (0, 2):
             high, low = split(jnp.concatenate([slabs[half], slabs[half + 1]], axis=1))
-            both = dot(forward_y[...], jnp.concatenate([high, low], axis=0))
-            total = both[0:64] + both[64:128]
+            both = dot(forward_y, high)
+            total = both[0:64] + both[64:128] + dot(forward_y[0:64], low)
             held[4 * p + half] = total[:, 0:LANES]
             held[4 * p + half + 1] = total[:, LANES : 2 * LANES]
         return carry
@@ -596,7 +700,7 @@
         values = [held[x, rows, :] for x in range(32)]
         even = [values[0]] + [values[x] + values[32 - x] for x in range(1, 16)] + [values[16]]
         odd = [None] + [values[x] - values[32 - x] for x in range(1, 16)]
-        base = lines[rows, :]
+        base = table[pl.ds(pl.multiple_of(64 + chunk * 8, 8), 8), :]
         totals = [None] * 5
         for k in range(17):
             cosine = even[0]
@@ -619,55 +723,46 @@
         return carry
 
     lax.fori_loop(0, 8, x_step, 0)
-    own_rows = back_y[own_y]
+    own_rows = table[pl.ds(pl.multiple_of(256 + own_y * 8, 8), 8), :][:, 0:64]
     solved = jnp.concatenate([exact_dot(own_rows, part[lx]) for lx in range(5)], axis=0)
-    out[...] = exact_dot(solved, hartley_z[...]) * (1.0 / (32 * 64 * 128))
+    out[...] = exact_dot(solved, table[128:256]) * (1.0 / (32 * 64 * 128))
+
+
+def coarse_table():
+    table_y = hartley(64)
+    out = np.zeros((384, 128), np.float32)
+    for q in range(16):
+        for ly in range(5):
+            out[0:64, ly * 16 + q] = table_y[:, (4 * q + ly) % 64]
+            out[256 + 8 * q + ly, 0:64] = table_y[(4 * q + ly) % 64]
+    out[64:128] = 24.0 * (line_eigen(64)[:, None] + line_eigen(128)[None, :]) + 0.5
+    out[128:256] = hartley(128)
+    return out
 
 
 def coarse(gathered):
     vmem = pl.BlockSpec(memory_space=pltpu.VMEM)
     smem = pl.BlockSpec(memory_space=pltpu.SMEM)
-    place = jnp.stack([lax.axis_index("px"), lax.axis_index("py")]).astype(jnp.int32)
-    table_y = hartley(64)
-    forward = np.zeros((64, 160), np.float32)
-    back = np.zeros((16, 8, 64), np.float32)
-    for q in range(16):
-        for ly in range(5):
-            forward[:, ly * 16 + q] = table_y[:, (4 * q + ly) % 64]
-            back[q, ly] = table_y[(4 * q + ly) % 64]
-    forward[:, 80:] = forward[:, :80]
-    high, low = split_np(forward)
-    low[:, 80:] = 0
-    lines = 24.0 * (line_eigen(64)[:, None] + line_eigen(128)[None, :]) + 0.5
     return pl.pallas_call(
         coarse_kernel,
         out_shape=jax.ShapeDtypeStruct((40, LANES), F32),
-        in_specs=[smem, smem] + [vmem] * 5,
+        in_specs=[smem, vmem, vmem],
         out_specs=vmem,
         scratch_shapes=[
             pltpu.VMEM((32, 64, LANES), F32),
             pltpu.VMEM((5, 64, LANES), F32),
         ],
-        compiler_params=pltpu.CompilerParams(vmem_limit_bytes=VMEM_LIMIT),
+        compiler_params=pltpu.CompilerParams(vmem_limit_bytes=16 * MIB),
         cost_estimate=pl.CostEstimate(
             flops=2 * 10**9, bytes_accessed=4 * 10**6, transcendentals=0
         ),
         name="coarse",
-    )(
-        place,
-        jnp.asarray(hartley(32), F32),
-        gathered,
-        jnp.asarray(np.concatenate([high, low], axis=0)),
-        jnp.asarray(back),
-        jnp.asarray(hartley(128), F32),
-        jnp.asarray(lines, F32),
-    )
-
-
-def average_faces(level, field, sides, x_low, x_high, y_low, y_high, diags):
+    )(jnp.asarray(hartley(32), F32), gathered, jnp.asarray(coarse_table()))
+
+
+def average_faces(level, field, sides, x_low, x_high, y_low, y_high):
     n, core = level.n, level.core
     base = 0 if n == 8 else 256
-    edge = 0 if n == 8 else 8
 
     def at(ex, ey):
         return 2 * ex + ey // 2, ey % 2
@@ -685,16 +780,6 @@
             field[q + 2, h, 0] = total
     for side, halo in ((0, y_low), (1, y_high)):
         sides[side] = halo[base : base + EX * core]
-        low = diags[0][side][edge : edge + n]
-        high = diags[1][side][edge : edge + n]
-        end = EX * core
-        sides[side, 0:n] = 0.5 * (sides[side, 0:n] + low)
-        sides[side, end - n : end] = 0.5 * (sides[side, end - n : end] + high)
-        for ex in range(EX - 1):
-            row = ex * core + core
-            total = 0.5 * (sides[side, row - n : row] + sides[side, row : row + n])
-            sides[side, row - n : row] = total
-            sides[side, row : row + n] = total
     for ex in range(EX):
         for a in range(n):
             row = (ex * n + a) * n
@@ -713,7 +798,7 @@
 
 
 def finish_kernel(
-    fine, middle, coarse_part, prolong, x_low, x_high, y_low, y_high, d_ll, d_lh, d_hl, d_hh,
+    fine, middle, coarse_part, prolong, x_low, x_high, y_low, y_high,
     out, field, sides, field_m, sides_m, corner, result, in_sems, out_sems,
 ):
     copies = []
@@ -721,9 +806,8 @@
         copy = pltpu.make_async_copy(fine.at[q], field.at[q], in_sems.at[q])
         copy.start()
         copies.append(copy)
-    diags = ((d_ll, d_lh), (d_hl, d_hh))
     field_m[...] = middle[...]
-    average_faces(MID, field_m, sides_m, x_low, x_high, y_low, y_high, diags)
+    average_faces(MID, field_m, sides_m, x_low, x_high, y_low, y_high)
     near = coarse_part[...]
     far = pltpu.roll(near, LANES - 1, 1)
     for q in range(8):
@@ -738,7 +822,7 @@
                     corner[q, h, place + 1 : place + 2] = far[row : row + 1]
     for copy in copies:
         copy.wait()
-    average_faces(FINE, field, sides, x_low, x_high, y_low, y_high, diags)
+    average_faces(FINE, field, sides, x_low, x_high, y_low, y_high)
 
     def step(q, carry):
         for h in (0, 1):
@@ -771,7 +855,7 @@
     return pl.pallas_call(
         finish_kernel,
         out_shape=jax.ShapeDtypeStruct((8, 2, 8, 64, LANES), F32),
-        in_specs=[hbm] + [vmem] * 11,
+        in_specs=[hbm] + [vmem] * 7,
         out_specs=hbm,
         scratch_shapes=[
             pltpu.VMEM((8, 2, 8, 64, LANES), F32),
@@ -783,7 +867,7 @@
             pltpu.SemaphoreType.DMA((8,)),
             pltpu.SemaphoreType.DMA((8,)),
         ],
-        compiler_params=pltpu.CompilerParams(vmem_limit_bytes=VMEM_LIMIT),
+        compiler_params=pltpu.CompilerParams(vmem_limit_bytes=16 * MIB),
         cost_estimate=pl.CostEstimate(
             flops=2 * 10**9, bytes_accessed=8 * 10**6, transcendentals=0
         ),
@@ -796,46 +880,25 @@
     return lax.ppermute(values, axis, [(i, (i + step) % count) for i in range(count)])
 
 
-def shift_both(values, step_x, step_y):
-    count_x, count_y = lax.axis_size("px"), lax.axis_size("py")
-    pairs = [
-        (i * count_y + j, (i + step_x) % count_x * count_y + (j + step_y) % count_y)
-        for i in range(count_x)
-        for j in range(count_y)
-    ]
-    return lax.ppermute(values, ("px", "py"), pairs)
-
-
-def exchange(sends):
-    x_up, x_down, y_up, y_down, d_uu, d_ud, d_du, d_dd = sends
-    return (
-        shift(x_up, "px", 1),
-        shift(x_down, "px", -1),
-        shift(y_up, "py", 1),
-        shift(y_down, "py", -1),
-        shift_both(d_uu, 1, 1),
-        shift_both(d_ud, 1, -1),
-        shift_both(d_du, -1, 1),
-        shift_both(d_dd, -1, -1),
-    )
-
-
 def on_device(residual, scale, fine_basis, fine_eigen, middle_basis, middle_eigen):
     shape = residual.shape
     residual = residual.reshape(EX, EY, 8, 64, LANES)
-    packed = pack(residual)
-    sends, middle, vertex = packed[:8], packed[8], packed[9]
-    halos = exchange(sends)
+    x_up, x_down, y_up, y_down, middle, vertex = pack(residual)
+    x_halos = shift(x_up, "px", 1), shift(x_down, "px", -1)
+    tables = solve_tables(fine_basis, fine_eigen, middle_basis, middle_eigen, vertex)
+    y_up, y_down, vertex = join(*x_halos, y_up, y_down, vertex, tables[-1])
+    halos = x_halos + (shift(y_up, "py", 1), shift(y_down, "py", -1))
     devices = lax.axis_size("px") * lax.axis_size("py")
-    copies = jnp.broadcast_to(vertex[None], (devices, 32, LANES))
-    gathered = lax.all_to_all(copies, ("px", "py"), 0, 0).reshape(devices * 32, LANES)
-    solved = schwarz(
-        residual, middle, scale, fine_basis, fine_eigen, middle_basis, middle_eigen, halos
+    gathered = lax.all_to_all(spread(vertex, devices), ("px", "py"), 0, 0)
+    gathered = gathered.reshape(devices * VERTEX_ROWS, LANES)
+    fine_solved, middle_solved, x_up, x_down, y_up, y_down = schwarz(
+        residual, middle, scale, halos, tables
     )
-    fine_solved, middle_solved, faces = solved[0], solved[1], solved[2:]
-    faces = exchange(faces)
+    x_halos = shift(x_up, "px", 1), shift(x_down, "px", -1)
+    y_up, y_down = join_faces(*x_halos, y_up, y_down)
+    halos = x_halos + (shift(y_up, "py", 1), shift(y_down, "py", -1))
     coarse_part = coarse(gathered)
-    return finish(fine_solved, middle_solved, coarse_part, faces).reshape(shape)
+    return finish(fine_solved, middle_solved, coarse_part, halos).reshape(shape)
 
 
 def solution(mesh):

time: 134 us -> 76.3 us (0.57)
  starting transfers between devices: 45.7 us -> 24.8 us
  waiting for transfers between devices: 24.8 us -> 4.71 us
  Pallas kernels: 56.3 us -> 42.9 us
  local copies, waits for them, and re-layouts: 6.39 us -> 3.08 us
    ppermute x8 -> x0, waiting for transfers between devices: 23.6 us -> none  [shift_both(): return lax.ppermute(values, ('px', 'py'), pairs)]
    ppermute x8 -> x0, starting transfers between devices: 17.9 us -> none  [shift_both(): return lax.ppermute(values, ('px', 'py'), pairs)]
    pallas_call x1, Pallas kernels: 37.1 us -> 20.1 us  [schwarz(): pl.pallas_call(schwarz_kernel, out_shape=[jax.ShapeDtypeStruct((8, 2, 8,...]
    pallas_call x1 -> x5, Pallas kernels: 5.15 us -> 13.9 us  [the longest x1 4.16 us: pack(): pl.pallas_call(pack_kernel, out_shape=[x_halo] * 2 + [y_halo] * 2 + [jax....]
    all_to_all x1, starting transfers between devices: 11.2 us -> 5.84 us  [on_device(): gathered = lax.all_to_all(spread(vertex, devices), ('px', 'py'), 0, 0)]
    ppermute x8, waiting for transfers between devices: 1.2 us -> 4.71 us  [shift(): lax.ppermute(values, axis, [(i, (i + step) % count) for i in range(count)])]
    pallas_call x1, Pallas kernels: 7.34 us -> 4.21 us  [finish(): pl.pallas_call(finish_kernel, out_shape=jax.ShapeDtypeStruct((8, 2, 8, 64...]
    broadcast_in_dim x1 -> x0, local copies, waits for them, and re-layouts: 2.36 us -> none  [on_device(): copies = jnp.broadcast_to(vertex[None], (devices, 32, LANES))]
  transfers between devices with their start and end apart: 17 -> 9, of which waited for: 3 -> 3; matrix products, arithmetic and copies ran while one was open for 2% -> 1% of each run, Pallas kernels for 33% -> 43%
where the time goes in v2:
time: 76.3 us; the launch traced here: 75.7 us
  Pallas kernels  42.9 us (56%)
  starting transfers between devices  24.8 us (33%)
  waiting for transfers between devices  4.71 us (6%)
  local copies, waits for them, and re-layouts  3.08 us (4%)
    pallas_call x1, Pallas kernels, schwarz(): pl.pallas_call(schwarz_kernel, out_shape=[jax.ShapeDtypeStruct((8, 2, 8,...  20.1 us
    ppermute x8, starting transfers between devices, shift(): lax.ppermute(values, axis, [(i, (i + step) % count) for i in range(count)])  18.9 us
    all_to_all x1, starting transfers between devices, on_device(): gathered = lax.all_to_all(spread(vertex, devices), ('px', 'py'), 0, 0)  5.84 us
    ppermute x8, waiting for transfers between devices, shift(): lax.ppermute(values, axis, [(i, (i + step) % count) for i in range(count)])  4.71 us
    pallas_call x1, Pallas kernels, coarse(): pl.pallas_call(coarse_kernel, out_shape=jax.ShapeDtypeStruct((40, LANES),...  4.68 us
    pallas_call x1, Pallas kernels, finish(): pl.pallas_call(finish_kernel, out_shape=jax.ShapeDtypeStruct((8, 2, 8, 64...  4.21 us
    pallas_call x1, Pallas kernels, pack(): pl.pallas_call(pack_kernel, out_shape=[x_halo] * 2 + [y_halo] * 2 + [jax....  4.16 us
    pallas_call x1, Pallas kernels, solve_tables(): pl.pallas_call(tables_kernel, out_shape=shapes, in_specs=[vmem] * 4 + [pl...  3.72 us
  transfers between devices with their start and end apart: 9, of which 3 were waited for; matrix products, arithmetic and copies ran while one was open for 1% of the time, Pallas kernels for 43%

profile of v2, /device:TPU:0, one launch (start us, length us, event | category | flops | bytes accessed | tf_op | source)
XLA Modules:
  0.0 75.7 jit_solution(9306753935671842147)
XLA Ops:
  0.0 4.2 %pack.1 = (f32[648,128]{1,0:T(8,128)}, f32[648,128]{1,0:T(8,128)}, f32[640,128]{1,0:T(8,128)}, f32[640,128]{1,0:T(8,128)}, f32[4,4,4,16,128]{4,3,2,1,0:T(8,128)}, /*index=5*/f32[32,128]{1,0:T(8,128)}) custom-call(f32[4,4,8,64,128]{4,3,2,1,0:T(8,128)} %bitcast.4, bf16[160,512]{1,0:T(8,128)(2,1)} %constant.36.clone.restrict_in, ...), custom_call_target="tpu_custom_call" | custom-call | flops 1000000000 | bytes 8000000 | tf_op jit(solution)/shard_map/pack/pallas_call | solution.py:245
  4.2 2.9 %collective-permute-start.1 = (f32[648,128]{1,0:T(8,128)}, f32[648,128]{1,0:T(8,128)S(1)}, u32[]{:S(2)}, u32[]{:S(2)}) collective-permute-start(f32[648,128]{1,0:T(8,128)} %get-tuple-element.35), channel_id=1, source_target_pairs={{0,112},{16,0},{32,16},{48,32},{64,48},{80,64},{96,80},{112,96},{1... | collective-permute-start | bytes 995336 | tf_op jit(solution)/shard_map/ppermute | solution.py:880
  7.1 0.6 copy.25.fine_basis
  7.8 3.7 %tables.1 = (bf16[224,192]{1,0:T(8,128)(2,1)}, bf16[128,224]{1,0:T(8,128)(2,1)}, f32[10,112,128]{2,1,0:T(8,128)}, bf16[96,64]{1,0:T(8,128)(2,1)}, bf16[32,96]{1,...) custom-call(f32[3,10,10]{2,1,0:T(8,128)} %copy.25.fine_basis, f32[3,10]{1,0:T(4,128)} %fine_eigen.1, ...), custom_call_target="tpu_custom_call" | custom-call | flops 100000000 | bytes 1000000 | tf_op jit(solution)/shard_map/tables/pallas_call | solution.py:533
  11.5 0.7 collective-permute-done.x_low
  12.2 0.7 copy-done.9
  12.9 0.1 copy-done.10
  13.0 2.1 %join.1 = (f32[664,128]{1,0:T(8,128)}, f32[664,128]{1,0:T(8,128)}, f32[24,128]{1,0:T(8,128)}) custom-call(f32[648,128]{1,0:T(8,128)} %copy-done.9, f32[648,128]{1,0:T(8,128)} %copy-done.10, f32[640,128]{1,0:T(8,128)} %get-tuple-element.36.y_up, f32[640,128]{1,0:T(8,128)} %get-tuple-element.37.y_down, f32[32,128]{1,0:T(8,128)} %get-tuple-element.31.after.vertex, ...), custom_call_target="tpu_custom_call" | custom-call | flops 1000000 | bytes 3000000 | tf_op jit(solution)/shard_map/join/pallas_call | solution.py:299
  15.1 1.7 %collective-permute-start.2 = (f32[664,128]{1,0:T(8,128)}, f32[664,128]{1,0:T(8,128)S(1)}, u32[]{:S(2)}, u32[]{:S(2)}) collective-permute-start(f32[664,128]{1,0:T(8,128)} %get-tuple-element.38), channel_id=1, source_target_pairs={{0,1},{1,2},{2,3},{3,4},{4,5},{5,6},{6,7},{7,8},{8,9},{9,10},{10,1... | collective-permute-start | bytes 1019912 | tf_op jit(solution)/shard_map/ppermute | solution.py:880
  16.8 4.9 %collective-permute-start.3 = (f32[664,128]{1,0:T(8,128)}, f32[664,128]{1,0:T(8,128)S(1)}, u32[]{:S(2)}, u32[]{:S(2)}) collective-permute-start(f32[664,128]{1,0:T(8,128)} %get-tuple-element.39), channel_id=1, source_target_pairs={{0,15},{1,0},{2,1},{3,2},{4,3},{5,4},{6,5},{7,6},{8,7},{9,8},{10,9... | collective-permute-start | bytes 1019912 | tf_op jit(solution)/shard_map/ppermute | solution.py:880
  21.7 2.0 %spread.1 = f32[128,24,128]{2,1,0:T(8,128)} custom-call(f32[24,128]{1,0:T(8,128)} %get-tuple-element.48.source), custom_call_target="tpu_custom_call" | custom-call | flops 1000000 | bytes 2000000 | tf_op jit(solution)/shard_map/spread/pallas_call | solution.py:346
  23.7 5.8 %all-to-all-start = ((f32[128,24,128]{2,1,0:T(8,128)}), f32[128,24,128]{2,1,0:T(8,128)S(1)}, u32[]{:S(2)}, u32[]{:S(2)}) async-start(f32[128,24,128]{2,1,0:T(8,128)} %spread.1), calls=%async_computation | async-start | bytes 3145728 | tf_op jit(solution)/shard_map/all_to_all | solution.py:892
  29.5 0.8 %collective-permute-done.2.y_low = f32[664,128]{1,0:T(8,128)S(1)} collective-permute-done((f32[664,128]{1,0:T(8,128)}, f32[664,128]{1,0:T(8,128)S(1)}, u32[]{:S(2)}, u32[]{:S(2)}) %collective-permute-start.2) | collective-permute-done | bytes 340000 | tf_op jit(solution)/shard_map/ppermute | solution.py:880
  30.3 0.7 copy-done.12
  31.0 0.1 copy-done.13
  31.2 20.1 %schwarz.1 = (f32[8,2,8,64,128]{4,3,2,1,0:T(8,128)}, f32[8,2,4,16,128]{4,3,2,1,0:T(8,128)}, f32[320,128]{1,0:T(8,128)}, f32[320,128]{1,0:T(8,128)}, f32[320,128]{1,0:T(8,128)}, /*index=5*/f32[320,128]{1,0:T(8,128)}) custom-call(f32[4,4,8,64,128]{4,3,2,1,0:T(8,128)} %bitcast.5, f32[4,4,4,16,128]{4,3,2,1,0:T(8,128)} %get-tuple-element.30.middle, ...), custom_call_target="tpu_custom_call" | custom-call | flops 99999997952 | bytes 12000000 | tf_op jit(solution)/shard_map/schwarz/pallas_call | solution.py:649
  51.4 2.9 %collective-permute-start.5 = (f32[320,128]{1,0:T(8,128)}, f32[320,128]{1,0:T(8,128)S(1)}, u32[]{:S(2)}, u32[]{:S(2)}) collective-permute-start(f32[320,128]{1,0:T(8,128)} %get-tuple-element.50), channel_id=1, source_target_pairs={{0,112},{16,0},{32,16},{48,32},{64,48},{80,64},{96,80},{112,96},{1... | collective-permute-start | bytes 491528 | tf_op jit(solution)/shard_map/ppermute | solution.py:880
  54.3 3.2 %collective-permute-done.4.x_low = f32[320,128]{1,0:T(8,128)S(1)} collective-permute-done((f32[320,128]{1,0:T(8,128)}, f32[320,128]{1,0:T(8,128)S(1)}, u32[]{:S(2)}, u32[]{:S(2)}) %collective-permute-start.4) | collective-permute-done | bytes 163872 | tf_op jit(solution)/shard_map/ppermute | solution.py:880
  57.5 0.7 copy-done.1
  58.3 1.9 %join_faces.1 = (f32[320,128]{1,0:T(8,128)}, f32[320,128]{1,0:T(8,128)}) custom-call(f32[320,128]{1,0:T(8,128)} %copy-done.1, f32[320,128]{1,0:T(8,128)} %copy-done.3, f32[320,128]{1,0:T(8,128)} %get-tuple-element.51.y_up, f32[320,128]{1,0:T(8,128)} %get-tuple-element.52.y_down), custom_call_target="tpu_custom_call" | custom-call | flops 1000000 | bytes 1000000 | tf_op jit(solution)/shard_map/join_faces/pallas_call | solution.py:329
  60.2 0.2 collective-permute-start.6
  60.4 6.2 %collective-permute-start.7 = (f32[320,128]{1,0:T(8,128)}, f32[320,128]{1,0:T(8,128)S(1)}, u32[]{:S(2)}, u32[]{:S(2)}) collective-permute-start(f32[320,128]{1,0:T(8,128)} %get-tuple-element.54), channel_id=1, source_target_pairs={{0,15},{1,0},{2,1},{3,2},{4,3},{5,4},{6,5},{7,6},{8,7},{9,8},{10,9... | collective-permute-start | bytes 491528 | tf_op jit(solution)/shard_map/ppermute | solution.py:880
  66.6 4.7 %coarse.1.coarse_part = f32[40,128]{1,0:T(8,128)S(1)} custom-call(f32[32,32]{1,0:T(8,128)S(1)} %copy-done.8, f32[3072,128]{1,0:T(8,128)S(1)} %bitcast.3, f32[384,128]{1,0:T(8,128)S(1)} %copy-done.7), custom_call_target="tpu_custom_call" | custom-call | flops 2000000000 | bytes 4000000 | tf_op jit(solution)/shard_map/coarse/pallas_call | solution.py:746
  71.4 4.2 %finish.1 = f32[8,2,8,64,128]{4,3,2,1,0:T(8,128)} custom-call(f32[8,2,8,64,128]{4,3,2,1,0:T(8,128)S(1)} %copy-done, f32[8,2,4,16,128]{4,3,2,1,0:T(8,128)S(1)} %copy-done.5, f32[40,128]{1,0:T(8,128)S(1)} %coarse.1.coarse_part, bf16[512,240]{1,0:T(8,128)(2,1)S(1)} %copy-done.6, f32[320,128]{1,0:T(8,128)S(1)} %copy-done.2, f32[320,128]{1,0:T(8,128)S(1)} %copy-done.4, ...), custom_call_target="tpu_custom_call" | custom-call | flops 2000000000 | bytes 8000000 | tf_op jit(solution)/shard_map/finish/pallas_call | solution.py:855
  (31 shorter events, 0.2 us)
Async XLA Ops:
  0.0 7.1 %copy-start.11 = (f32[3,10,10]{2,0,1:T(4,128)S(1)}, f32[3,10,10]{2,0,1:T(4,128)}, u32[]{:S(2)}) copy-start(f32[3,10,10]{2,0,1:T(4,128)} %param.26) | copy-start | bytes 3604
  4.2 8.0 %collective-permute-start = (f32[648,128]{1,0:T(8,128)}, f32[648,128]{1,0:T(8,128)S(1)}, u32[]{:S(2)}, u32[]{:S(2)}) collective-permute-start(f32[648,128]{1,0:T(8,128)} %get-tuple-element.34), channel_id=1, source_target_pairs={{0,16},{16,32},{32,48},{48,64},{64,80},{80,96},{96,112},{112,0},{1... | collective-permute-start | bytes 995336 | tf_op jit(solution)/shard_map/ppermute | solution.py:880
  4.2 8.0 %collective-permute-start.1 = (f32[648,128]{1,0:T(8,128)}, f32[648,128]{1,0:T(8,128)S(1)}, u32[]{:S(2)}, u32[]{:S(2)}) collective-permute-start(f32[648,128]{1,0:T(8,128)} %get-tuple-element.35), channel_id=1, source_target_pairs={{0,112},{16,0},{32,16},{48,32},{64,48},{80,64},{96,80},{112,96},{1... | collective-permute-start | bytes 995336 | tf_op jit(solution)/shard_map/ppermute | solution.py:880
  12.1 0.7 copy-start.9
  12.2 0.8 %copy-start.10 = (f32[648,128]{1,0:T(8,128)}, f32[648,128]{1,0:T(8,128)S(1)}, u32[]{:S(2)}) copy-start(f32[648,128]{1,0:T(8,128)S(1)} %collective-permute-done.1.x_high) | copy-start | bytes 995332
  15.1 15.2 %collective-permute-start.2 = (f32[664,128]{1,0:T(8,128)}, f32[664,128]{1,0:T(8,128)S(1)}, u32[]{:S(2)}, u32[]{:S(2)}) collective-permute-start(f32[664,128]{1,0:T(8,128)} %get-tuple-element.38), channel_id=1, source_target_pairs={{0,1},{1,2},{2,3},{3,4},{4,5},{5,6},{6,7},{7,8},{8,9},{9,10},{10,1... | collective-permute-start | bytes 1019912 | tf_op jit(solution)/shard_map/ppermute | solution.py:880
  16.8 13.5 %collective-permute-start.3 = (f32[664,128]{1,0:T(8,128)}, f32[664,128]{1,0:T(8,128)S(1)}, u32[]{:S(2)}, u32[]{:S(2)}) collective-permute-start(f32[664,128]{1,0:T(8,128)} %get-tuple-element.39), channel_id=1, source_target_pairs={{0,15},{1,0},{2,1},{3,2},{4,3},{5,4},{6,5},{7,6},{8,7},{9,8},{10,9... | collective-permute-start | bytes 1019912 | tf_op jit(solution)/shard_map/ppermute | solution.py:880
  23.7 42.9 %all-to-all-start = ((f32[128,24,128]{2,1,0:T(8,128)}), f32[128,24,128]{2,1,0:T(8,128)S(1)}, u32[]{:S(2)}, u32[]{:S(2)}) async-start(f32[128,24,128]{2,1,0:T(8,128)} %spread.1), calls=%async_computation | async-start | bytes 3145728 | tf_op jit(solution)/shard_map/all_to_all | solution.py:892
  30.3 0.7 copy-start.12
  30.3 0.8 %copy-start.13 = (f32[664,128]{1,0:T(8,128)}, f32[664,128]{1,0:T(8,128)S(1)}, u32[]{:S(2)}) copy-start(f32[664,128]{1,0:T(8,128)S(1)} %collective-permute-done.3.y_high) | copy-start | bytes 1019908
  31.2 35.5 %copy-start.7 = (f32[384,128]{1,0:T(8,128)S(1)}, f32[384,128]{1,0:T(8,128)}, u32[]{:S(2)}) copy-start(f32[384,128]{1,0:T(8,128)} %constant.52.clone.table) | copy-start | bytes 589828
  31.2 35.5 %copy-start.8 = (f32[32,32]{1,0:T(8,128)S(1)}, f32[32,32]{1,0:T(8,128)}, u32[]{:S(2)}) copy-start(f32[32,32]{1,0:T(8,128)} %constant.51.clone.rows_x) | copy-start | bytes 12292
  51.3 20.1 %copy-start.5 = (f32[8,2,4,16,128]{4,3,2,1,0:T(8,128)S(1)}, f32[8,2,4,16,128]{4,3,2,1,0:T(8,128)}, u32[]{:S(2)}) copy-start(f32[8,2,4,16,128]{4,3,2,1,0:T(8,128)} %get-tuple-element.47.middle) | copy-start | bytes 1572868
  51.3 20.1 %copy-start.6 = (bf16[512,240]{1,0:T(8,128)(2,1)S(1)}, bf16[512,240]{1,0:T(8,128)(2,1)}, u32[]{:S(2)}) copy-start(bf16[512,240]{1,0:T(8,128)(2,1)} %constant.53.clone.prolong) | copy-start | bytes 737284
  51.3 6.2 %collective-permute-start.4 = (f32[320,128]{1,0:T(8,128)}, f32[320,128]{1,0:T(8,128)S(1)}, u32[]{:S(2)}, u32[]{:S(2)}) collective-permute-start(f32[320,128]{1,0:T(8,128)} %get-tuple-element.49), channel_id=1, source_target_pairs={{0,16},{16,32},{32,48},{48,64},{64,80},{80,96},{96,112},{112,0},{1... | collective-permute-start | bytes 491528 | tf_op jit(solution)/shard_map/ppermute | solution.py:880
  51.4 6.2 %collective-permute-start.5 = (f32[320,128]{1,0:T(8,128)}, f32[320,128]{1,0:T(8,128)S(1)}, u32[]{:S(2)}, u32[]{:S(2)}) collective-permute-start(f32[320,128]{1,0:T(8,128)} %get-tuple-element.50), channel_id=1, source_target_pairs={{0,112},{16,0},{32,16},{48,32},{64,48},{80,64},{96,80},{112,96},{1... | collective-permute-start | bytes 491528 | tf_op jit(solution)/shard_map/ppermute | solution.py:880
  57.5 0.7 copy-start.1
  57.5 0.8 %copy-start.3 = (f32[320,128]{1,0:T(8,128)}, f32[320,128]{1,0:T(8,128)S(1)}, u32[]{:S(2)}) copy-start(f32[320,128]{1,0:T(8,128)S(1)} %collective-permute-done.5.x_high) | copy-start | bytes 491524
  60.2 11.2 %copy-start.2 = (f32[320,128]{1,0:T(8,128)S(1)}, f32[320,128]{1,0:T(8,128)}, u32[]{:S(2)}) copy-start(f32[320,128]{1,0:T(8,128)} %copy-done.1) | copy-start | bytes 491524
  60.2 11.2 %copy-start.4 = (f32[320,128]{1,0:T(8,128)S(1)}, f32[320,128]{1,0:T(8,128)}, u32[]{:S(2)}) copy-start(f32[320,128]{1,0:T(8,128)} %copy-done.3) | copy-start | bytes 491524
  60.2 11.2 %collective-permute-start.6 = (f32[320,128]{1,0:T(8,128)}, f32[320,128]{1,0:T(8,128)S(1)}, u32[]{:S(2)}, u32[]{:S(2)}) collective-permute-start(f32[320,128]{1,0:T(8,128)} %get-tuple-element.53), channel_id=1, source_target_pairs={{0,1},{1,2},{2,3},{3,4},{4,5},{5,6},{6,7},{7,8},{8,9},{9,10},{10,1... | collective-permute-start | bytes 491528 | tf_op jit(solution)/shard_map/ppermute | solution.py:880
  60.4 11.0 %collective-permute-start.7 = (f32[320,128]{1,0:T(8,128)}, f32[320,128]{1,0:T(8,128)S(1)}, u32[]{:S(2)}, u32[]{:S(2)}) collective-permute-start(f32[320,128]{1,0:T(8,128)} %get-tuple-element.54), channel_id=1, source_target_pairs={{0,15},{1,0},{2,1},{3,2},{4,3},{5,4},{6,5},{7,6},{8,7},{9,8},{10,9... | collective-permute-start | bytes 491528 | tf_op jit(solution)/shard_map/ppermute | solution.py:880
  66.6 4.8 %copy-start = (f32[8,2,8,64,128]{4,3,2,1,0:T(8,128)S(1)}, f32[8,2,8,64,128]{4,3,2,1,0:T(8,128)}, u32[]{:S(2)}) copy-start(f32[8,2,8,64,128]{4,3,2,1,0:T(8,128)} %get-tuple-element.46.fine) | copy-start | bytes 12582916

commit v3 on v2

--- a/solution.py
+++ b/solution.py
@@ -149,13 +149,45 @@
 
 LAYER_ROWS = 640
 X_ROWS = 648
-Y_ROWS = 664
 FACE_ROWS = 320
 VERTEX_ROWS = 24
-
-
-def plane_line(n, side):
-    return (640 if n == 8 else 656) + side * n
+EDGE_ROWS = 72
+EDGE_FACE_ROWS = 24
+
+
+def edge_row(n, side, kind):
+    return (0 if n == 8 else 48) + (side * 3 + kind) * n
+
+
+def edge_face_row(n, side):
+    return (0 if n == 8 else 16) + side * n
+
+
+class Either:
+    def __init__(self, flag, yes, no):
+        self.flag, self.yes, self.no = flag, yes, no
+
+    def __getitem__(self, index):
+        return jnp.where(self.flag, self.yes[index], self.no[index])
+
+
+def is_even(axis):
+    return lax.rem(lax.axis_index(axis), 2) == 0
+
+
+def received(axis, first, second):
+    flag = is_even(axis)
+    return Either(flag, second, first), Either(flag, first, second)
+
+
+def for_partners(axis, first, second, write):
+    @pl.when(is_even(axis))
+    def _():
+        write(first, second)
+
+    @pl.when(jnp.logical_not(is_even(axis)))
+    def _():
+        write(second, first)
 
 
 def pack_kernel(
@@ -163,10 +195,10 @@
     restrict_in,
     vertex_pick_in,
     hartley_in,
-    x_up,
-    x_down,
-    y_up,
-    y_down,
+    x_first,
+    x_second,
+    y_first,
+    y_second,
     middle,
     vertex,
     field,
@@ -201,41 +233,46 @@
                     middle[ex, ey + h, i] = part[16 * i : 16 * i + 16]
                 column = ex * EY + ey + h
                 corners[8 * column : 8 * column + 8] = part[64:72]
-    for out, ex, nodes, mids in ((x_up, EX - 1, (7, 6), (3, 2)), (x_down, 0, (0, 1), (0, 1))):
-        for layer in (0, 1):
-            for ey in range(EY):
-                row = (layer * EY + ey) * 64
-                out[row : row + 64] = field[ex, ey, nodes[layer]]
-                row = 512 + (layer * EY + ey) * 16
-                out[row : row + 16] = middle[ex, ey, mids[layer]]
-    for out, ey, nodes, mids in ((y_up, EY - 1, (7, 6), (3, 2)), (y_down, 0, (0, 1), (0, 1))):
-        for layer in (0, 1):
-            for ex in range(EX):
-                for a in range(8):
-                    row = (layer * EX + ex) * 64 + a * 8
-                    line = nodes[layer] * 8
-                    out[row : row + 8] = field[ex, ey, a, line : line + 8]
-                for a in range(4):
-                    row = 512 + (layer * EX + ex) * 16 + a * 4
-                    line = mids[layer] * 4
-                    out[row : row + 4] = middle[ex, ey, a, line : line + 4]
-    for out in (y_up, y_down):
-        for n, base in ((8, 0), (4, 512)):
-            core = n * n
-            for row in [base + k * core for k in (1, 2, 3, 5, 6, 7)]:
-                total = out[row - n : row] + out[row : row + n]
-                out[row - n : row] = total
-                out[row : row + n] = total
     copies[EX + 1].wait()
     copies[EX + 2].wait()
     values = corners[...]
-    low = exact_dot(vertex_pick[0], values)
-    high = exact_dot(vertex_pick[1], values)
-    total = low + pltpu.roll(high, 1, 1)
-    total = exact_dot(total, hartley_z[...])
+    near = exact_dot(vertex_pick[0], values)
+    far = exact_dot(vertex_pick[1], values)
+    total = exact_dot(near + pltpu.roll(far, 1, 1), hartley_z[...])
     vertex[...] = total
-    x_up[LAYER_ROWS:X_ROWS] = total[20:28]
-    x_down[LAYER_ROWS:X_ROWS] = jnp.zeros((8, LANES), F32)
+
+    def write_x(x_up, x_down):
+        for out, ex, nodes, mids in ((x_up, EX - 1, (7, 6), (3, 2)), (x_down, 0, (0, 1), (0, 1))):
+            for layer in (0, 1):
+                for ey in range(EY):
+                    row = (layer * EY + ey) * 64
+                    out[row : row + 64] = field[ex, ey, nodes[layer]]
+                    row = 512 + (layer * EY + ey) * 16
+                    out[row : row + 16] = middle[ex, ey, mids[layer]]
+        x_up[LAYER_ROWS:X_ROWS] = vertex[20:28]
+        x_down[LAYER_ROWS:X_ROWS] = jnp.zeros((8, LANES), F32)
+
+    for_partners("px", x_first, x_second, write_x)
+    def write_y(y_up, y_down):
+        for out, ey, nodes, mids in ((y_up, EY - 1, (7, 6), (3, 2)), (y_down, 0, (0, 1), (0, 1))):
+            for layer in (0, 1):
+                for ex in range(EX):
+                    for a in range(8):
+                        row = (layer * EX + ex) * 64 + a * 8
+                        line = nodes[layer] * 8
+                        out[row : row + 8] = field[ex, ey, a, line : line + 8]
+                    for a in range(4):
+                        row = 512 + (layer * EX + ex) * 16 + a * 4
+                        line = mids[layer] * 4
+                        out[row : row + 4] = middle[ex, ey, a, line : line + 4]
+            for n, base in ((8, 0), (4, 512)):
+                core = n * n
+                for row in [base + k * core for k in (1, 2, 3, 5, 6, 7)]:
+                    total = out[row - n : row] + out[row : row + n]
+                    out[row - n : row] = total
+                    out[row : row + n] = total
+
+    for_partners("py", y_first, y_second, write_y)
 
 
 def pack(residual):
@@ -271,70 +308,67 @@
     )
 
 
-def join_kernel(x_low, x_high, y_up, y_down, vertex, after, up, down, summed):
+def join_kernel(x_first, x_second, vertex, after, first, second, summed):
     del after
-    for out, source, ey, ends in ((up, y_up, EY - 1, True), (down, y_down, 0, False)):
-        out[0:LAYER_ROWS] = source[...]
-        for n, base in ((8, 0), (4, 512)):
-            core = n * n
-            nodes = (n - 1, n - 2) if ends else (0, 1)
-            for layer in (0, 1):
-                line = base + ey * core + nodes[layer] * n
-                row = base + layer * EX * core
-                out[row : row + n] += x_low[line : line + n]
-                row += EX * core - n
-                out[row : row + n] += x_high[line : line + n]
-            line = base + (EY + ey) * core + nodes[0] * n
-            for side, halo in ((0, x_low), (1, x_high)):
-                row = plane_line(n, side)
-                out[row : row + n] = halo[line : line + n]
+    x_low, x_high = received("px", x_first, x_second)
+
+    def write(up, down):
+        for out, ey, ends in ((up, EY - 1, True), (down, 0, False)):
+            for n, base in ((8, 0), (4, 512)):
+                face, inner = (n - 1, n - 2) if ends else (0, 1)
+                for kind, (layer, node) in enumerate(((0, face), (0, inner), (1, face))):
+                    line = base + (layer * EY + ey) * n * n + node * n
+                    for side, halo in ((0, x_low), (1, x_high)):
+                        row = edge_row(n, side, kind)
+                        out[row : row + n] = halo[line : line + n]
+
+    for_partners("py", first, second, write)
     summed[...] = vertex[0:VERTEX_ROWS]
     summed[0:5] += x_low[LAYER_ROWS : LAYER_ROWS + 5]
     summed[20:24] = jnp.zeros((4, LANES), F32)
 
 
-def join(x_low, x_high, y_up, y_down, vertex, after):
+def join(x_halos, vertex, after):
     vmem = pl.BlockSpec(memory_space=pltpu.VMEM)
-    halo = jax.ShapeDtypeStruct((Y_ROWS, LANES), F32)
+    edge = jax.ShapeDtypeStruct((EDGE_ROWS, LANES), F32)
     return pl.pallas_call(
         join_kernel,
-        out_shape=[halo, halo, jax.ShapeDtypeStruct((VERTEX_ROWS, LANES), F32)],
-        in_specs=[vmem] * 5 + [pl.BlockSpec(memory_space=pl.ANY)],
+        out_shape=[edge, edge, jax.ShapeDtypeStruct((VERTEX_ROWS, LANES), F32)],
+        in_specs=[vmem] * 3 + [pl.BlockSpec(memory_space=pl.ANY)],
         out_specs=[vmem] * 3,
-        compiler_params=pltpu.CompilerParams(vmem_limit_bytes=VMEM_LIMIT),
-        cost_estimate=pl.CostEstimate(flops=10**6, bytes_accessed=3 * 10**6, transcendentals=0),
+        compiler_params=pltpu.CompilerParams(vmem_limit_bytes=8 * MIB),
+        cost_estimate=pl.CostEstimate(flops=10**6, bytes_accessed=10**6, transcendentals=0),
         name="join",
-    )(x_low, x_high, y_up, y_down, vertex, after)
-
-
-def join_faces_kernel(x_low, x_high, y_up, y_down, up, down):
-    for out, source, ey, ends in ((up, y_up, EY - 1, True), (down, y_down, 0, False)):
-        out[...] = source[...]
-        for n, base in ((8, 0), (4, 256)):
-            core = n * n
-            line = base + ey * core + (core - n if ends else 0)
-            out[base : base + n] = 0.5 * (source[base : base + n] + x_low[line : line + n])
-            row = base + EX * core - n
-            out[row : row + n] = 0.5 * (source[row : row + n] + x_high[line : line + n])
-            for ex in range(EX - 1):
-                row = base + ex * core + core
-                total = 0.5 * (source[row - n : row] + source[row : row + n])
-                out[row - n : row] = total
-                out[row : row + n] = total
-
-
-def join_faces(x_low, x_high, y_up, y_down):
+    )(*x_halos, vertex, after)
+
+
+def join_faces_kernel(x_first, x_second, first, second):
+    x_low, x_high = received("px", x_first, x_second)
+
+    def write(up, down):
+        for out, ey, ends in ((up, EY - 1, True), (down, 0, False)):
+            for n, base in ((8, 0), (4, 256)):
+                core = n * n
+                line = base + ey * core + (core - n if ends else 0)
+                for side, halo in ((0, x_low), (1, x_high)):
+                    row = edge_face_row(n, side)
+                    out[row : row + n] = halo[line : line + n]
+
+    for_partners("py", first, second, write)
+
+
+def join_faces(x_halos):
     vmem = pl.BlockSpec(memory_space=pltpu.VMEM)
-    face = jax.ShapeDtypeStruct((FACE_ROWS, LANES), F32)
+    edge = jax.ShapeDtypeStruct((EDGE_FACE_ROWS, LANES), F32)
     return pl.pallas_call(
         join_faces_kernel,
-        out_shape=[face, face],
-        in_specs=[vmem] * 4,
+        out_shape=[edge, edge],
+        in_specs=[vmem] * 2,
         out_specs=[vmem] * 2,
-        compiler_params=pltpu.CompilerParams(vmem_limit_bytes=VMEM_LIMIT),
+        compiler_params=pltpu.CompilerParams(vmem_limit_bytes=8 * MIB),
         cost_estimate=pl.CostEstimate(flops=10**6, bytes_accessed=10**6, transcendentals=0),
         name="join_faces",
-    )(x_low, x_high, y_up, y_down)
+    )(*x_halos)
 
 
 def spread_kernel(source, out):
@@ -367,7 +401,7 @@
     ref[high_rows] = new_high
 
 
-def assemble(level, planes, rims, sides, x_low, x_high, y_low, y_high):
+def assemble(level, planes, rims, sides, x_low, x_high, y_low, y_high, edges):
     n, core = level.n, level.core
     last = EX * n + 3
     base = 0 if n == 8 else 512
@@ -388,14 +422,18 @@
             kind = 2 * side + layer
             start = base + layer * EX * core
             sides[kind] = halo[start : start + EX * core]
+            row = edge_row(n, 0, layer)
+            sides[kind, 0:n] += edges[side][row : row + n]
+            row = edge_row(n, 1, layer)
+            sides[kind, EX * core - n : EX * core] += edges[side][row : row + n]
     for plane in range(EX * n):
         row = plane * n
         planes[0, 2 + plane, 0:n] += sides[0, row : row + n]
         planes[EY - 1, 2 + plane, core - n : core] += sides[2, row : row + n]
     for side, plane in ((0, 0), (1, last)):
-        row = plane_line(n, side)
-        planes[0, plane, 0:n] += y_low[row : row + n]
-        planes[EY - 1, plane, core - n : core] += y_high[row : row + n]
+        row = edge_row(n, side, 2)
+        planes[0, plane, 0:n] += edges[0][row : row + n]
+        planes[EY - 1, plane, core - n : core] += edges[1][row : row + n]
     for ey in range(EY - 1):
         for plane in [0, last] + list(range(2, 2 + EX * n)):
             total = planes[ey, plane, core - n : core] + planes[ey + 1, plane, 0:n]
@@ -422,7 +460,7 @@
             )
 
 
-def build_tables(level, tables, basis, eigen, forward, backward, inverse):
+def build_tables(level, tables, basis, eigen, forward, backward, lines_out):
     first, second, pick_b, pick_c, core_b, core_c = tables
     modes, depth = level.modes, level.depth
     rows_b = exact_dot(first[0:modes], basis[1], ((1,), (1,)))
@@ -444,17 +482,15 @@
     spread_c = jnp.broadcast_to(eigen[2:3, :], (LANES, wide))
     lines = exact_dot(first[0:modes], spread_b, ((1,), (1,)))
     lines += exact_dot(second[0:modes], spread_c, ((1,), (1,)))
-    for i in range(wide):
-        inverse[i] = 1.0 / (lines + eigen[0:1, i : i + 1])
-
-
-def solve_pairs(
-    level, start, group, planes, rims, coeff, forward, backward, inverse, scale, spectrum, hats, out
-):
-    n, wide, core, modes, depth = level.n, level.wide, level.core, level.modes, level.depth
+    lines_out[...] = lines
+
+
+def first_steps(level, q, planes, rims, coeff, spectrum):
+    n, wide, core, depth = level.n, level.wide, level.core, level.depth
     offsets = [0] + [2 + a for a in range(n)] + [n + 3]
-
-    def contract(slot, load, nodes, row):
+    base, ey = q // 2 * n, q % 2 * 2
+
+    def contract(load, nodes, row):
         held = [[load(h, e) for h in (0, 1)] for e in nodes]
         for i in range(wide):
             for h in (0, 1):
@@ -463,55 +499,58 @@
                     total += coeff[nodes[position], i] * held[position][h]
                 high, low = split(total)
                 lanes = slice(h * LANES, (h + 1) * LANES)
-                spectrum[slot, i, row : row + 16, lanes] = high
-                spectrum[slot, i, depth + row : depth + row + 16, lanes] = low
-
-    for slot in range(group):
-        q = start + slot
-        base, ey = q // 2 * n, q % 2 * 2
-        for row in range(0, core, 16):
-            contract(
-                slot,
-                lambda h, e, row=row: planes[ey + h, base + offsets[e], row : row + 16],
-                list(range(wide)),
-                row,
-            )
-        for row in range(0, level.rim, 16):
-            contract(
-                slot,
-                lambda h, e, row=row: rims[ey + h, base + e - 1, row : row + 16],
-                list(range(1, n + 1)),
-                core + row,
-            )
+                spectrum[i, row : row + 16, lanes] = high
+                spectrum[i, depth + row : depth + row + 16, lanes] = low
+
+    def inner(row):
+        load = lambda h, e: planes[ey + h, base + offsets[e], row : row + 16]
+        contract(load, list(range(wide)), row)
+
+    def outer(row):
+        load = lambda h, e: rims[ey + h, base + e - 1, row : row + 16]
+        contract(load, list(range(1, n + 1)), core + row)
+
+    steps = [functools.partial(inner, row) for row in range(0, core, 16)]
+    return steps + [functools.partial(outer, row) for row in range(0, level.rim, 16)]
+
+
+def last_steps(level, q, hats, coeff, scale, out):
+    n, wide, core = level.n, level.wide, level.core
+    ex, ey = q // 2, q % 2 * 2
+
+    def back(h, row):
+        inv = 1.0 / scale[ex, pl.ds(ey + h, 1), :]
+        lanes = slice(h * LANES, (h + 1) * LANES)
+        held = [hats[i, row : row + 16, lanes] for i in range(wide)]
+        for a in range(n):
+            total = coeff[a + 1, 0] * held[0]
+            for i in range(1, wide):
+                total += coeff[a + 1, i] * held[i]
+            out[q, h, a, row : row + 16] = total * inv
+
+    return [functools.partial(back, h, row) for h in (0, 1) for row in range(0, core, 16)]
+
+
+def products(level, slots, forward, backward, inverse, lag):
+    core, modes = level.core, level.modes
     waiting = []
-    steps = [(slot, i) for slot in range(group) for i in range(wide)]
-    for step in range(len(steps) + LAG):
+    steps = [(spectrum, hats, i) for spectrum, hats in slots for i in range(level.wide)]
+    for step in range(len(steps) + lag):
         if step < len(steps):
-            slot, i = steps[step]
-            both = dot(forward[...], spectrum[slot, i])
+            spectrum, _, i = steps[step]
+            both = dot(forward[...], spectrum[i])
             damp = inverse[i]
             hat = (both[0:modes] + both[modes : 2 * modes]) * jnp.concatenate([damp, damp], axis=1)
             waiting.append(jnp.concatenate(split(hat), axis=0))
-        if step >= LAG:
-            slot, i = steps[step - LAG]
-            both = dot(backward[...], waiting[step - LAG])
-            hats[slot, i] = both[0:core] + both[core : 2 * core]
-    for slot in range(group):
-        q = start + slot
-        ex, ey = q // 2, q % 2 * 2
-        for h in (0, 1):
-            inv = 1.0 / scale[ex, pl.ds(ey + h, 1), :]
-            lanes = slice(h * LANES, (h + 1) * LANES)
-            for row in range(0, core, 16):
-                held = [hats[slot, i, row : row + 16, lanes] for i in range(wide)]
-                for a in range(n):
-                    total = coeff[a + 1, 0] * held[0]
-                    for i in range(1, wide):
-                        total += coeff[a + 1, i] * held[i]
-                    out[q, h, a, row : row + 16] = total * inv
-
-
-def tables_kernel(fine_basis, fine_eigen, middle_basis, middle_eigen, after, *refs):
+        if step >= lag:
+            _, hats, i = steps[step - lag]
+            both = dot(backward[...], waiting[step - lag])
+            hats[i] = both[0:core] + both[core : 2 * core]
+
+
+def tables_kernel(
+    fine_basis, fine_eigen, middle_basis, middle_eigen, after, *refs
+):
     del after
     fine_in, middle_in, outs = refs[:6], refs[6:12], refs[12:]
     build_tables(FINE, fine_in, fine_basis, fine_eigen, *outs[:3])
@@ -527,7 +566,7 @@
         shapes += [
             jax.ShapeDtypeStruct((2 * level.modes, 2 * level.depth), BF16),
             jax.ShapeDtypeStruct((2 * level.core, 2 * level.modes), BF16),
-            jax.ShapeDtypeStruct((level.wide, level.modes, LANES), F32),
+            jax.ShapeDtypeStruct((level.modes, LANES), F32),
         ]
     shapes += [jax.ShapeDtypeStruct((level.wide, level.wide), F32) for level in (FINE, MID)]
     return pl.pallas_call(
@@ -550,22 +589,26 @@
     scale,
     fine_coeff,
     middle_coeff,
-    x_low,
-    x_high,
-    y_low,
-    y_high,
+    x_first,
+    x_second,
+    y_first,
+    y_second,
+    edge_first,
+    edge_second,
     forward,
     backward,
-    inverse,
+    lines,
     forward_m,
     backward_m,
-    inverse_m,
+    lines_m,
+    fine_eigen,
+    middle_eigen,
     fine_out,
     middle_out,
-    x_up,
-    x_down,
-    y_up,
-    y_down,
+    face_first,
+    face_second,
+    line_first,
+    line_second,
     planes,
     rims,
     sides,
@@ -577,9 +620,14 @@
     spectrum_m,
     hats_m,
     solved,
+    inverse,
+    inverse_m,
     in_sems,
     out_sems,
 ):
+    x_low, x_high = received("px", x_first, x_second)
+    y_low, y_high = received("py", y_first, y_second)
+    edges = received("py", edge_first, edge_second)
     copies = []
     for ex in range(EX):
         for ey in range(EY):
@@ -591,59 +639,86 @@
     for ex in range(EX):
         for ey in range(EY):
             planes_m[ey, 2 + 4 * ex : 6 + 4 * ex] = middle[ex, ey]
-    assemble(MID, planes_m, rims_m, sides_m, x_low, x_high, y_low, y_high)
+    assemble(MID, planes_m, rims_m, sides_m, x_low, x_high, y_low, y_high, edges)
+
+    for level, inverse_out, lines_in, eigen in (
+        (FINE, inverse, lines, fine_eigen),
+        (MID, inverse_m, lines_m, middle_eigen),
+    ):
+        for i in range(level.wide):
+            inverse_out[i] = 1.0 / (lines_in[...] + eigen[0, i])
 
     def middle_step(step, carry):
-        solve_pairs(
-            MID, step * MID_GROUP, MID_GROUP, planes_m, rims_m, middle_coeff, forward_m, backward_m,
-            inverse_m, scale, spectrum_m, hats_m, middle_out,
-        )
+        pairs = [MID_GROUP * step + k for k in range(MID_GROUP)]
+        for k, q in enumerate(pairs):
+            for run in first_steps(MID, q, planes_m, rims_m, middle_coeff, spectrum_m.at[k]):
+                run()
+        slots = [(spectrum_m.at[k], hats_m.at[k]) for k in range(MID_GROUP)]
+        products(MID, slots, forward_m, backward_m, inverse_m, LAG)
+        for k, q in enumerate(pairs):
+            for run in last_steps(MID, q, hats_m.at[k], middle_coeff, scale, middle_out):
+                run()
         return carry
 
     lax.fori_loop(0, 8 // MID_GROUP, middle_step, 0)
     for copy in copies:
         copy.wait()
-    assemble(FINE, planes, rims, sides, x_low, x_high, y_low, y_high)
+    assemble(FINE, planes, rims, sides, x_low, x_high, y_low, y_high, edges)
 
     def fine_step(q, carry):
-        solve_pairs(
-            FINE, q, 1, planes, rims, fine_coeff, forward, backward,
-            inverse, scale, spectrum, hats, solved,
-        )
+        for run in first_steps(FINE, q, planes, rims, fine_coeff, spectrum):
+            run()
+        products(FINE, [(spectrum, hats)], forward, backward, inverse, LAG)
+        for run in last_steps(FINE, q, hats, fine_coeff, scale, solved):
+            run()
         pltpu.make_async_copy(solved.at[q], fine_out.at[q], out_sems.at[q]).start()
         return carry
 
     lax.fori_loop(0, 8, fine_step, 0)
-    for n, source, base in ((8, solved, 0), (4, middle_out, 256)):
-        core = n * n
-        for out, ex, node in ((x_up, EX - 1, n - 1), (x_down, 0, 0)):
-            for ey in range(EY):
-                row = base + ey * core
-                out[row : row + core] = source[2 * ex + ey // 2, ey % 2, node]
-        for out, ey, node in ((y_up, EY - 1, n - 1), (y_down, 0, 0)):
-            for ex in range(EX):
-                for a in range(n):
-                    row = base + (ex * n + a) * n
-                    out[row : row + n] = source[
-                        2 * ex + ey // 2, ey % 2, a, node * n : node * n + n
-                    ]
+
+    def write_x(x_up, x_down):
+        for n, source, base in ((8, solved, 0), (4, middle_out, 256)):
+            for out, ex, node in ((x_up, EX - 1, n - 1), (x_down, 0, 0)):
+                for ey in range(EY):
+                    row = base + ey * n * n
+                    out[row : row + n * n] = source[2 * ex + ey // 2, ey % 2, node]
+
+    for_partners("px", face_first, face_second, write_x)
+
+    def write_y(y_up, y_down):
+        for n, source, base in ((8, solved, 0), (4, middle_out, 256)):
+            core = n * n
+            for out, ey, node in ((y_up, EY - 1, n - 1), (y_down, 0, 0)):
+                for ex in range(EX):
+                    for a in range(n):
+                        row = base + (ex * n + a) * n
+                        out[row : row + n] = source[
+                            2 * ex + ey // 2, ey % 2, a, node * n : node * n + n
+                        ]
+                for ex in range(1, EX):
+                    row = base + ex * core
+                    total = 0.5 * (out[row - n : row] + out[row : row + n])
+                    out[row - n : row] = total
+                    out[row : row + n] = total
+
+    for_partners("py", line_first, line_second, write_y)
     for q in range(8):
         pltpu.make_async_copy(solved.at[q], fine_out.at[q], out_sems.at[q]).wait()
 
 
-def schwarz(residual, middle, scale, halos, tables):
+def schwarz(residual, middle, scale, fine_eigen, middle_eigen, halos, tables):
     vmem = pl.BlockSpec(memory_space=pltpu.VMEM)
     smem = pl.BlockSpec(memory_space=pltpu.SMEM)
     hbm = pl.BlockSpec(memory_space=pltpu.HBM)
     face = jax.ShapeDtypeStruct((FACE_ROWS, LANES), F32)
 
-    def scratch(level, group):
+    def scratch(level, *group):
         return [
             pltpu.VMEM((EY, level.planes, level.core, LANES), F32),
             pltpu.VMEM((EY, EX * level.n, level.rim, LANES), F32),
             pltpu.VMEM((4, EX * level.core, LANES), F32),
-            pltpu.VMEM((group, level.wide, 2 * level.depth, 2 * LANES), BF16),
-            pltpu.VMEM((group, level.wide, level.core, 2 * LANES), F32),
+            pltpu.VMEM(group + (level.wide, 2 * level.depth, 2 * LANES), BF16),
+            pltpu.VMEM(group + (level.wide, level.core, 2 * LANES), F32),
         ]
 
     return pl.pallas_call(
@@ -653,12 +728,14 @@
             jax.ShapeDtypeStruct((8, 2, 4, 16, LANES), F32),
         ]
         + [face] * 4,
-        in_specs=[hbm, vmem, vmem, smem, smem] + [vmem] * 10,
+        in_specs=[hbm, vmem, vmem, smem, smem] + [vmem] * 12 + [smem] * 2,
         out_specs=[hbm] + [vmem] * 5,
-        scratch_shapes=scratch(FINE, 1)
+        scratch_shapes=scratch(FINE)
         + scratch(MID, MID_GROUP)
         + [
             pltpu.VMEM((8, 2, 8, 64, LANES), F32),
+            pltpu.VMEM((FINE.wide, FINE.modes, LANES), F32),
+            pltpu.VMEM((MID.wide, MID.modes, LANES), F32),
             pltpu.SemaphoreType.DMA((16,)),
             pltpu.SemaphoreType.DMA((8,)),
         ],
@@ -667,7 +744,7 @@
             flops=10**11, bytes_accessed=12 * 10**6, transcendentals=0
         ),
         name="schwarz",
-    )(residual, middle, scale, *tables[6:], *halos, *tables[:6])
+    )(residual, middle, scale, *tables[6:], *halos, *tables[:6], fine_eigen, middle_eigen)
 
 
 def coarse_kernel(rows_x, gathered, table, out, held, part):
@@ -691,7 +768,7 @@
             held[4 * p + half + 1] = total[:, LANES : 2 * LANES]
         return carry
 
-    lax.fori_loop(0, 8, y_step, 0)
+    lax.fori_loop(0, 8, y_step, 0, unroll=4)
     angle = 2.0 * np.pi / 32
     eigen_x = line_eigen(32)
 
@@ -760,7 +837,7 @@
     )(jnp.asarray(hartley(32), F32), gathered, jnp.asarray(coarse_table()))
 
 
-def average_faces(level, field, sides, x_low, x_high, y_low, y_high):
+def average_faces(level, field, sides, x_low, x_high, y_low, y_high, edges):
     n, core = level.n, level.core
     base = 0 if n == 8 else 256
 
@@ -780,6 +857,10 @@
             field[q + 2, h, 0] = total
     for side, halo in ((0, y_low), (1, y_high)):
         sides[side] = halo[base : base + EX * core]
+        row = edge_face_row(n, 0)
+        sides[side, 0:n] = 0.5 * (sides[side, 0:n] + edges[side][row : row + n])
+        row, end = edge_face_row(n, 1), EX * core
+        sides[side, end - n : end] = 0.5 * (sides[side, end - n : end] + edges[side][row : row + n])
     for ex in range(EX):
         for a in range(n):
             row = (ex * n + a) * n
@@ -798,7 +879,7 @@
 
 
 def finish_kernel(
-    fine, middle, coarse_part, prolong, x_low, x_high, y_low, y_high,
+    fine, middle, coarse_part, prolong, x_first, x_second, y_first, y_second, edge_first, edge_second,
     out, field, sides, field_m, sides_m, corner, result, in_sems, out_sems,
 ):
     copies = []
@@ -806,8 +887,11 @@
         copy = pltpu.make_async_copy(fine.at[q], field.at[q], in_sems.at[q])
         copy.start()
         copies.append(copy)
+    x_low, x_high = received("px", x_first, x_second)
+    y_low, y_high = received("py", y_first, y_second)
+    edges = received("py", edge_first, edge_second)
     field_m[...] = middle[...]
-    average_faces(MID, field_m, sides_m, x_low, x_high, y_low, y_high)
+    average_faces(MID, field_m, sides_m, x_low, x_high, y_low, y_high, edges)
     near = coarse_part[...]
     far = pltpu.roll(near, LANES - 1, 1)
     for q in range(8):
@@ -822,7 +906,7 @@
                     corner[q, h, place + 1 : place + 2] = far[row : row + 1]
     for copy in copies:
         copy.wait()
-    average_faces(FINE, field, sides, x_low, x_high, y_low, y_high)
+    average_faces(FINE, field, sides, x_low, x_high, y_low, y_high, edges)
 
     def step(q, carry):
         for h in (0, 1):
@@ -844,7 +928,7 @@
         pltpu.make_async_copy(result.at[q], out.at[q], out_sems.at[q]).start()
         return carry
 
-    lax.fori_loop(0, 8, step, 0)
+    lax.fori_loop(0, 8, step, 0, unroll=4)
     for q in range(8):
         pltpu.make_async_copy(result.at[q], out.at[q], out_sems.at[q]).wait()
 
@@ -855,7 +939,7 @@
     return pl.pallas_call(
         finish_kernel,
         out_shape=jax.ShapeDtypeStruct((8, 2, 8, 64, LANES), F32),
-        in_specs=[hbm] + [vmem] * 7,
+        in_specs=[hbm] + [vmem] * 9,
         out_specs=hbm,
         scratch_shapes=[
             pltpu.VMEM((8, 2, 8, 64, LANES), F32),
@@ -875,28 +959,31 @@
     )(fine, middle, coarse_part, jnp.asarray(prolong_matrix()), *halos)
 
 
-def shift(values, axis, step):
+def swap(first, second, axis):
     count = lax.axis_size(axis)
-    return lax.ppermute(values, axis, [(i, (i + step) % count) for i in range(count)])
+    pairs = [(i, i + 1 - 2 * (i % 2)) for i in range(count)]
+    others = [(i, (i - 1 + 2 * (i % 2)) % count) for i in range(count)]
+    return lax.ppermute(first, axis, pairs), lax.ppermute(second, axis, others)
 
 
 def on_device(residual, scale, fine_basis, fine_eigen, middle_basis, middle_eigen):
     shape = residual.shape
+    devices = lax.axis_size("px") * lax.axis_size("py")
     residual = residual.reshape(EX, EY, 8, 64, LANES)
-    x_up, x_down, y_up, y_down, middle, vertex = pack(residual)
-    x_halos = shift(x_up, "px", 1), shift(x_down, "px", -1)
+    x_first, x_second, y_first, y_second, middle, vertex = pack(residual)
+    x_halos = swap(x_first, x_second, "px")
+    halos = x_halos + swap(y_first, y_second, "py")
     tables = solve_tables(fine_basis, fine_eigen, middle_basis, middle_eigen, vertex)
-    y_up, y_down, vertex = join(*x_halos, y_up, y_down, vertex, tables[-1])
-    halos = x_halos + (shift(y_up, "py", 1), shift(y_down, "py", -1))
-    devices = lax.axis_size("px") * lax.axis_size("py")
+    edge_first, edge_second, vertex = join(x_halos, vertex, tables[7])
+    halos += swap(edge_first, edge_second, "py")
     gathered = lax.all_to_all(spread(vertex, devices), ("px", "py"), 0, 0)
     gathered = gathered.reshape(devices * VERTEX_ROWS, LANES)
-    fine_solved, middle_solved, x_up, x_down, y_up, y_down = schwarz(
-        residual, middle, scale, halos, tables
+    fine_solved, middle_solved, x_first, x_second, y_first, y_second = schwarz(
+        residual, middle, scale, fine_eigen, middle_eigen, halos, tables
     )
-    x_halos = shift(x_up, "px", 1), shift(x_down, "px", -1)
-    y_up, y_down = join_faces(*x_halos, y_up, y_down)
-    halos = x_halos + (shift(y_up, "py", 1), shift(y_down, "py", -1))
+    x_halos = swap(x_first, x_second, "px")
+    halos = x_halos + swap(y_first, y_second, "py")
+    halos += swap(*join_faces(x_halos), "py")
     coarse_part = coarse(gathered)
     return finish(fine_solved, middle_solved, coarse_part, halos).reshape(shape)
 

time: 76.3 us -> 71.6 us (0.938)
  Pallas kernels: 42.9 us -> 37.3 us
  starting transfers between devices: 24.8 us -> 30.1 us
  waiting for transfers between devices: 4.71 us -> 0.07 us
    ppermute x8 -> x12, starting transfers between devices: 18.9 us -> 23.8 us  [the longest x6 20.6 us: swap(): lax.ppermute(second, axis, others)]
    ppermute x8 -> x12, waiting for transfers between devices: 4.71 us -> 0.07 us  [the longest x6 0.06 us: swap(): lax.ppermute(first, axis, pairs)]
    pallas_call x2, Pallas kernels: 4.03 us -> 0.03 us  [the longest x1 0.02 us: join(): pl.pallas_call(join_kernel, out_shape=[edge, edge, jax.ShapeDtypeStruct((...]
    pallas_call x1, Pallas kernels: 4.21 us -> 3.29 us  [finish(): pl.pallas_call(finish_kernel, out_shape=jax.ShapeDtypeStruct((8, 2, 8, 64...]
    pallas_call x1, Pallas kernels: 4.68 us -> 3.77 us  [coarse(): pl.pallas_call(coarse_kernel, out_shape=jax.ShapeDtypeStruct((40, LANES),...]
    unnamed x29 -> x31, local copies, waits for them, and re-layouts: 3.08 us -> 3.47 us
  transfers between devices with their start and end apart: 9 -> 13, of which waited for: 3 -> 0; matrix products, arithmetic and copies ran while one was open for 1% -> 1% of each run, Pallas kernels for 43% -> 41%
where the time goes in v3:
time: 71.6 us; the launch traced here: 71.2 us
  Pallas kernels  37.3 us (52%)
  starting transfers between devices  30.1 us (42%)
  local copies, waits for them, and re-layouts  3.47 us (5%)
    ppermute x6, starting transfers between devices, swap(): lax.ppermute(second, axis, others)  20.6 us
    pallas_call x1, Pallas kernels, schwarz(): pl.pallas_call(schwarz_kernel, out_shape=[jax.ShapeDtypeStruct((8, 2, 8,...  20.1 us
    all_to_all x1, starting transfers between devices, on_device(): gathered = lax.all_to_all(spread(vertex, devices), ('px', 'py'), 0, 0)  6.23 us
    pallas_call x1, Pallas kernels, pack(): pl.pallas_call(pack_kernel, out_shape=[x_halo] * 2 + [y_halo] * 2 + [jax....  4.52 us
    pallas_call x1, Pallas kernels, coarse(): pl.pallas_call(coarse_kernel, out_shape=jax.ShapeDtypeStruct((40, LANES),...  3.77 us
    pallas_call x1, Pallas kernels, solve_tables(): pl.pallas_call(tables_kernel, out_shape=shapes, in_specs=[vmem] * 4 + [pl...  3.65 us
    unnamed x31, local copies, waits for them, and re-layouts  3.47 us
    ppermute x6, starting transfers between devices, swap(): lax.ppermute(first, axis, pairs)  3.29 us
  transfers between devices with their start and end apart: 13, of which 0 were waited for; matrix products, arithmetic and copies ran while one was open for 1% of the time, Pallas kernels for 41%

profile of v3, /device:TPU:0, one launch (start us, length us, event | category | flops | bytes accessed | tf_op | source)
XLA Modules:
  0.0 71.2 jit_solution(9635410634634035423)
XLA Ops:
  0.0 4.5 %pack.1 = (f32[648,128]{1,0:T(8,128)}, f32[648,128]{1,0:T(8,128)}, f32[640,128]{1,0:T(8,128)}, f32[640,128]{1,0:T(8,128)}, f32[4,4,4,16,128]{4,3,2,1,0:T(8,128)}, /*index=5*/f32[32,128]{1,0:T(8,128)}) custom-call(f32[4,4,8,64,128]{4,3,2,1,0:T(8,128)} %bitcast.4, bf16[160,512]{1,0:T(8,128)(2,1)} %constant.36.clone.restrict_in, ...), custom_call_target="tpu_custom_call" | custom-call | flops 1000000000 | bytes 8000000 | tf_op jit(solution)/shard_map/pack/pallas_call | solution.py:282
  4.5 0.1 collective-permute-start
  4.6 3.0 %collective-permute-start.1 = (f32[648,128]{1,0:T(8,128)}, f32[648,128]{1,0:T(8,128)S(1)}, u32[]{:S(2)}, u32[]{:S(2)}) collective-permute-start(f32[648,128]{1,0:T(8,128)} %get-tuple-element.35), channel_id=1, source_target_pairs={{0,112},{16,32},{32,16},{48,64},{64,48},{80,96},{96,80},{112,0},{1... | collective-permute-start | bytes 995336 | tf_op jit(solution)/shard_map/ppermute | solution.py:966
  7.6 1.6 %collective-permute-start.2 = (f32[640,128]{1,0:T(8,128)}, f32[640,128]{1,0:T(8,128)S(1)}, u32[]{:S(2)}, u32[]{:S(2)}) collective-permute-start(f32[640,128]{1,0:T(8,128)} %get-tuple-element.36), channel_id=1, source_target_pairs={{0,1},{1,0},{2,3},{3,2},{4,5},{5,4},{6,7},{7,6},{8,9},{9,8},{10,11... | collective-permute-start | bytes 983048 | tf_op jit(solution)/shard_map/ppermute | solution.py:966
  9.1 5.7 %collective-permute-start.3 = (f32[640,128]{1,0:T(8,128)}, f32[640,128]{1,0:T(8,128)S(1)}, u32[]{:S(2)}, u32[]{:S(2)}) collective-permute-start(f32[640,128]{1,0:T(8,128)} %get-tuple-element.37), channel_id=1, source_target_pairs={{0,15},{1,2},{2,1},{3,4},{4,3},{5,6},{6,5},{7,8},{8,7},{9,10},{10,... | collective-permute-start | bytes 983048 | tf_op jit(solution)/shard_map/ppermute | solution.py:966
  14.8 0.6 copy.25.fine_basis
  15.4 3.6 %tables.1 = (bf16[224,192]{1,0:T(8,128)(2,1)}, bf16[128,224]{1,0:T(8,128)(2,1)}, f32[112,128]{1,0:T(8,128)}, bf16[96,64]{1,0:T(8,128)(2,1)}, bf16[32,96]{1,0:T(8...) custom-call(f32[3,10,10]{2,1,0:T(8,128)} %copy.25.fine_basis, f32[3,10]{1,0:T(4,128)} %fine_eigen.3, ...), custom_call_target="tpu_custom_call" | custom-call | flops 100000000 | bytes 1000000 | tf_op jit(solution)/shard_map/tables/pallas_call | solution.py:572
  19.1 0.7 %copy-done.5 = f32[32,128]{1,0:T(8,128)S(1)} copy-done((f32[32,128]{1,0:T(8,128)S(1)}, f32[32,128]{1,0:T(8,128)}, u32[]{:S(2)}) %copy-start.5) | copy-done | bytes 16408
  19.9 0.7 copy-done.7
  20.6 0.6 copy-done.6
  21.2 1.3 %collective-permute-start.5 = (f32[72,128]{1,0:T(8,128)S(1)}, f32[72,128]{1,0:T(8,128)S(1)}, u32[]{:S(2)}, u32[]{:S(2)}) collective-permute-start(f32[72,128]{1,0:T(8,128)S(1)} %get-tuple-element.39), channel_id=1, source_target_pairs={{0,15},{1,2},{2,1},{3,4},{4,3},{5,6},{6,5},{7,8},{8,7},{9,10},{10,... | collective-permute-start | bytes 110600 | tf_op jit(solution)/shard_map/ppermute | solution.py:966
  22.5 2.0 %spread.1 = f32[128,24,128]{2,1,0:T(8,128)} custom-call(f32[24,128]{1,0:T(8,128)} %copy-done.6), custom_call_target="tpu_custom_call" | custom-call | flops 1000000 | bytes 2000000 | tf_op jit(solution)/shard_map/spread/pallas_call | solution.py:380
  24.4 6.2 %all-to-all-start = ((f32[128,24,128]{2,1,0:T(8,128)}), f32[128,24,128]{2,1,0:T(8,128)S(1)}, u32[]{:S(2)}, u32[]{:S(2)}) async-start(f32[128,24,128]{2,1,0:T(8,128)} %spread.1), calls=%async_computation | async-start | bytes 3145728 | tf_op jit(solution)/shard_map/all_to_all | solution.py:979
  30.8 0.7 copy-done.11
  31.4 0.1 copy-done.12
  31.6 20.1 %schwarz.1 = (f32[8,2,8,64,128]{4,3,2,1,0:T(8,128)}, f32[8,2,4,16,128]{4,3,2,1,0:T(8,128)}, f32[320,128]{1,0:T(8,128)}, f32[320,128]{1,0:T(8,128)}, f32[320,128]{1,0:T(8,128)}, /*index=5*/f32[320,128]{1,0:T(8,128)}) custom-call(f32[4,4,8,64,128]{4,3,2,1,0:T(8,128)} %bitcast.5, f32[4,4,4,16,128]{4,3,2,1,0:T(8,128)} %get-tuple-element.30.middle, ...), custom_call_target="tpu_custom_call" | custom-call | flops 99999997952 | bytes 12000000 | tf_op jit(solution)/shard_map/schwarz/pallas_call | solution.py:724
  51.7 0.1 collective-permute-start.6
  51.8 2.3 %collective-permute-start.7 = (f32[320,128]{1,0:T(8,128)}, f32[320,128]{1,0:T(8,128)S(1)}, u32[]{:S(2)}, u32[]{:S(2)}) collective-permute-start(f32[320,128]{1,0:T(8,128)} %get-tuple-element.50), channel_id=1, source_target_pairs={{0,112},{16,32},{32,16},{48,64},{64,48},{80,96},{96,80},{112,0},{1... | collective-permute-start | bytes 491528 | tf_op jit(solution)/shard_map/ppermute | solution.py:966
  54.1 1.5 %collective-permute-start.8 = (f32[320,128]{1,0:T(8,128)}, f32[320,128]{1,0:T(8,128)S(1)}, u32[]{:S(2)}, u32[]{:S(2)}) collective-permute-start(f32[320,128]{1,0:T(8,128)} %get-tuple-element.51), channel_id=1, source_target_pairs={{0,1},{1,0},{2,3},{3,2},{4,5},{5,4},{6,7},{7,6},{8,9},{9,8},{10,11... | collective-permute-start | bytes 491528 | tf_op jit(solution)/shard_map/ppermute | solution.py:966
  55.5 5.0 %collective-permute-start.9 = (f32[320,128]{1,0:T(8,128)}, f32[320,128]{1,0:T(8,128)S(1)}, u32[]{:S(2)}, u32[]{:S(2)}) collective-permute-start(f32[320,128]{1,0:T(8,128)} %get-tuple-element.52), channel_id=1, source_target_pairs={{0,15},{1,2},{2,1},{3,4},{4,3},{5,6},{6,5},{7,8},{8,7},{9,10},{10,... | collective-permute-start | bytes 491528 | tf_op jit(solution)/shard_map/ppermute | solution.py:966
  60.6 0.1 collective-permute-start.10
  60.7 3.4 %collective-permute-start.11 = (f32[24,128]{1,0:T(8,128)S(1)}, f32[24,128]{1,0:T(8,128)S(1)}, u32[]{:S(2)}, u32[]{:S(2)}) collective-permute-start(f32[24,128]{1,0:T(8,128)S(1)} %get-tuple-element.54), channel_id=1, source_target_pairs={{0,15},{1,2},{2,1},{3,4},{4,3},{5,6},{6,5},{7,8},{8,7},{9,10},{10,... | collective-permute-start | bytes 36872 | tf_op jit(solution)/shard_map/ppermute | solution.py:966
  64.0 3.8 %coarse.1.coarse_part = f32[40,128]{1,0:T(8,128)S(1)} custom-call(f32[32,32]{1,0:T(8,128)S(1)} %copy-done.9, f32[3072,128]{1,0:T(8,128)S(1)} %bitcast.3, f32[384,128]{1,0:T(8,128)S(1)} %copy-done.8), custom_call_target="tpu_custom_call" | custom-call | flops 2000000000 | bytes 4000000 | tf_op jit(solution)/shard_map/coarse/pallas_call | solution.py:823
  67.9 3.3 %finish.1 = f32[8,2,8,64,128]{4,3,2,1,0:T(8,128)} custom-call(f32[8,2,8,64,128]{4,3,2,1,0:T(8,128)S(1)} %copy-done, f32[8,2,4,16,128]{4,3,2,1,0:T(8,128)S(1)} %copy-done.1, f32[40,128]{1,0:T(8,128)S(1)} %coarse.1.coarse_part, bf16[512,240]{1,0:T(8,128)(2,1)S(1)} %copy-done.4, f32[320,128]{1,0:T(8,128)S(1)} %collective-permute-done.6.x_first, ...), custom_call_target="tpu_custom_call" | custom-call | flops 2000000000 | bytes 8000000 | tf_op jit(solution)/shard_map/finish/pallas_call | solution.py:939
  (41 shorter events, 0.2 us)
Async XLA Ops:
  0.0 14.8 %copy-start.10 = (f32[3,10,10]{2,0,1:T(4,128)S(1)}, f32[3,10,10]{2,0,1:T(4,128)}, u32[]{:S(2)}) copy-start(f32[3,10,10]{2,0,1:T(4,128)} %param.26) | copy-start | bytes 3604
  4.5 14.6 %collective-permute-start = (f32[648,128]{1,0:T(8,128)}, f32[648,128]{1,0:T(8,128)S(1)}, u32[]{:S(2)}, u32[]{:S(2)}) collective-permute-start(f32[648,128]{1,0:T(8,128)} %get-tuple-element.34), channel_id=1, source_target_pairs={{0,16},{16,0},{32,48},{48,32},{64,80},{80,64},{96,112},{112,96},{1... | collective-permute-start | bytes 995336 | tf_op jit(solution)/shard_map/ppermute | solution.py:966
  4.6 14.5 %collective-permute-start.1 = (f32[648,128]{1,0:T(8,128)}, f32[648,128]{1,0:T(8,128)S(1)}, u32[]{:S(2)}, u32[]{:S(2)}) collective-permute-start(f32[648,128]{1,0:T(8,128)} %get-tuple-element.35), channel_id=1, source_target_pairs={{0,112},{16,32},{32,16},{48,64},{64,48},{80,96},{96,80},{112,0},{1... | collective-permute-start | bytes 995336 | tf_op jit(solution)/shard_map/ppermute | solution.py:966
  7.6 23.1 %collective-permute-start.2 = (f32[640,128]{1,0:T(8,128)}, f32[640,128]{1,0:T(8,128)S(1)}, u32[]{:S(2)}, u32[]{:S(2)}) collective-permute-start(f32[640,128]{1,0:T(8,128)} %get-tuple-element.36), channel_id=1, source_target_pairs={{0,1},{1,0},{2,3},{3,2},{4,5},{5,4},{6,7},{7,6},{8,9},{9,8},{10,11... | collective-permute-start | bytes 983048 | tf_op jit(solution)/shard_map/ppermute | solution.py:966
  9.1 21.6 %collective-permute-start.3 = (f32[640,128]{1,0:T(8,128)}, f32[640,128]{1,0:T(8,128)S(1)}, u32[]{:S(2)}, u32[]{:S(2)}) collective-permute-start(f32[640,128]{1,0:T(8,128)} %get-tuple-element.37), channel_id=1, source_target_pairs={{0,15},{1,2},{2,1},{3,4},{4,3},{5,6},{6,5},{7,8},{8,7},{9,10},{10,... | collective-permute-start | bytes 983048 | tf_op jit(solution)/shard_map/ppermute | solution.py:966
  19.1 11.7 %copy-start.2 = (f32[648,128]{1,0:T(8,128)}, f32[648,128]{1,0:T(8,128)S(1)}, u32[]{:S(2)}) copy-start(f32[648,128]{1,0:T(8,128)S(1)} %collective-permute-done.x_first) | copy-start | bytes 995332
  19.1 11.7 %copy-start.3 = (f32[648,128]{1,0:T(8,128)}, f32[648,128]{1,0:T(8,128)S(1)}, u32[]{:S(2)}) copy-start(f32[648,128]{1,0:T(8,128)S(1)} %collective-permute-done.1.x_second) | copy-start | bytes 995332
  21.2 9.5 %collective-permute-start.4 = (f32[72,128]{1,0:T(8,128)S(1)}, f32[72,128]{1,0:T(8,128)S(1)}, u32[]{:S(2)}, u32[]{:S(2)}) collective-permute-start(f32[72,128]{1,0:T(8,128)S(1)} %get-tuple-element.38), channel_id=1, source_target_pairs={{0,1},{1,0},{2,3},{3,2},{4,5},{5,4},{6,7},{7,6},{8,9},{9,8},{10,11... | collective-permute-start | bytes 110600 | tf_op jit(solution)/shard_map/ppermute | solution.py:966
  21.2 9.6 %collective-permute-start.5 = (f32[72,128]{1,0:T(8,128)S(1)}, f32[72,128]{1,0:T(8,128)S(1)}, u32[]{:S(2)}, u32[]{:S(2)}) collective-permute-start(f32[72,128]{1,0:T(8,128)S(1)} %get-tuple-element.39), channel_id=1, source_target_pairs={{0,15},{1,2},{2,1},{3,4},{4,3},{5,6},{6,5},{7,8},{8,7},{9,10},{10,... | collective-permute-start | bytes 110600 | tf_op jit(solution)/shard_map/ppermute | solution.py:966
  24.4 39.6 %all-to-all-start = ((f32[128,24,128]{2,1,0:T(8,128)}), f32[128,24,128]{2,1,0:T(8,128)S(1)}, u32[]{:S(2)}, u32[]{:S(2)}) async-start(f32[128,24,128]{2,1,0:T(8,128)} %spread.1), calls=%async_computation | async-start | bytes 3145728 | tf_op jit(solution)/shard_map/all_to_all | solution.py:979
  30.7 0.8 %copy-start.12 = (f32[640,128]{1,0:T(8,128)}, f32[640,128]{1,0:T(8,128)S(1)}, u32[]{:S(2)}) copy-start(f32[640,128]{1,0:T(8,128)S(1)} %collective-permute-done.3.y_second) | copy-start | bytes 983044
  30.7 0.8 %copy-start.13 = (f32[72,128]{1,0:T(8,128)}, f32[72,128]{1,0:T(8,128)S(1)}, u32[]{:S(2)}) copy-start(f32[72,128]{1,0:T(8,128)S(1)} %collective-permute-done.4.edge_first) | copy-start | bytes 110596
  30.8 0.8 %copy-start.14 = (f32[72,128]{1,0:T(8,128)}, f32[72,128]{1,0:T(8,128)S(1)}, u32[]{:S(2)}) copy-start(f32[72,128]{1,0:T(8,128)S(1)} %collective-permute-done.5.edge_second) | copy-start | bytes 110596
  31.6 32.5 %copy-start.8 = (f32[384,128]{1,0:T(8,128)S(1)}, f32[384,128]{1,0:T(8,128)}, u32[]{:S(2)}) copy-start(f32[384,128]{1,0:T(8,128)} %constant.52.clone.table) | copy-start | bytes 589828
  31.6 32.5 %copy-start.9 = (f32[32,32]{1,0:T(8,128)S(1)}, f32[32,32]{1,0:T(8,128)}, u32[]{:S(2)}) copy-start(f32[32,32]{1,0:T(8,128)} %constant.51.clone.rows_x) | copy-start | bytes 12292
  51.7 16.2 %copy-start.1 = (f32[8,2,4,16,128]{4,3,2,1,0:T(8,128)S(1)}, f32[8,2,4,16,128]{4,3,2,1,0:T(8,128)}, u32[]{:S(2)}) copy-start(f32[8,2,4,16,128]{4,3,2,1,0:T(8,128)} %get-tuple-element.47.middle) | copy-start | bytes 1572868
  51.7 16.2 %copy-start.4 = (bf16[512,240]{1,0:T(8,128)(2,1)S(1)}, bf16[512,240]{1,0:T(8,128)(2,1)}, u32[]{:S(2)}) copy-start(bf16[512,240]{1,0:T(8,128)(2,1)} %constant.53.clone.prolong) | copy-start | bytes 737284
  51.7 8.9 %collective-permute-start.6 = (f32[320,128]{1,0:T(8,128)}, f32[320,128]{1,0:T(8,128)S(1)}, u32[]{:S(2)}, u32[]{:S(2)}) collective-permute-start(f32[320,128]{1,0:T(8,128)} %get-tuple-element.49), channel_id=1, source_target_pairs={{0,16},{16,0},{32,48},{48,32},{64,80},{80,64},{96,112},{112,96},{1... | collective-permute-start | bytes 491528 | tf_op jit(solution)/shard_map/ppermute | solution.py:966
  51.8 8.8 %collective-permute-start.7 = (f32[320,128]{1,0:T(8,128)}, f32[320,128]{1,0:T(8,128)S(1)}, u32[]{:S(2)}, u32[]{:S(2)}) collective-permute-start(f32[320,128]{1,0:T(8,128)} %get-tuple-element.50), channel_id=1, source_target_pairs={{0,112},{16,32},{32,16},{48,64},{64,48},{80,96},{96,80},{112,0},{1... | collective-permute-start | bytes 491528 | tf_op jit(solution)/shard_map/ppermute | solution.py:966
  54.1 13.8 %collective-permute-start.8 = (f32[320,128]{1,0:T(8,128)}, f32[320,128]{1,0:T(8,128)S(1)}, u32[]{:S(2)}, u32[]{:S(2)}) collective-permute-start(f32[320,128]{1,0:T(8,128)} %get-tuple-element.51), channel_id=1, source_target_pairs={{0,1},{1,0},{2,3},{3,2},{4,5},{5,4},{6,7},{7,6},{8,9},{9,8},{10,11... | collective-permute-start | bytes 491528 | tf_op jit(solution)/shard_map/ppermute | solution.py:966
  55.5 12.3 %collective-permute-start.9 = (f32[320,128]{1,0:T(8,128)}, f32[320,128]{1,0:T(8,128)S(1)}, u32[]{:S(2)}, u32[]{:S(2)}) collective-permute-start(f32[320,128]{1,0:T(8,128)} %get-tuple-element.52), channel_id=1, source_target_pairs={{0,15},{1,2},{2,1},{3,4},{4,3},{5,6},{6,5},{7,8},{8,7},{9,10},{10,... | collective-permute-start | bytes 491528 | tf_op jit(solution)/shard_map/ppermute | solution.py:966
  60.6 7.3 %collective-permute-start.10 = (f32[24,128]{1,0:T(8,128)S(1)}, f32[24,128]{1,0:T(8,128)S(1)}, u32[]{:S(2)}, u32[]{:S(2)}) collective-permute-start(f32[24,128]{1,0:T(8,128)S(1)} %get-tuple-element.53), channel_id=1, source_target_pairs={{0,1},{1,0},{2,3},{3,2},{4,5},{5,4},{6,7},{7,6},{8,9},{9,8},{10,11... | collective-permute-start | bytes 36872 | tf_op jit(solution)/shard_map/ppermute | solution.py:966
  60.7 7.2 %collective-permute-start.11 = (f32[24,128]{1,0:T(8,128)S(1)}, f32[24,128]{1,0:T(8,128)S(1)}, u32[]{:S(2)}, u32[]{:S(2)}) collective-permute-start(f32[24,128]{1,0:T(8,128)S(1)} %get-tuple-element.54), channel_id=1, source_target_pairs={{0,15},{1,2},{2,1},{3,4},{4,3},{5,6},{6,5},{7,8},{8,7},{9,10},{10,... | collective-permute-start | bytes 36872 | tf_op jit(solution)/shard_map/ppermute | solution.py:966
  64.0 3.9 %copy-start = (f32[8,2,8,64,128]{4,3,2,1,0:T(8,128)S(1)}, f32[8,2,8,64,128]{4,3,2,1,0:T(8,128)}, u32[]{:S(2)}) copy-start(f32[8,2,8,64,128]{4,3,2,1,0:T(8,128)} %get-tuple-element.46.fine) | copy-start | bytes 12582916
  (4 other events, 2.8 us)

commit v4 on v3

--- a/solution.py
+++ b/solution.py
@@ -323,17 +323,20 @@
                         out[row : row + n] = halo[line : line + n]
 
     for_partners("py", first, second, write)
-    summed[...] = vertex[0:VERTEX_ROWS]
-    summed[0:5] += x_low[LAYER_ROWS : LAYER_ROWS + 5]
-    summed[20:24] = jnp.zeros((4, LANES), F32)
-
-
-def join(x_halos, vertex, after):
+    total = vertex[0:8] + jnp.concatenate(
+        [x_low[LAYER_ROWS : LAYER_ROWS + 5], jnp.zeros((3, LANES), F32)], axis=0
+    )
+    last = jnp.concatenate([vertex[16:20], jnp.zeros((4, LANES), F32)], axis=0)
+    total = jnp.concatenate([total, vertex[8:16], last], axis=0)
+    summed[...] = jnp.broadcast_to(total[None], summed.shape)
+
+
+def join(x_halos, vertex, after, devices):
     vmem = pl.BlockSpec(memory_space=pltpu.VMEM)
     edge = jax.ShapeDtypeStruct((EDGE_ROWS, LANES), F32)
     return pl.pallas_call(
         join_kernel,
-        out_shape=[edge, edge, jax.ShapeDtypeStruct((VERTEX_ROWS, LANES), F32)],
+        out_shape=[edge, edge, jax.ShapeDtypeStruct((devices, VERTEX_ROWS, LANES), F32)],
         in_specs=[vmem] * 3 + [pl.BlockSpec(memory_space=pl.ANY)],
         out_specs=[vmem] * 3,
         compiler_params=pltpu.CompilerParams(vmem_limit_bytes=8 * MIB),
@@ -369,23 +372,6 @@
         cost_estimate=pl.CostEstimate(flops=10**6, bytes_accessed=10**6, transcendentals=0),
         name="join_faces",
     )(*x_halos)
-
-
-def spread_kernel(source, out):
-    out[...] = jnp.broadcast_to(source[...][None], out.shape)
-
-
-def spread(values, count):
-    vmem = pl.BlockSpec(memory_space=pltpu.VMEM)
-    return pl.pallas_call(
-        spread_kernel,
-        out_shape=jax.ShapeDtypeStruct((count,) + values.shape, F32),
-        in_specs=[vmem],
-        out_specs=vmem,
-        compiler_params=pltpu.CompilerParams(vmem_limit_bytes=VMEM_LIMIT),
-        cost_estimate=pl.CostEstimate(flops=10**6, bytes_accessed=2 * 10**6, transcendentals=0),
-        name="spread",
-    )(values)
 
 
 def sum_lines(ref, lead, n, scale=None):
@@ -779,22 +765,33 @@
         odd = [None] + [values[x] - values[32 - x] for x in range(1, 16)]
         base = table[pl.ds(pl.multiple_of(64 + chunk * 8, 8), 8), :]
         totals = [None] * 5
-        for k in range(17):
-            cosine = even[0]
-            for x in range(1, 17):
-                cosine = cosine + float(np.cos(angle * (k * x % 32))) * even[x]
+
+        def series(wave, terms, k, start):
+            total = None
+            for x in range(start, len(terms), 2):
+                value = float(wave(angle * (k * x % 32))) * terms[x]
+                total = value if total is None else total + value
+            return total
+
+        def add(k, cosine, sine):
+            damp = 1.0 / (base + float(24.0 * eigen_x[k]))
             modes = [(k, cosine)]
-            if 0 < k < 16:
-                sine = float(np.sin(angle * k)) * odd[1]
-                for x in range(2, 16):
-                    sine = sine + float(np.sin(angle * (k * x % 32))) * odd[x]
+            if sine is not None:
                 modes = [(k, cosine + sine), (32 - k, cosine - sine)]
-            damp = 1.0 / (base + float(24.0 * eigen_x[k]))
             for kx, value in modes:
                 value = value * damp
                 for lx in range(5):
                     term = rows_x[lax.rem(own_x * 4 + lx, 32), kx] * value
                     totals[lx] = term if totals[lx] is None else totals[lx] + term
+
+        for k in range(9):
+            cos_a, cos_b = series(np.cos, even, k, 0), series(np.cos, even, k, 1)
+            sin_a = sin_b = None
+            if k > 0:
+                sin_a, sin_b = series(np.sin, odd, k, 2), series(np.sin, odd, k, 1)
+            add(k, cos_a + cos_b, None if k == 0 else sin_a + sin_b)
+            if k < 8:
+                add(16 - k, cos_a - cos_b, None if k == 0 else sin_b - sin_a)
         for lx in range(5):
             part[lx, rows, :] = totals[lx]
         return carry
@@ -974,9 +971,9 @@
     x_halos = swap(x_first, x_second, "px")
     halos = x_halos + swap(y_first, y_second, "py")
     tables = solve_tables(fine_basis, fine_eigen, middle_basis, middle_eigen, vertex)
-    edge_first, edge_second, vertex = join(x_halos, vertex, tables[7])
+    edge_first, edge_second, vertex = join(x_halos, vertex, tables[7], devices)
     halos += swap(edge_first, edge_second, "py")
-    gathered = lax.all_to_all(spread(vertex, devices), ("px", "py"), 0, 0)
+    gathered = lax.all_to_all(vertex, ("px", "py"), 0, 0)
     gathered = gathered.reshape(devices * VERTEX_ROWS, LANES)
     fine_solved, middle_solved, x_first, x_second, y_first, y_second = schwarz(
         residual, middle, scale, fine_eigen, middle_eigen, halos, tables

time: 71.6 us -> 70 us (0.978)
  Pallas kernels: 37.3 us -> 36.2 us
    pallas_call x1 -> x0, Pallas kernels: 1.99 us -> none  [spread(): pl.pallas_call(spread_kernel, out_shape=jax.ShapeDtypeStruct((count,) + v...]
    pallas_call x1, Pallas kernels: 0.02 us -> 1.3 us  [join(): pl.pallas_call(join_kernel, out_shape=[edge, edge, jax.ShapeDtypeStruct((...]
    unnamed x31 -> x29, local copies, waits for them, and re-layouts: 3.47 us -> 2.86 us
  transfers between devices with their start and end apart: 13 -> 13, of which waited for: 0 -> 1; matrix products, arithmetic and copies ran while one was open for 1% -> 1% of each run, Pallas kernels for 41% -> 41%
where the time goes in v4:
time: 70 us; the launch traced here: 69.7 us
  Pallas kernels  36.2 us (52%)
  starting transfers between devices  30.1 us (43%)
  local copies, waits for them, and re-layouts  2.86 us (4%)
    ppermute x6, starting transfers between devices, swap(): lax.ppermute(second, axis, others)  20.6 us
    pallas_call x1, Pallas kernels, schwarz(): pl.pallas_call(schwarz_kernel, out_shape=[jax.ShapeDtypeStruct((8, 2, 8,...  20.1 us
    all_to_all x1, starting transfers between devices, on_device(): gathered = lax.all_to_all(vertex, ('px', 'py'), 0, 0)  6.23 us
    pallas_call x1, Pallas kernels, pack(): pl.pallas_call(pack_kernel, out_shape=[x_halo] * 2 + [y_halo] * 2 + [jax....  4.52 us
    pallas_call x1, Pallas kernels, solve_tables(): pl.pallas_call(tables_kernel, out_shape=shapes, in_specs=[vmem] * 4 + [pl...  3.61 us
    pallas_call x1, Pallas kernels, coarse(): pl.pallas_call(coarse_kernel, out_shape=jax.ShapeDtypeStruct((40, LANES),...  3.36 us
    ppermute x6, starting transfers between devices, swap(): lax.ppermute(first, axis, pairs)  3.28 us
    pallas_call x1, Pallas kernels, finish(): pl.pallas_call(finish_kernel, out_shape=jax.ShapeDtypeStruct((8, 2, 8, 64...  3.27 us
  transfers between devices with their start and end apart: 13, of which 1 were waited for; matrix products, arithmetic and copies ran while one was open for 1% of the time, Pallas kernels for 41%

profile of v4, /device:TPU:0, one launch (start us, length us, event | category | flops | bytes accessed | tf_op | source)
XLA Modules:
  0.0 69.7 jit_solution(12108086957610693672)
XLA Ops:
  0.0 4.5 %pack.1 = (f32[648,128]{1,0:T(8,128)}, f32[648,128]{1,0:T(8,128)}, f32[640,128]{1,0:T(8,128)}, f32[640,128]{1,0:T(8,128)}, f32[4,4,4,16,128]{4,3,2,1,0:T(8,128)}, /*index=5*/f32[32,128]{1,0:T(8,128)}) custom-call(f32[4,4,8,64,128]{4,3,2,1,0:T(8,128)} %bitcast.4, bf16[160,512]{1,0:T(8,128)(2,1)} %constant.36.clone.restrict_in, ...), custom_call_target="tpu_custom_call" | custom-call | flops 1000000000 | bytes 8000000 | tf_op jit(solution)/shard_map/pack/pallas_call | solution.py:282
  4.5 0.1 collective-permute-start
  4.6 3.0 %collective-permute-start.1 = (f32[648,128]{1,0:T(8,128)}, f32[648,128]{1,0:T(8,128)S(1)}, u32[]{:S(2)}, u32[]{:S(2)}) collective-permute-start(f32[648,128]{1,0:T(8,128)} %get-tuple-element.35), channel_id=1, source_target_pairs={{0,112},{16,32},{32,16},{48,64},{64,48},{80,96},{96,80},{112,0},{1... | collective-permute-start | bytes 995336 | tf_op jit(solution)/shard_map/ppermute | solution.py:963
  7.6 1.6 %collective-permute-start.2 = (f32[640,128]{1,0:T(8,128)}, f32[640,128]{1,0:T(8,128)S(1)}, u32[]{:S(2)}, u32[]{:S(2)}) collective-permute-start(f32[640,128]{1,0:T(8,128)} %get-tuple-element.36), channel_id=1, source_target_pairs={{0,1},{1,0},{2,3},{3,2},{4,5},{5,4},{6,7},{7,6},{8,9},{9,8},{10,11... | collective-permute-start | bytes 983048 | tf_op jit(solution)/shard_map/ppermute | solution.py:963
  9.2 5.7 %collective-permute-start.3 = (f32[640,128]{1,0:T(8,128)}, f32[640,128]{1,0:T(8,128)S(1)}, u32[]{:S(2)}, u32[]{:S(2)}) collective-permute-start(f32[640,128]{1,0:T(8,128)} %get-tuple-element.37), channel_id=1, source_target_pairs={{0,15},{1,2},{2,1},{3,4},{4,3},{5,6},{6,5},{7,8},{8,7},{9,10},{10,... | collective-permute-start | bytes 983048 | tf_op jit(solution)/shard_map/ppermute | solution.py:963
  14.8 0.6 copy.25.fine_basis
  15.4 3.6 %tables.1 = (bf16[224,192]{1,0:T(8,128)(2,1)}, bf16[128,224]{1,0:T(8,128)(2,1)}, f32[112,128]{1,0:T(8,128)}, bf16[96,64]{1,0:T(8,128)(2,1)}, bf16[32,96]{1,0:T(8...) custom-call(f32[3,10,10]{2,1,0:T(8,128)} %copy.25.fine_basis, f32[3,10]{1,0:T(4,128)} %fine_eigen.3, ...), custom_call_target="tpu_custom_call" | custom-call | flops 100000000 | bytes 1000000 | tf_op jit(solution)/shard_map/tables/pallas_call | solution.py:558
  19.1 0.7 %copy-done.5 = f32[32,128]{1,0:T(8,128)S(1)} copy-done((f32[32,128]{1,0:T(8,128)S(1)}, f32[32,128]{1,0:T(8,128)}, u32[]{:S(2)}) %copy-start.5) | copy-done | bytes 16408
  19.8 0.7 copy-done.6
  20.5 1.3 %join.1 = (f32[72,128]{1,0:T(8,128)S(1)}, f32[72,128]{1,0:T(8,128)S(1)}, f32[128,24,128]{2,1,0:T(8,128)}) custom-call(f32[648,128]{1,0:T(8,128)S(1)} %collective-permute-done.x_first, f32[648,128]{1,0:T(8,128)S(1)} %collective-permute-done.1.x_second, f32[32,128]{1,0:T(8,128)S(1)} %copy-done.5, f32[6,6]{1,0:T(8,128)S(1)} %copy-done.6), custom_call_target="tpu_custom_call" | custom-call | flops 1000000 | bytes 1000000 | tf_op jit(solution)/shard_map/join/pallas_call | solution.py:337
  21.8 1.3 %collective-permute-start.5 = (f32[72,128]{1,0:T(8,128)S(1)}, f32[72,128]{1,0:T(8,128)S(1)}, u32[]{:S(2)}, u32[]{:S(2)}) collective-permute-start(f32[72,128]{1,0:T(8,128)S(1)} %get-tuple-element.39), channel_id=1, source_target_pairs={{0,15},{1,2},{2,1},{3,4},{4,3},{5,6},{6,5},{7,8},{8,7},{9,10},{10,... | collective-permute-start | bytes 110600 | tf_op jit(solution)/shard_map/ppermute | solution.py:963
  23.1 6.2 %all-to-all-start = ((f32[128,24,128]{2,1,0:T(8,128)}), f32[128,24,128]{2,1,0:T(8,128)S(1)}, u32[]{:S(2)}, u32[]{:S(2)}) async-start(f32[128,24,128]{2,1,0:T(8,128)} %get-tuple-element.48), calls=%async_computation | async-start | bytes 3145728 | tf_op jit(solution)/shard_map/all_to_all | solution.py:976
  29.4 0.7 copy-done.10
  30.1 0.1 copy-done.11
  30.2 20.1 %schwarz.1 = (f32[8,2,8,64,128]{4,3,2,1,0:T(8,128)}, f32[8,2,4,16,128]{4,3,2,1,0:T(8,128)}, f32[320,128]{1,0:T(8,128)}, f32[320,128]{1,0:T(8,128)}, f32[320,128]{1,0:T(8,128)}, /*index=5*/f32[320,128]{1,0:T(8,128)}) custom-call(f32[4,4,8,64,128]{4,3,2,1,0:T(8,128)} %bitcast.5, f32[4,4,4,16,128]{4,3,2,1,0:T(8,128)} %get-tuple-element.30.middle, ...), custom_call_target="tpu_custom_call" | custom-call | flops 99999997952 | bytes 12000000 | tf_op jit(solution)/shard_map/schwarz/pallas_call | solution.py:710
  50.4 0.1 collective-permute-start.6
  50.4 2.3 %collective-permute-start.7 = (f32[320,128]{1,0:T(8,128)}, f32[320,128]{1,0:T(8,128)S(1)}, u32[]{:S(2)}, u32[]{:S(2)}) collective-permute-start(f32[320,128]{1,0:T(8,128)} %get-tuple-element.50), channel_id=1, source_target_pairs={{0,112},{16,32},{32,16},{48,64},{64,48},{80,96},{96,80},{112,0},{1... | collective-permute-start | bytes 491528 | tf_op jit(solution)/shard_map/ppermute | solution.py:963
  52.7 1.5 %collective-permute-start.8 = (f32[320,128]{1,0:T(8,128)}, f32[320,128]{1,0:T(8,128)S(1)}, u32[]{:S(2)}, u32[]{:S(2)}) collective-permute-start(f32[320,128]{1,0:T(8,128)} %get-tuple-element.51), channel_id=1, source_target_pairs={{0,1},{1,0},{2,3},{3,2},{4,5},{5,4},{6,7},{7,6},{8,9},{9,8},{10,11... | collective-permute-start | bytes 491528 | tf_op jit(solution)/shard_map/ppermute | solution.py:963
  54.2 5.0 %collective-permute-start.9 = (f32[320,128]{1,0:T(8,128)}, f32[320,128]{1,0:T(8,128)S(1)}, u32[]{:S(2)}, u32[]{:S(2)}) collective-permute-start(f32[320,128]{1,0:T(8,128)} %get-tuple-element.52), channel_id=1, source_target_pairs={{0,15},{1,2},{2,1},{3,4},{4,3},{5,6},{6,5},{7,8},{8,7},{9,10},{10,... | collective-permute-start | bytes 491528 | tf_op jit(solution)/shard_map/ppermute | solution.py:963
  59.2 0.1 collective-permute-start.10
  59.3 3.4 %collective-permute-start.11 = (f32[24,128]{1,0:T(8,128)S(1)}, f32[24,128]{1,0:T(8,128)S(1)}, u32[]{:S(2)}, u32[]{:S(2)}) collective-permute-start(f32[24,128]{1,0:T(8,128)S(1)} %get-tuple-element.54), channel_id=1, source_target_pairs={{0,15},{1,2},{2,1},{3,4},{4,3},{5,6},{6,5},{7,8},{8,7},{9,10},{10,... | collective-permute-start | bytes 36872 | tf_op jit(solution)/shard_map/ppermute | solution.py:963
  62.7 3.4 %coarse.1.coarse_part = f32[40,128]{1,0:T(8,128)S(1)} custom-call(f32[32,32]{1,0:T(8,128)S(1)} %copy-done.8, f32[3072,128]{1,0:T(8,128)S(1)} %bitcast.3, f32[384,128]{1,0:T(8,128)S(1)} %copy-done.7), custom_call_target="tpu_custom_call" | custom-call | flops 2000000000 | bytes 4000000 | tf_op jit(solution)/shard_map/coarse/pallas_call | solution.py:820
  66.1 0.3 collective-permute-done.11.edge_second
  66.4 3.3 %finish.1 = f32[8,2,8,64,128]{4,3,2,1,0:T(8,128)} custom-call(f32[8,2,8,64,128]{4,3,2,1,0:T(8,128)S(1)} %copy-done, f32[8,2,4,16,128]{4,3,2,1,0:T(8,128)S(1)} %copy-done.1, f32[40,128]{1,0:T(8,128)S(1)} %coarse.1.coarse_part, bf16[512,240]{1,0:T(8,128)(2,1)S(1)} %copy-done.4, f32[320,128]{1,0:T(8,128)S(1)} %collective-permute-done.6.x_first, ...), custom_call_target="tpu_custom_call" | custom-call | flops 2000000000 | bytes 8000000 | tf_op jit(solution)/shard_map/finish/pallas_call | solution.py:936
  (38 shorter events, 0.2 us)
Async XLA Ops:
  0.0 14.8 %copy-start.9 = (f32[3,10,10]{2,0,1:T(4,128)S(1)}, f32[3,10,10]{2,0,1:T(4,128)}, u32[]{:S(2)}) copy-start(f32[3,10,10]{2,0,1:T(4,128)} %param.26) | copy-start | bytes 3604
  4.5 14.5 %collective-permute-start = (f32[648,128]{1,0:T(8,128)}, f32[648,128]{1,0:T(8,128)S(1)}, u32[]{:S(2)}, u32[]{:S(2)}) collective-permute-start(f32[648,128]{1,0:T(8,128)} %get-tuple-element.34), channel_id=1, source_target_pairs={{0,16},{16,0},{32,48},{48,32},{64,80},{80,64},{96,112},{112,96},{1... | collective-permute-start | bytes 995336 | tf_op jit(solution)/shard_map/ppermute | solution.py:963
  4.6 14.4 %collective-permute-start.1 = (f32[648,128]{1,0:T(8,128)}, f32[648,128]{1,0:T(8,128)S(1)}, u32[]{:S(2)}, u32[]{:S(2)}) collective-permute-start(f32[648,128]{1,0:T(8,128)} %get-tuple-element.35), channel_id=1, source_target_pairs={{0,112},{16,32},{32,16},{48,64},{64,48},{80,96},{96,80},{112,0},{1... | collective-permute-start | bytes 995336 | tf_op jit(solution)/shard_map/ppermute | solution.py:963
  7.6 21.7 %collective-permute-start.2 = (f32[640,128]{1,0:T(8,128)}, f32[640,128]{1,0:T(8,128)S(1)}, u32[]{:S(2)}, u32[]{:S(2)}) collective-permute-start(f32[640,128]{1,0:T(8,128)} %get-tuple-element.36), channel_id=1, source_target_pairs={{0,1},{1,0},{2,3},{3,2},{4,5},{5,4},{6,7},{7,6},{8,9},{9,8},{10,11... | collective-permute-start | bytes 983048 | tf_op jit(solution)/shard_map/ppermute | solution.py:963
  9.2 20.2 %collective-permute-start.3 = (f32[640,128]{1,0:T(8,128)}, f32[640,128]{1,0:T(8,128)S(1)}, u32[]{:S(2)}, u32[]{:S(2)}) collective-permute-start(f32[640,128]{1,0:T(8,128)} %get-tuple-element.37), channel_id=1, source_target_pairs={{0,15},{1,2},{2,1},{3,4},{4,3},{5,6},{6,5},{7,8},{8,7},{9,10},{10,... | collective-permute-start | bytes 983048 | tf_op jit(solution)/shard_map/ppermute | solution.py:963
  19.0 10.4 %copy-start.2 = (f32[648,128]{1,0:T(8,128)}, f32[648,128]{1,0:T(8,128)S(1)}, u32[]{:S(2)}) copy-start(f32[648,128]{1,0:T(8,128)S(1)} %collective-permute-done.x_first) | copy-start | bytes 995332
  19.1 10.4 %copy-start.3 = (f32[648,128]{1,0:T(8,128)}, f32[648,128]{1,0:T(8,128)S(1)}, u32[]{:S(2)}) copy-start(f32[648,128]{1,0:T(8,128)S(1)} %collective-permute-done.1.x_second) | copy-start | bytes 995332
  21.8 7.6 %collective-permute-start.4 = (f32[72,128]{1,0:T(8,128)S(1)}, f32[72,128]{1,0:T(8,128)S(1)}, u32[]{:S(2)}, u32[]{:S(2)}) collective-permute-start(f32[72,128]{1,0:T(8,128)S(1)} %get-tuple-element.38), channel_id=1, source_target_pairs={{0,1},{1,0},{2,3},{3,2},{4,5},{5,4},{6,7},{7,6},{8,9},{9,8},{10,11... | collective-permute-start | bytes 110600 | tf_op jit(solution)/shard_map/ppermute | solution.py:963
  21.8 7.6 %collective-permute-start.5 = (f32[72,128]{1,0:T(8,128)S(1)}, f32[72,128]{1,0:T(8,128)S(1)}, u32[]{:S(2)}, u32[]{:S(2)}) collective-permute-start(f32[72,128]{1,0:T(8,128)S(1)} %get-tuple-element.39), channel_id=1, source_target_pairs={{0,15},{1,2},{2,1},{3,4},{4,3},{5,6},{6,5},{7,8},{8,7},{9,10},{10,... | collective-permute-start | bytes 110600 | tf_op jit(solution)/shard_map/ppermute | solution.py:963
  23.1 39.6 %all-to-all-start = ((f32[128,24,128]{2,1,0:T(8,128)}), f32[128,24,128]{2,1,0:T(8,128)S(1)}, u32[]{:S(2)}, u32[]{:S(2)}) async-start(f32[128,24,128]{2,1,0:T(8,128)} %get-tuple-element.48), calls=%async_computation | async-start | bytes 3145728 | tf_op jit(solution)/shard_map/all_to_all | solution.py:976
  29.4 0.8 %copy-start.11 = (f32[640,128]{1,0:T(8,128)}, f32[640,128]{1,0:T(8,128)S(1)}, u32[]{:S(2)}) copy-start(f32[640,128]{1,0:T(8,128)S(1)} %collective-permute-done.3.y_second) | copy-start | bytes 983044
  29.4 0.8 %copy-start.12 = (f32[72,128]{1,0:T(8,128)}, f32[72,128]{1,0:T(8,128)S(1)}, u32[]{:S(2)}) copy-start(f32[72,128]{1,0:T(8,128)S(1)} %collective-permute-done.4.edge_first) | copy-start | bytes 110596
  29.4 0.8 %copy-start.13 = (f32[72,128]{1,0:T(8,128)}, f32[72,128]{1,0:T(8,128)S(1)}, u32[]{:S(2)}) copy-start(f32[72,128]{1,0:T(8,128)S(1)} %collective-permute-done.5.edge_second) | copy-start | bytes 110596
  30.2 32.5 %copy-start.7 = (f32[384,128]{1,0:T(8,128)S(1)}, f32[384,128]{1,0:T(8,128)}, u32[]{:S(2)}) copy-start(f32[384,128]{1,0:T(8,128)} %constant.52.clone.table) | copy-start | bytes 589828
  30.2 32.5 %copy-start.8 = (f32[32,32]{1,0:T(8,128)S(1)}, f32[32,32]{1,0:T(8,128)}, u32[]{:S(2)}) copy-start(f32[32,32]{1,0:T(8,128)} %constant.51.clone.rows_x) | copy-start | bytes 12292
  50.3 16.1 %copy-start.1 = (f32[8,2,4,16,128]{4,3,2,1,0:T(8,128)S(1)}, f32[8,2,4,16,128]{4,3,2,1,0:T(8,128)}, u32[]{:S(2)}) copy-start(f32[8,2,4,16,128]{4,3,2,1,0:T(8,128)} %get-tuple-element.47.middle) | copy-start | bytes 1572868
  50.3 16.1 %copy-start.4 = (bf16[512,240]{1,0:T(8,128)(2,1)S(1)}, bf16[512,240]{1,0:T(8,128)(2,1)}, u32[]{:S(2)}) copy-start(bf16[512,240]{1,0:T(8,128)(2,1)} %constant.53.clone.prolong) | copy-start | bytes 737284
  50.4 8.9 %collective-permute-start.6 = (f32[320,128]{1,0:T(8,128)}, f32[320,128]{1,0:T(8,128)S(1)}, u32[]{:S(2)}, u32[]{:S(2)}) collective-permute-start(f32[320,128]{1,0:T(8,128)} %get-tuple-element.49), channel_id=1, source_target_pairs={{0,16},{16,0},{32,48},{48,32},{64,80},{80,64},{96,112},{112,96},{1... | collective-permute-start | bytes 491528 | tf_op jit(solution)/shard_map/ppermute | solution.py:963
  50.4 8.8 %collective-permute-start.7 = (f32[320,128]{1,0:T(8,128)}, f32[320,128]{1,0:T(8,128)S(1)}, u32[]{:S(2)}, u32[]{:S(2)}) collective-permute-start(f32[320,128]{1,0:T(8,128)} %get-tuple-element.50), channel_id=1, source_target_pairs={{0,112},{16,32},{32,16},{48,64},{64,48},{80,96},{96,80},{112,0},{1... | collective-permute-start | bytes 491528 | tf_op jit(solution)/shard_map/ppermute | solution.py:963
  52.7 13.4 %collective-permute-start.8 = (f32[320,128]{1,0:T(8,128)}, f32[320,128]{1,0:T(8,128)S(1)}, u32[]{:S(2)}, u32[]{:S(2)}) collective-permute-start(f32[320,128]{1,0:T(8,128)} %get-tuple-element.51), channel_id=1, source_target_pairs={{0,1},{1,0},{2,3},{3,2},{4,5},{5,4},{6,7},{7,6},{8,9},{9,8},{10,11... | collective-permute-start | bytes 491528 | tf_op jit(solution)/shard_map/ppermute | solution.py:963
  54.2 11.9 %collective-permute-start.9 = (f32[320,128]{1,0:T(8,128)}, f32[320,128]{1,0:T(8,128)S(1)}, u32[]{:S(2)}, u32[]{:S(2)}) collective-permute-start(f32[320,128]{1,0:T(8,128)} %get-tuple-element.52), channel_id=1, source_target_pairs={{0,15},{1,2},{2,1},{3,4},{4,3},{5,6},{6,5},{7,8},{8,7},{9,10},{10,... | collective-permute-start | bytes 491528 | tf_op jit(solution)/shard_map/ppermute | solution.py:963
  59.2 6.9 %collective-permute-start.10 = (f32[24,128]{1,0:T(8,128)S(1)}, f32[24,128]{1,0:T(8,128)S(1)}, u32[]{:S(2)}, u32[]{:S(2)}) collective-permute-start(f32[24,128]{1,0:T(8,128)S(1)} %get-tuple-element.53), channel_id=1, source_target_pairs={{0,1},{1,0},{2,3},{3,2},{4,5},{5,4},{6,7},{7,6},{8,9},{9,8},{10,11... | collective-permute-start | bytes 36872 | tf_op jit(solution)/shard_map/ppermute | solution.py:963
  59.3 7.1 %collective-permute-start.11 = (f32[24,128]{1,0:T(8,128)S(1)}, f32[24,128]{1,0:T(8,128)S(1)}, u32[]{:S(2)}, u32[]{:S(2)}) collective-permute-start(f32[24,128]{1,0:T(8,128)S(1)} %get-tuple-element.54), channel_id=1, source_target_pairs={{0,15},{1,2},{2,1},{3,4},{4,3},{5,6},{6,5},{7,8},{8,7},{9,10},{10,... | collective-permute-start | bytes 36872 | tf_op jit(solution)/shard_map/ppermute | solution.py:963
  62.7 3.7 %copy-start = (f32[8,2,8,64,128]{4,3,2,1,0:T(8,128)S(1)}, f32[8,2,8,64,128]{4,3,2,1,0:T(8,128)}, u32[]{:S(2)}) copy-start(f32[8,2,8,64,128]{4,3,2,1,0:T(8,128)} %get-tuple-element.46.fine) | copy-start | bytes 12582916
  (3 other events, 2.2 us)

commit v5 on v4

--- a/solution.py
+++ b/solution.py
@@ -517,9 +517,9 @@
     return [functools.partial(back, h, row) for h in (0, 1) for row in range(0, core, 16)]
 
 
-def products(level, slots, forward, backward, inverse, lag):
+def products(level, slots, forward, backward, inverse, waiting, lag):
     core, modes = level.core, level.modes
-    waiting = []
+    places = waiting.shape[0]
     steps = [(spectrum, hats, i) for spectrum, hats in slots for i in range(level.wide)]
     for step in range(len(steps) + lag):
         if step < len(steps):
@@ -527,10 +527,12 @@
             both = dot(forward[...], spectrum[i])
             damp = inverse[i]
             hat = (both[0:modes] + both[modes : 2 * modes]) * jnp.concatenate([damp, damp], axis=1)
-            waiting.append(jnp.concatenate(split(hat), axis=0))
+            high, low = split(hat)
+            waiting[step % places, 0:modes] = high
+            waiting[step % places, modes : 2 * modes] = low
         if step >= lag:
             _, hats, i = steps[step - lag]
-            both = dot(backward[...], waiting[step - lag])
+            both = dot(backward[...], waiting[(step - lag) % places, 0 : 2 * modes])
             hats[i] = both[0:core] + both[core : 2 * core]
 
 
@@ -608,6 +610,7 @@
     solved,
     inverse,
     inverse_m,
+    waiting,
     in_sems,
     out_sems,
 ):
@@ -640,7 +643,7 @@
             for run in first_steps(MID, q, planes_m, rims_m, middle_coeff, spectrum_m.at[k]):
                 run()
         slots = [(spectrum_m.at[k], hats_m.at[k]) for k in range(MID_GROUP)]
-        products(MID, slots, forward_m, backward_m, inverse_m, LAG)
+        products(MID, slots, forward_m, backward_m, inverse_m, waiting, LAG)
         for k, q in enumerate(pairs):
             for run in last_steps(MID, q, hats_m.at[k], middle_coeff, scale, middle_out):
                 run()
@@ -654,7 +657,7 @@
     def fine_step(q, carry):
         for run in first_steps(FINE, q, planes, rims, fine_coeff, spectrum):
             run()
-        products(FINE, [(spectrum, hats)], forward, backward, inverse, LAG)
+        products(FINE, [(spectrum, hats)], forward, backward, inverse, waiting, LAG)
         for run in last_steps(FINE, q, hats, fine_coeff, scale, solved):
             run()
         pltpu.make_async_copy(solved.at[q], fine_out.at[q], out_sems.at[q]).start()
@@ -722,6 +725,7 @@
             pltpu.VMEM((8, 2, 8, 64, LANES), F32),
             pltpu.VMEM((FINE.wide, FINE.modes, LANES), F32),
             pltpu.VMEM((MID.wide, MID.modes, LANES), F32),
+            pltpu.VMEM((10, 2 * FINE.modes, 2 * LANES), BF16),
             pltpu.SemaphoreType.DMA((16,)),
             pltpu.SemaphoreType.DMA((8,)),
         ],

time: 70 us -> 70.1 us (level)
  no operation moved by 1% of the time
where the time goes in v5:
time: 70.1 us; the launch traced here: 69.8 us
  Pallas kernels  36.3 us (52%)
  starting transfers between devices  30.1 us (43%)
  local copies, waits for them, and re-layouts  2.86 us (4%)
    ppermute x6, starting transfers between devices, swap(): lax.ppermute(second, axis, others)  20.6 us
    pallas_call x1, Pallas kernels, schwarz(): pl.pallas_call(schwarz_kernel, out_shape=[jax.ShapeDtypeStruct((8, 2, 8,...  20.2 us
    all_to_all x1, starting transfers between devices, on_device(): gathered = lax.all_to_all(vertex, ('px', 'py'), 0, 0)  6.23 us
    pallas_call x1, Pallas kernels, pack(): pl.pallas_call(pack_kernel, out_shape=[x_halo] * 2 + [y_halo] * 2 + [jax....  4.52 us
    pallas_call x1, Pallas kernels, solve_tables(): pl.pallas_call(tables_kernel, out_shape=shapes, in_specs=[vmem] * 4 + [pl...  3.61 us
    pallas_call x1, Pallas kernels, coarse(): pl.pallas_call(coarse_kernel, out_shape=jax.ShapeDtypeStruct((40, LANES),...  3.36 us
    ppermute x6, starting transfers between devices, swap(): lax.ppermute(first, axis, pairs)  3.29 us
    pallas_call x1, Pallas kernels, finish(): pl.pallas_call(finish_kernel, out_shape=jax.ShapeDtypeStruct((8, 2, 8, 64...  3.27 us
  transfers between devices with their start and end apart: 13, of which 1 were waited for; matrix products, arithmetic and copies ran while one was open for 1% of the time, Pallas kernels for 41%

profile of v5, /device:TPU:0, one launch (start us, length us, event | category | flops | bytes accessed | tf_op | source)
XLA Modules:
  0.0 69.8 jit_solution(8777869124797374012)
XLA Ops:
  0.0 4.5 %pack.1 = (f32[648,128]{1,0:T(8,128)}, f32[648,128]{1,0:T(8,128)}, f32[640,128]{1,0:T(8,128)}, f32[640,128]{1,0:T(8,128)}, f32[4,4,4,16,128]{4,3,2,1,0:T(8,128)}, /*index=5*/f32[32,128]{1,0:T(8,128)}) custom-call(f32[4,4,8,64,128]{4,3,2,1,0:T(8,128)} %bitcast.4, bf16[160,512]{1,0:T(8,128)(2,1)} %constant.36.clone.restrict_in, ...), custom_call_target="tpu_custom_call" | custom-call | flops 1000000000 | bytes 8000000 | tf_op jit(solution)/shard_map/pack/pallas_call | solution.py:282
  4.5 0.1 collective-permute-start
  4.6 3.0 %collective-permute-start.1 = (f32[648,128]{1,0:T(8,128)}, f32[648,128]{1,0:T(8,128)S(1)}, u32[]{:S(2)}, u32[]{:S(2)}) collective-permute-start(f32[648,128]{1,0:T(8,128)} %get-tuple-element.35), channel_id=1, source_target_pairs={{0,112},{16,32},{32,16},{48,64},{64,48},{80,96},{96,80},{112,0},{1... | collective-permute-start | bytes 995336 | tf_op jit(solution)/shard_map/ppermute | solution.py:967
  7.6 1.6 %collective-permute-start.2 = (f32[640,128]{1,0:T(8,128)}, f32[640,128]{1,0:T(8,128)S(1)}, u32[]{:S(2)}, u32[]{:S(2)}) collective-permute-start(f32[640,128]{1,0:T(8,128)} %get-tuple-element.36), channel_id=1, source_target_pairs={{0,1},{1,0},{2,3},{3,2},{4,5},{5,4},{6,7},{7,6},{8,9},{9,8},{10,11... | collective-permute-start | bytes 983048 | tf_op jit(solution)/shard_map/ppermute | solution.py:967
  9.2 5.7 %collective-permute-start.3 = (f32[640,128]{1,0:T(8,128)}, f32[640,128]{1,0:T(8,128)S(1)}, u32[]{:S(2)}, u32[]{:S(2)}) collective-permute-start(f32[640,128]{1,0:T(8,128)} %get-tuple-element.37), channel_id=1, source_target_pairs={{0,15},{1,2},{2,1},{3,4},{4,3},{5,6},{6,5},{7,8},{8,7},{9,10},{10,... | collective-permute-start | bytes 983048 | tf_op jit(solution)/shard_map/ppermute | solution.py:967
  14.8 0.6 copy.25.fine_basis
  15.4 3.6 %tables.1 = (bf16[224,192]{1,0:T(8,128)(2,1)}, bf16[128,224]{1,0:T(8,128)(2,1)}, f32[112,128]{1,0:T(8,128)}, bf16[96,64]{1,0:T(8,128)(2,1)}, bf16[32,96]{1,0:T(8...) custom-call(f32[3,10,10]{2,1,0:T(8,128)} %copy.25.fine_basis, f32[3,10]{1,0:T(4,128)} %fine_eigen.3, ...), custom_call_target="tpu_custom_call" | custom-call | flops 100000000 | bytes 1000000 | tf_op jit(solution)/shard_map/tables/pallas_call | solution.py:560
  19.1 0.7 %copy-done.5 = f32[32,128]{1,0:T(8,128)S(1)} copy-done((f32[32,128]{1,0:T(8,128)S(1)}, f32[32,128]{1,0:T(8,128)}, u32[]{:S(2)}) %copy-start.5) | copy-done | bytes 16408
  19.8 0.7 copy-done.6
  20.5 1.3 %join.1 = (f32[72,128]{1,0:T(8,128)S(1)}, f32[72,128]{1,0:T(8,128)S(1)}, f32[128,24,128]{2,1,0:T(8,128)}) custom-call(f32[648,128]{1,0:T(8,128)S(1)} %collective-permute-done.x_first, f32[648,128]{1,0:T(8,128)S(1)} %collective-permute-done.1.x_second, f32[32,128]{1,0:T(8,128)S(1)} %copy-done.5, f32[6,6]{1,0:T(8,128)S(1)} %copy-done.6), custom_call_target="tpu_custom_call" | custom-call | flops 1000000 | bytes 1000000 | tf_op jit(solution)/shard_map/join/pallas_call | solution.py:337
  21.8 1.3 %collective-permute-start.5 = (f32[72,128]{1,0:T(8,128)S(1)}, f32[72,128]{1,0:T(8,128)S(1)}, u32[]{:S(2)}, u32[]{:S(2)}) collective-permute-start(f32[72,128]{1,0:T(8,128)S(1)} %get-tuple-element.39), channel_id=1, source_target_pairs={{0,15},{1,2},{2,1},{3,4},{4,3},{5,6},{6,5},{7,8},{8,7},{9,10},{10,... | collective-permute-start | bytes 110600 | tf_op jit(solution)/shard_map/ppermute | solution.py:967
  23.1 6.2 %all-to-all-start = ((f32[128,24,128]{2,1,0:T(8,128)}), f32[128,24,128]{2,1,0:T(8,128)S(1)}, u32[]{:S(2)}, u32[]{:S(2)}) async-start(f32[128,24,128]{2,1,0:T(8,128)} %get-tuple-element.48), calls=%async_computation | async-start | bytes 3145728 | tf_op jit(solution)/shard_map/all_to_all | solution.py:980
  29.4 0.7 copy-done.10
  30.1 0.1 copy-done.11
  30.2 20.2 %schwarz.1 = (f32[8,2,8,64,128]{4,3,2,1,0:T(8,128)}, f32[8,2,4,16,128]{4,3,2,1,0:T(8,128)}, f32[320,128]{1,0:T(8,128)}, f32[320,128]{1,0:T(8,128)}, f32[320,128]{1,0:T(8,128)}, /*index=5*/f32[320,128]{1,0:T(8,128)}) custom-call(f32[4,4,8,64,128]{4,3,2,1,0:T(8,128)} %bitcast.5, f32[4,4,4,16,128]{4,3,2,1,0:T(8,128)} %get-tuple-element.30.middle, ...), custom_call_target="tpu_custom_call" | custom-call | flops 99999997952 | bytes 12000000 | tf_op jit(solution)/shard_map/schwarz/pallas_call | solution.py:713
  50.4 0.1 collective-permute-start.6
  50.5 2.3 %collective-permute-start.7 = (f32[320,128]{1,0:T(8,128)}, f32[320,128]{1,0:T(8,128)S(1)}, u32[]{:S(2)}, u32[]{:S(2)}) collective-permute-start(f32[320,128]{1,0:T(8,128)} %get-tuple-element.50), channel_id=1, source_target_pairs={{0,112},{16,32},{32,16},{48,64},{64,48},{80,96},{96,80},{112,0},{1... | collective-permute-start | bytes 491528 | tf_op jit(solution)/shard_map/ppermute | solution.py:967
  52.8 1.5 %collective-permute-start.8 = (f32[320,128]{1,0:T(8,128)}, f32[320,128]{1,0:T(8,128)S(1)}, u32[]{:S(2)}, u32[]{:S(2)}) collective-permute-start(f32[320,128]{1,0:T(8,128)} %get-tuple-element.51), channel_id=1, source_target_pairs={{0,1},{1,0},{2,3},{3,2},{4,5},{5,4},{6,7},{7,6},{8,9},{9,8},{10,11... | collective-permute-start | bytes 491528 | tf_op jit(solution)/shard_map/ppermute | solution.py:967
  54.3 5.0 %collective-permute-start.9 = (f32[320,128]{1,0:T(8,128)}, f32[320,128]{1,0:T(8,128)S(1)}, u32[]{:S(2)}, u32[]{:S(2)}) collective-permute-start(f32[320,128]{1,0:T(8,128)} %get-tuple-element.52), channel_id=1, source_target_pairs={{0,15},{1,2},{2,1},{3,4},{4,3},{5,6},{6,5},{7,8},{8,7},{9,10},{10,... | collective-permute-start | bytes 491528 | tf_op jit(solution)/shard_map/ppermute | solution.py:967
  59.3 0.1 collective-permute-start.10
  59.4 3.4 %collective-permute-start.11 = (f32[24,128]{1,0:T(8,128)S(1)}, f32[24,128]{1,0:T(8,128)S(1)}, u32[]{:S(2)}, u32[]{:S(2)}) collective-permute-start(f32[24,128]{1,0:T(8,128)S(1)} %get-tuple-element.54), channel_id=1, source_target_pairs={{0,15},{1,2},{2,1},{3,4},{4,3},{5,6},{6,5},{7,8},{8,7},{9,10},{10,... | collective-permute-start | bytes 36872 | tf_op jit(solution)/shard_map/ppermute | solution.py:967
  62.8 3.4 %coarse.1.coarse_part = f32[40,128]{1,0:T(8,128)S(1)} custom-call(f32[32,32]{1,0:T(8,128)S(1)} %copy-done.8, f32[3072,128]{1,0:T(8,128)S(1)} %bitcast.3, f32[384,128]{1,0:T(8,128)S(1)} %copy-done.7), custom_call_target="tpu_custom_call" | custom-call | flops 2000000000 | bytes 4000000 | tf_op jit(solution)/shard_map/coarse/pallas_call | solution.py:824
  66.2 0.3 collective-permute-done.11.edge_second
  66.5 3.3 %finish.1 = f32[8,2,8,64,128]{4,3,2,1,0:T(8,128)} custom-call(f32[8,2,8,64,128]{4,3,2,1,0:T(8,128)S(1)} %copy-done, f32[8,2,4,16,128]{4,3,2,1,0:T(8,128)S(1)} %copy-done.1, f32[40,128]{1,0:T(8,128)S(1)} %coarse.1.coarse_part, bf16[512,240]{1,0:T(8,128)(2,1)S(1)} %copy-done.4, f32[320,128]{1,0:T(8,128)S(1)} %collective-permute-done.6.x_first, ...), custom_call_target="tpu_custom_call" | custom-call | flops 2000000000 | bytes 8000000 | tf_op jit(solution)/shard_map/finish/pallas_call | solution.py:940
  (38 shorter events, 0.2 us)
Async XLA Ops:
  0.0 14.8 %copy-start.9 = (f32[3,10,10]{2,0,1:T(4,128)S(1)}, f32[3,10,10]{2,0,1:T(4,128)}, u32[]{:S(2)}) copy-start(f32[3,10,10]{2,0,1:T(4,128)} %param.26) | copy-start | bytes 3604
  4.5 14.5 %collective-permute-start = (f32[648,128]{1,0:T(8,128)}, f32[648,128]{1,0:T(8,128)S(1)}, u32[]{:S(2)}, u32[]{:S(2)}) collective-permute-start(f32[648,128]{1,0:T(8,128)} %get-tuple-element.34), channel_id=1, source_target_pairs={{0,16},{16,0},{32,48},{48,32},{64,80},{80,64},{96,112},{112,96},{1... | collective-permute-start | bytes 995336 | tf_op jit(solution)/shard_map/ppermute | solution.py:967
  4.6 14.4 %collective-permute-start.1 = (f32[648,128]{1,0:T(8,128)}, f32[648,128]{1,0:T(8,128)S(1)}, u32[]{:S(2)}, u32[]{:S(2)}) collective-permute-start(f32[648,128]{1,0:T(8,128)} %get-tuple-element.35), channel_id=1, source_target_pairs={{0,112},{16,32},{32,16},{48,64},{64,48},{80,96},{96,80},{112,0},{1... | collective-permute-start | bytes 995336 | tf_op jit(solution)/shard_map/ppermute | solution.py:967
  7.6 21.7 %collective-permute-start.2 = (f32[640,128]{1,0:T(8,128)}, f32[640,128]{1,0:T(8,128)S(1)}, u32[]{:S(2)}, u32[]{:S(2)}) collective-permute-start(f32[640,128]{1,0:T(8,128)} %get-tuple-element.36), channel_id=1, source_target_pairs={{0,1},{1,0},{2,3},{3,2},{4,5},{5,4},{6,7},{7,6},{8,9},{9,8},{10,11... | collective-permute-start | bytes 983048 | tf_op jit(solution)/shard_map/ppermute | solution.py:967
  9.2 20.2 %collective-permute-start.3 = (f32[640,128]{1,0:T(8,128)}, f32[640,128]{1,0:T(8,128)S(1)}, u32[]{:S(2)}, u32[]{:S(2)}) collective-permute-start(f32[640,128]{1,0:T(8,128)} %get-tuple-element.37), channel_id=1, source_target_pairs={{0,15},{1,2},{2,1},{3,4},{4,3},{5,6},{6,5},{7,8},{8,7},{9,10},{10,... | collective-permute-start | bytes 983048 | tf_op jit(solution)/shard_map/ppermute | solution.py:967
  19.0 10.4 %copy-start.2 = (f32[648,128]{1,0:T(8,128)}, f32[648,128]{1,0:T(8,128)S(1)}, u32[]{:S(2)}) copy-start(f32[648,128]{1,0:T(8,128)S(1)} %collective-permute-done.x_first) | copy-start | bytes 995332
  19.1 10.4 %copy-start.3 = (f32[648,128]{1,0:T(8,128)}, f32[648,128]{1,0:T(8,128)S(1)}, u32[]{:S(2)}) copy-start(f32[648,128]{1,0:T(8,128)S(1)} %collective-permute-done.1.x_second) | copy-start | bytes 995332
  21.8 7.6 %collective-permute-start.4 = (f32[72,128]{1,0:T(8,128)S(1)}, f32[72,128]{1,0:T(8,128)S(1)}, u32[]{:S(2)}, u32[]{:S(2)}) collective-permute-start(f32[72,128]{1,0:T(8,128)S(1)} %get-tuple-element.38), channel_id=1, source_target_pairs={{0,1},{1,0},{2,3},{3,2},{4,5},{5,4},{6,7},{7,6},{8,9},{9,8},{10,11... | collective-permute-start | bytes 110600 | tf_op jit(solution)/shard_map/ppermute | solution.py:967
  21.8 7.6 %collective-permute-start.5 = (f32[72,128]{1,0:T(8,128)S(1)}, f32[72,128]{1,0:T(8,128)S(1)}, u32[]{:S(2)}, u32[]{:S(2)}) collective-permute-start(f32[72,128]{1,0:T(8,128)S(1)} %get-tuple-element.39), channel_id=1, source_target_pairs={{0,15},{1,2},{2,1},{3,4},{4,3},{5,6},{6,5},{7,8},{8,7},{9,10},{10,... | collective-permute-start | bytes 110600 | tf_op jit(solution)/shard_map/ppermute | solution.py:967
  23.1 39.7 %all-to-all-start = ((f32[128,24,128]{2,1,0:T(8,128)}), f32[128,24,128]{2,1,0:T(8,128)S(1)}, u32[]{:S(2)}, u32[]{:S(2)}) async-start(f32[128,24,128]{2,1,0:T(8,128)} %get-tuple-element.48), calls=%async_computation | async-start | bytes 3145728 | tf_op jit(solution)/shard_map/all_to_all | solution.py:980
  29.4 0.8 %copy-start.11 = (f32[640,128]{1,0:T(8,128)}, f32[640,128]{1,0:T(8,128)S(1)}, u32[]{:S(2)}) copy-start(f32[640,128]{1,0:T(8,128)S(1)} %collective-permute-done.3.y_second) | copy-start | bytes 983044
  29.4 0.8 %copy-start.12 = (f32[72,128]{1,0:T(8,128)}, f32[72,128]{1,0:T(8,128)S(1)}, u32[]{:S(2)}) copy-start(f32[72,128]{1,0:T(8,128)S(1)} %collective-permute-done.4.edge_first) | copy-start | bytes 110596
  29.4 0.8 %copy-start.13 = (f32[72,128]{1,0:T(8,128)}, f32[72,128]{1,0:T(8,128)S(1)}, u32[]{:S(2)}) copy-start(f32[72,128]{1,0:T(8,128)S(1)} %collective-permute-done.5.edge_second) | copy-start | bytes 110596
  30.2 32.6 %copy-start.7 = (f32[384,128]{1,0:T(8,128)S(1)}, f32[384,128]{1,0:T(8,128)}, u32[]{:S(2)}) copy-start(f32[384,128]{1,0:T(8,128)} %constant.52.clone.table) | copy-start | bytes 589828
  30.2 32.6 %copy-start.8 = (f32[32,32]{1,0:T(8,128)S(1)}, f32[32,32]{1,0:T(8,128)}, u32[]{:S(2)}) copy-start(f32[32,32]{1,0:T(8,128)} %constant.51.clone.rows_x) | copy-start | bytes 12292
  50.4 16.1 %copy-start.1 = (f32[8,2,4,16,128]{4,3,2,1,0:T(8,128)S(1)}, f32[8,2,4,16,128]{4,3,2,1,0:T(8,128)}, u32[]{:S(2)}) copy-start(f32[8,2,4,16,128]{4,3,2,1,0:T(8,128)} %get-tuple-element.47.middle) | copy-start | bytes 1572868
  50.4 16.1 %copy-start.4 = (bf16[512,240]{1,0:T(8,128)(2,1)S(1)}, bf16[512,240]{1,0:T(8,128)(2,1)}, u32[]{:S(2)}) copy-start(bf16[512,240]{1,0:T(8,128)(2,1)} %constant.53.clone.prolong) | copy-start | bytes 737284
  50.4 8.9 %collective-permute-start.6 = (f32[320,128]{1,0:T(8,128)}, f32[320,128]{1,0:T(8,128)S(1)}, u32[]{:S(2)}, u32[]{:S(2)}) collective-permute-start(f32[320,128]{1,0:T(8,128)} %get-tuple-element.49), channel_id=1, source_target_pairs={{0,16},{16,0},{32,48},{48,32},{64,80},{80,64},{96,112},{112,96},{1... | collective-permute-start | bytes 491528 | tf_op jit(solution)/shard_map/ppermute | solution.py:967
  50.5 8.8 %collective-permute-start.7 = (f32[320,128]{1,0:T(8,128)}, f32[320,128]{1,0:T(8,128)S(1)}, u32[]{:S(2)}, u32[]{:S(2)}) collective-permute-start(f32[320,128]{1,0:T(8,128)} %get-tuple-element.50), channel_id=1, source_target_pairs={{0,112},{16,32},{32,16},{48,64},{64,48},{80,96},{96,80},{112,0},{1... | collective-permute-start | bytes 491528 | tf_op jit(solution)/shard_map/ppermute | solution.py:967
  52.8 13.4 %collective-permute-start.8 = (f32[320,128]{1,0:T(8,128)}, f32[320,128]{1,0:T(8,128)S(1)}, u32[]{:S(2)}, u32[]{:S(2)}) collective-permute-start(f32[320,128]{1,0:T(8,128)} %get-tuple-element.51), channel_id=1, source_target_pairs={{0,1},{1,0},{2,3},{3,2},{4,5},{5,4},{6,7},{7,6},{8,9},{9,8},{10,11... | collective-permute-start | bytes 491528 | tf_op jit(solution)/shard_map/ppermute | solution.py:967
  54.3 11.9 %collective-permute-start.9 = (f32[320,128]{1,0:T(8,128)}, f32[320,128]{1,0:T(8,128)S(1)}, u32[]{:S(2)}, u32[]{:S(2)}) collective-permute-start(f32[320,128]{1,0:T(8,128)} %get-tuple-element.52), channel_id=1, source_target_pairs={{0,15},{1,2},{2,1},{3,4},{4,3},{5,6},{6,5},{7,8},{8,7},{9,10},{10,... | collective-permute-start | bytes 491528 | tf_op jit(solution)/shard_map/ppermute | solution.py:967
  59.3 6.9 %collective-permute-start.10 = (f32[24,128]{1,0:T(8,128)S(1)}, f32[24,128]{1,0:T(8,128)S(1)}, u32[]{:S(2)}, u32[]{:S(2)}) collective-permute-start(f32[24,128]{1,0:T(8,128)S(1)} %get-tuple-element.53), channel_id=1, source_target_pairs={{0,1},{1,0},{2,3},{3,2},{4,5},{5,4},{6,7},{7,6},{8,9},{9,8},{10,11... | collective-permute-start | bytes 36872 | tf_op jit(solution)/shard_map/ppermute | solution.py:967
  59.4 7.1 %collective-permute-start.11 = (f32[24,128]{1,0:T(8,128)S(1)}, f32[24,128]{1,0:T(8,128)S(1)}, u32[]{:S(2)}, u32[]{:S(2)}) collective-permute-start(f32[24,128]{1,0:T(8,128)S(1)} %get-tuple-element.54), channel_id=1, source_target_pairs={{0,15},{1,2},{2,1},{3,4},{4,3},{5,6},{6,5},{7,8},{8,7},{9,10},{10,... | collective-permute-start | bytes 36872 | tf_op jit(solution)/shard_map/ppermute | solution.py:967
  62.8 3.7 %copy-start = (f32[8,2,8,64,128]{4,3,2,1,0:T(8,128)S(1)}, f32[8,2,8,64,128]{4,3,2,1,0:T(8,128)}, u32[]{:S(2)}) copy-start(f32[8,2,8,64,128]{4,3,2,1,0:T(8,128)} %get-tuple-element.46.fine) | copy-start | bytes 12582916
  (3 other events, 2.2 us)
